TPU v7x, 32 devices: a whole 2x2x4 slice. The times are simulated.
32 devices in a mesh: groups: 2 (over y), expert: 4 (over z), dp: 4 (over x, core).
Axes of the slice: x: 2, y: 2, z: 4, core: 2. Of those that a mesh axis runs over, the one named last changes fastest.
Arguments:
- tokens: bfloat16 [1024, 2048], P(('groups', 'expert', 'dp')), parts along dimension 0, may hold values from -6 to 6
- routing: int32 [1024, 2], P(('groups', 'expert', 'dp')), parts along dimension 0, may hold values from 0 to 3, all different within a row; in each aligned block of 32 rows (0 to 31, 32 to 63, ...) at most 32 rows name the same one
- gates: float32 [1024, 2], P(('groups', 'expert', 'dp')), parts along dimension 0, may hold values from 0.5 to 1.5
- ln_gain: float32 [2048], replicated, may hold values from 0.1 to 1.9
- w_in: bfloat16 [4, 2048, 4096], P('expert', None, 'dp'), may hold values from -0.125 to 0.125
- w_out: bfloat16 [4, 4096, 2048], P('expert', 'dp'), may hold values from -0.09375 to 0.09375
Outputs:
- mixed: bfloat16 [1024, 2048], P(('groups', 'expert', 'dp')), parts along dimension 0
There are 2 independent parts, one for each index of `groups`. A program takes and returns all parts, laid end to end along the dimension named above; an argument that names none is the same for every part. Nothing has to cross between parts.
Inputs may be any that keep to these rules, and one draw needn't show every extreme that they name: `routing`: the 32 rows of one device name each expert at most 32 times, a bound that some block reaches; a row's two experts differ.
All inputs are finite; a program needn't handle non-finite values.
Results may differ from a plain program's by a relative error of at most 0.006.
Values may be sent and summed in bfloat16 or wider, within the bound.
No kernel may reach another device: no remote copies, remote signals or barrier semaphores. Data moves between devices by JAX's collectives and lax.ppermute only.
A program may use at most 64 MiB of HBM per device.

v0:
```python
import jax
import jax.numpy as jnp
from jax import lax
from jax.sharding import PartitionSpec as P


def layer_norm(tokens, ln_gain):
    values = tokens.astype(jnp.float32)
    center = values - jnp.mean(values, axis=1, keepdims=True)
    variance = jnp.mean(center * center, axis=1, keepdims=True)
    return (center * lax.rsqrt(variance + 1e-05) * ln_gain).astype(jnp.bfloat16)


def slot_index(routing, experts, capacity):
    flat_ids = routing.reshape(-1)
    onehot = (flat_ids[:, None] == jnp.arange(experts, dtype=jnp.int32)[None, :]).astype(jnp.int32)
    rank_run = jnp.cumsum(onehot, axis=0) - 1
    own_rank = jnp.sum(onehot * rank_run, axis=1)
    return flat_ids * capacity + own_rank


def pack_slots(normed, routing, experts, capacity):
    slots = slot_index(routing, experts, capacity)
    picker = (slots[None, :] == jnp.arange(experts * capacity, dtype=jnp.int32)[:, None]).astype(
        jnp.bfloat16
    )
    picker = picker.reshape(experts * capacity, normed.shape[0], routing.shape[1]).sum(axis=2)
    outgoing = jnp.dot(picker, normed, preferred_element_type=jnp.float32).astype(jnp.bfloat16)
    return outgoing.reshape(experts, capacity, normed.shape[1])


def run_experts(block_in, w_first, w_second):
    dims_in = block_in.shape
    row_mat = block_in.reshape(-1, dims_in[-1])
    hidden = jnp.maximum(jnp.dot(row_mat, w_first, preferred_element_type=jnp.float32), 0.0).astype(
        jnp.bfloat16
    )
    product = jnp.dot(hidden, w_second, preferred_element_type=jnp.float32).astype(jnp.bfloat16)
    return product.reshape(dims_in)


def body(tokens, routing, gates, ln_gain, w_in, w_out):
    rows_dev = tokens.shape[0]
    feature_dim = tokens.shape[1]
    top_count = routing.shape[1]
    experts = lax.axis_size("expert")
    dp_size = lax.axis_size("dp")
    capacity = max(2, min(rows_dev, 2 * rows_dev * top_count // experts))
    w_first = w_in[0]
    w_second = w_out[0]
    normed = layer_norm(tokens, ln_gain)
    own_slots = slot_index(routing, experts, capacity)
    all_normed, all_routes = (
        lax.all_gather(normed, "dp", axis=0, tiled=True),
        lax.all_gather(routing, "dp", axis=0, tiled=True),
    )

    def pack_member(member_rows, member_routes):
        return pack_slots(member_rows, member_routes, experts, capacity)

    packed = jax.vmap(pack_member)(
        all_normed.reshape(dp_size, rows_dev, feature_dim),
        all_routes.reshape(dp_size, rows_dev, top_count),
    )
    partials = run_experts(
        lax.all_to_all(packed, "expert", split_axis=1, concat_axis=1, tiled=True), w_first, w_second
    )
    returned = lax.all_to_all(
        lax.all_to_all(partials, "expert", split_axis=1, concat_axis=1, tiled=True),
        "dp",
        split_axis=0,
        concat_axis=0,
        tiled=True,
    )
    block_total = returned.astype(jnp.float32).sum(axis=0)
    expert_out = block_total.astype(jnp.bfloat16).reshape(experts * capacity, feature_dim)
    expert_out = lax.optimization_barrier(expert_out)
    picker = (
        own_slots[:, None] == jnp.arange(experts * capacity, dtype=jnp.int32)[None, :]
    ).astype(jnp.bfloat16)
    values = jnp.dot(picker, expert_out, preferred_element_type=jnp.float32)
    weighted = values.reshape(rows_dev, top_count, feature_dim) * gates[:, :, None]
    return (tokens.astype(jnp.float32) + weighted.sum(axis=1)).astype(jnp.bfloat16)


def solution(mesh):
    placed = (
        P(("groups", "expert", "dp"), None),
        P(("groups", "expert", "dp"), None),
        P(("groups", "expert", "dp"), None),
        P(),
        P("expert", None, "dp"),
        P("expert", "dp", None),
    )
    return jax.shard_map(
        body,
        mesh=mesh,
        in_specs=placed,
        out_specs=P(("groups", "expert", "dp"), None),
        check_vma=False,
    )
```

profile of v0, /device:TPU:0, one launch (start us, length us, event | category | flops | bytes accessed | tf_op | source)
XLA Modules:
  0.0 167.4 jit_solution(16426321920921526746)
XLA Ops:
  0.0 6.2 %all-gather = s32[4,32,2]{1,2,0:T(2,128)S(1)} all-gather(s32[1,32,2]{1,2,0:T(2,128)} %bitcast.31), channel_id=1, replica_groups=mesh['groups'=2,'expert'=4,'dp'=4] {'dp'}, dimensions={0}, use_global_device_ids=true | all-gather | bytes 1280 | tf_op jit(solution)/shard_map/all_gather | solution.py:55
  6.5 0.1 reduce_window_sum.23
  6.7 0.2 select_reduce_fusion
  7.1 0.1 fusion.19
  7.2 1.0 convert_reduce_fusion
  8.3 1.1 fusion.13
  9.4 1.0 fusion.15
  10.4 7.6 %all_gather.7 = bf16[128,2048]{1,0:T(8,128)(2,1)S(1)} all-gather(bf16[32,2048]{1,0:T(8,128)(2,1)S(1)} %fusion.15), channel_id=1, replica_groups=mesh['groups'=2,'expert'=4,'dp'=4] {'dp'}, dimensions={0}, use_global_device_ids=true | all-gather | bytes 655360 | tf_op jit(solution)/shard_map/all_gather | solution.py:54
  18.1 0.7 convolution_convert_fusion
  18.8 0.2 copy.68
  19.1 53.5 %all_to_all.15 = bf16[4,4,32,2048]{3,2,0,1:T(8,128)(2,1)S(1)} all-to-all(bf16[4,4,32,2048]{3,2,0,1:T(8,128)(2,1)S(1)} %copy.68), channel_id=1, replica_groups=mesh['groups'=2,'expert'=4,'dp'=4] {'expert'}, dimensions={1} | all-to-all | bytes 4194304 | tf_op jit(solution)/shard_map/all_to_all | solution.py:66
  72.5 0.1 copy.69
  72.7 9.3 %fusion.4 = bf16[512,2048]{1,0:T(8,128)(2,1)} fusion(bf16[1,1024,2048]{2,1,0:T(8,128)(2,1)} %param.11, bf16[512,2048]{1,0:T(8,128)(2,1)S(1)} %bitcast.25, bf16[1,2048,1024]{2,1,0:T(8,128)(2,1)} %param.10), kind=kOutput, calls=%fused_computation.4 | convolution fusion | flops 4297064448 | bytes 12582912 | tf_op jit(solution)/shard_map/dot_general | solution.py:38
  82.0 1.7 %copy.70 = bf16[4,4,32,2048]{3,2,0,1:T(8,128)(2,1)S(1)} copy(bf16[4,4,32,2048]{3,2,1,0:T(8,128)(2,1)} %bitcast.26) | data formatting | bytes 4194304 | tf_op jit(solution)/shard_map/reshape | solution.py:39
  83.7 50.4 %all_to_all.16 = bf16[4,4,32,2048]{3,2,0,1:T(8,128)(2,1)S(1)} all-to-all(bf16[4,4,32,2048]{3,2,0,1:T(8,128)(2,1)S(1)} %copy.70), channel_id=1, replica_groups=mesh['groups'=2,'expert'=4,'dp'=4] {'expert'}, dimensions={1} | all-to-all | bytes 4194304 | tf_op jit(solution)/shard_map/all_to_all | solution.py:69
  134.1 1.5 copy.71
  135.6 3.7 %all-to-all-start.2 = ((bf16[4,4,32,2048]{3,2,1,0:T(8,128)(2,1)}), bf16[4,4,32,2048]{3,2,1,0:T(8,128)(2,1)S(1)}, u32[]{:S(2)}, u32[]{:S(2)}) async-start(bf16[4,4,32,2048]{3,2,1,0:T(8,128)(2,1)} %copy.71), calls=%async_computation.2 | async-start | bytes 4194304 | tf_op jit(solution)/shard_map/all_to_all | solution.py:68
  139.8 0.2 select_reduce_fusion.1
  140.0 25.0 %all-to-all-done.2 = bf16[4,4,32,2048]{3,2,1,0:T(8,128)(2,1)S(1)} async-done(((bf16[4,4,32,2048]{3,2,1,0:T(8,128)(2,1)}), bf16[4,4,32,2048]{3,2,1,0:T(8,128)(2,1)S(1)}, u32[]{:S(2)}, u32[]{:S(2)}) %all-to-all-start.2) | async-done | bytes 2097184 | tf_op jit(solution)/shard_map/all_to_all | solution.py:68
  165.0 0.4 reduce_sum.77
  165.4 0.3 fusion.21
  165.7 0.3 reshape.65
  166.0 0.7 multiply_reduce_fusion
  166.8 0.7 fusion.16
  (21 shorter events, 1.0 us)
Async XLA Ops:
  135.6 3.8 %copy-start.1 = (s32[32,2]{0,1:T(2,128)S(1)}, s32[32,2]{0,1:T(2,128)}, u32[]{:S(2)}) copy-start(s32[32,2]{0,1:T(2,128)} %param.7) | copy-start | bytes 772
  135.6 4.1 %copy-start.2 = (f32[32,2]{0,1:T(2,128)S(1)}, f32[32,2]{0,1:T(2,128)}, u32[]{:S(2)}) copy-start(f32[32,2]{0,1:T(2,128)} %param.8) | copy-start | bytes 772
  135.6 29.4 %all-to-all-start.2 = ((bf16[4,4,32,2048]{3,2,1,0:T(8,128)(2,1)}), bf16[4,4,32,2048]{3,2,1,0:T(8,128)(2,1)S(1)}, u32[]{:S(2)}, u32[]{:S(2)}) async-start(bf16[4,4,32,2048]{3,2,1,0:T(8,128)(2,1)} %copy.71), calls=%async_computation.2 | async-start | bytes 4194304 | tf_op jit(solution)/shard_map/all_to_all | solution.py:68
  165.4 1.3 copy-start
where the time goes:
time: 168 us; the launch traced here: 167 us
  blocking collectives  118 us (70%)
  waiting for transfers between devices  25 us (15%)
  matrix products  10.3 us (6%)
  other arithmetic  5.97 us (4%)
  local copies, waits for them, and re-layouts  4.56 us (3%)
  starting transfers between devices  3.74 us (2%)
    all_to_all x1, blocking collectives, body(): lax.all_to_all(packed, 'expert', split_axis=1, concat_axis=1, tiled=True)  53.5 us
    all_to_all x1, blocking collectives, body(): lax.all_to_all(partials, 'expert', split_axis=1, concat_axis=1, tiled=True)  50.4 us
    all_to_all x1, waiting for transfers between devices, body(): lax.all_to_all(lax.all_to_all(partials, 'expert', split_axis=1, concat_ax...  25 us
    dot_general x1, matrix products, run_experts(): jnp.dot(hidden, w_second, preferred_element_type=jnp.float32)  9.32 us
    all_gather x1, blocking collectives, body(): lax.all_gather(normed, 'dp', axis=0, tiled=True)  7.65 us
    all_gather x1, blocking collectives, body(): lax.all_gather(routing, 'dp', axis=0, tiled=True)  6.24 us
    all_to_all x1, starting transfers between devices, body(): lax.all_to_all(lax.all_to_all(partials, 'expert', split_axis=1, concat_ax...  3.74 us
  transfers between devices with their start and end apart: 1, of which 1 were waited for; matrix products, arithmetic and copies ran while one was open for 0% of the time, Pallas kernels for 0%

commit v1 on v0

--- a/solution.py
+++ b/solution.py
@@ -1,7 +1,139 @@
+import functools
+
 import jax
 import jax.numpy as jnp
 from jax import lax
+from jax.experimental import pallas as pl
+from jax.experimental.pallas import tpu as pltpu
 from jax.sharding import PartitionSpec as P
+
+LANES = 128
+GATE_TERMS = 3
+
+
+def norm_kernel(experts, tokens_ref, routing_ref, gates_ref, gain_ref, out_ref):
+    width = tokens_ref.shape[1]
+    values = tokens_ref[...].astype(jnp.float32)
+    center = values - jnp.mean(values, axis=1, keepdims=True)
+    variance = jnp.mean(center * center, axis=1, keepdims=True)
+    normed = center * lax.rsqrt(variance + 1e-05) * gain_ref[...]
+    out_ref[:, :width] = normed.astype(jnp.bfloat16)
+    lane = lax.broadcasted_iota(jnp.int32, (tokens_ref.shape[0], LANES), 1)
+    expert = lax.rem(lane, experts)
+    term = lax.div(lane, experts)
+    gate = jnp.zeros(lane.shape, jnp.float32)
+    for k in range(routing_ref.shape[1]):
+        gate += jnp.where(routing_ref[:, k : k + 1] == expert, gates_ref[:, k : k + 1], 0.0)
+    rest = gate
+    packed = jnp.zeros(lane.shape, jnp.float32)
+    for i in range(GATE_TERMS):
+        part = rest.astype(jnp.bfloat16).astype(jnp.float32)
+        packed = jnp.where(term == i, part, packed)
+        rest = rest - part
+    out_ref[:, width:] = packed.astype(jnp.bfloat16)
+
+
+def norm_and_pack(tokens, routing, gates, ln_gain, experts):
+    rows, width = tokens.shape
+    return pl.pallas_call(
+        functools.partial(norm_kernel, experts),
+        out_shape=jax.ShapeDtypeStruct((rows, width + LANES), jnp.bfloat16),
+        name="norm",
+    )(tokens, routing, gates, ln_gain.reshape(1, width))
+
+
+def ffn_kernel(experts, pieces, expert_ref, *refs):
+    kept, sent = refs[:pieces], refs[pieces : 2 * pieces]
+    w_first, w_second = refs[2 * pieces : 2 * pieces + 2]
+    keep_ref, send_ref, rows_ref, hidden_ref = refs[2 * pieces + 2 :]
+    width, units = w_first.shape
+    at = 0
+    for ref in kept + sent:
+        rows_ref[at : at + ref.shape[0], :] = ref[...]
+        at += ref.shape[0]
+    half = at // 2
+    lane = lax.broadcasted_iota(jnp.int32, (at, LANES), 1)
+    chosen = (lax.rem(lane, experts) == expert_ref[0]) & (lane < GATE_TERMS * experts)
+    tail = rows_ref[:, width:].astype(jnp.float32)
+    gate = jnp.sum(jnp.where(chosen, tail, 0.0), axis=1, keepdims=True)
+    step = 256
+    for j in range(0, units, step):
+        dot = jnp.dot(
+            rows_ref[:, :width], w_first[:, j : j + step], preferred_element_type=jnp.float32
+        )
+        hidden_ref[:, j : j + step] = jnp.maximum(dot, 0.0).astype(jnp.bfloat16)
+    for j in range(0, width, step):
+        dot = jnp.dot(
+            hidden_ref[...], w_second[:, j : j + step], preferred_element_type=jnp.float32
+        )
+        out = (dot * gate).astype(jnp.bfloat16)
+        send_ref[:, j : j + step] = out[half:]
+        keep_ref[:, j : j + step] = out[:half]
+
+
+def ffn(kept, sent, w_first, w_second, experts, expert):
+    width, units = w_first.shape
+    half = sum(a.shape[0] for a in kept)
+    out = jax.ShapeDtypeStruct((half, width), jnp.bfloat16)
+    vmem = pl.BlockSpec(memory_space=pltpu.VMEM)
+    count = len(kept)
+    return pl.pallas_call(
+        functools.partial(ffn_kernel, experts, count),
+        out_shape=(out, out),
+        in_specs=[pl.BlockSpec(memory_space=pltpu.SMEM)] + [vmem] * (2 * count + 2),
+        out_specs=(vmem, vmem),
+        scratch_shapes=[
+            pltpu.VMEM((2 * half, width + LANES), jnp.bfloat16),
+            pltpu.VMEM((2 * half, units), jnp.bfloat16),
+        ],
+        compiler_params=pltpu.CompilerParams(vmem_limit_bytes=32 * 1024 * 1024),
+        cost_estimate=pl.CostEstimate(
+            flops=8 * half * width * units, bytes_accessed=4 * width * units, transcendentals=0
+        ),
+        name="ffn",
+    )(expert, *kept, *sent, w_first, w_second)
+
+
+def swap(array, axis, distance):
+    pairs = [(i, i ^ distance) for i in range(lax.axis_size(axis))]
+    return lax.ppermute(array, axis, pairs)
+
+
+def add(*arrays):
+    return sum(a.astype(jnp.float32) for a in arrays)
+
+
+GROUPS = ((0, 1), (2, 3))
+
+
+def dense_body(tokens, routing, gates, ln_gain, w_in, w_out):
+    rows = tokens.shape[0]
+    experts = lax.axis_size("expert")
+    core_bit, chip_bit = 1, 2
+    w_first, w_second = w_in[0], w_out[0]
+    expert = lax.axis_index("expert").reshape(1)
+    own = norm_and_pack(tokens, routing, gates, ln_gain, experts)
+    lane = [own] + [swap(own, "expert", k) for k in range(1, experts)]
+    across = [swap(a, "dp", chip_bit) for a in lane]
+    lane_other = [swap(a, "dp", core_bit) for a in lane]
+    across_other = [swap(a, "dp", core_bit) for a in across]
+    total = [None] * experts
+    for group in GROUPS:
+        kept = [lane[k] for k in group] + [across[k] for k in group]
+        sent = [lane_other[k] for k in group] + [across_other[k] for k in group]
+        keep, send = ffn(kept, sent, w_first, w_second, experts, expert)
+        back = swap(send, "dp", core_bit)
+        half = keep.shape[0] // 2
+        far = add(keep[half:], back[half:]).astype(jnp.bfloat16)
+        far_back = swap(far, "dp", chip_bit)
+        for i, k in enumerate(group):
+            at = slice(i * rows, (i + 1) * rows)
+            if k == 0:
+                total[k] = add(keep[at], back[at], far_back[at])
+            else:
+                block = add(keep[at], back[at], far_back[at]).astype(jnp.bfloat16)
+                total[k] = swap(block, "expert", k)
+    return add(tokens, *total).astype(jnp.bfloat16)
 
 
 def layer_norm(tokens, ln_gain):
@@ -39,7 +171,7 @@
     return product.reshape(dims_in)
 
 
-def body(tokens, routing, gates, ln_gain, w_in, w_out):
+def slot_body(tokens, routing, gates, ln_gain, w_in, w_out):
     rows_dev = tokens.shape[0]
     feature_dim = tokens.shape[1]
     top_count = routing.shape[1]
@@ -83,6 +215,15 @@
     return (tokens.astype(jnp.float32) + weighted.sum(axis=1)).astype(jnp.bfloat16)
 
 
+def body(tokens, routing, gates, ln_gain, w_in, w_out):
+    rows_dev = tokens.shape[0]
+    experts = lax.axis_size("expert")
+    capacity = max(2, min(rows_dev, 2 * rows_dev * routing.shape[1] // experts))
+    if capacity == rows_dev and experts == 4 and lax.axis_size("dp") == 4:
+        return dense_body(tokens, routing, gates, ln_gain, w_in, w_out)
+    return slot_body(tokens, routing, gates, ln_gain, w_in, w_out)
+
+
 def solution(mesh):
     placed = (
         P(("groups", "expert", "dp"), None),

time: 168 us -> 66.8 us (0.40)
  blocking collectives: 118 us -> 0 us
  starting transfers between devices: 3.74 us -> 21.1 us
  matrix products: 10.3 us -> 0 us
  Pallas kernels: 0 us -> 6.53 us
  waiting for transfers between devices: 25 us -> 30.6 us
  other arithmetic: 5.97 us -> 1.05 us
  local copies, waits for them, and re-layouts: 4.56 us -> 7.11 us
    all_to_all x2 -> x0, blocking collectives: 104 us -> none  [the longest x1 53.5 us: body(): lax.all_to_all(packed, 'expert', split_axis=1, concat_axis=1, tiled=True)]
    ppermute x0 -> x22, waiting for transfers between devices: none -> 30.6 us  [swap(): return lax.ppermute(array, axis, pairs)]
    all_to_all x1 -> x0, waiting for transfers between devices: 25 us -> none  [body(): lax.all_to_all(lax.all_to_all(partials, 'expert', split_axis=1, concat_ax...]
    ppermute x0 -> x22, starting transfers between devices: none -> 21.1 us  [swap(): return lax.ppermute(array, axis, pairs)]
    all_gather x2 -> x0, blocking collectives: 13.9 us -> none  [the longest x1 7.65 us: body(): lax.all_gather(normed, 'dp', axis=0, tiled=True)]
    dot_general x3 -> x0, matrix products: 10.3 us -> none  [the longest x1 9.32 us: run_experts(): jnp.dot(hidden, w_second, preferred_element_type=jnp.float32)]
    unnamed x8 -> x14, local copies, waits for them, and re-layouts: 0.19 us -> 7.11 us
    pallas_call x0 -> x3, Pallas kernels: none -> 6.53 us  [the longest x2 4.71 us: ffn(): pl.pallas_call(functools.partial(ffn_kernel, experts, count), out_shape=(...]
  transfers between devices with their start and end apart: 1 -> 22, of which waited for: 1 -> 13; matrix products, arithmetic and copies ran while one was open for 0% -> 0% of each run, Pallas kernels for 0% -> 7%
where the time goes in v1:
time: 66.8 us; the launch traced here: 66.5 us
  waiting for transfers between devices  30.6 us (46%)
  starting transfers between devices  21.1 us (32%)
  local copies, waits for them, and re-layouts  7.11 us (11%)
  Pallas kernels  6.53 us (10%)
  other arithmetic  1.05 us (2%)
    ppermute x22, waiting for transfers between devices, swap(): return lax.ppermute(array, axis, pairs)  30.6 us
    ppermute x22, starting transfers between devices, swap(): return lax.ppermute(array, axis, pairs)  21.1 us
    unnamed x14, local copies, waits for them, and re-layouts  7.11 us
    pallas_call x2, Pallas kernels, ffn(): pl.pallas_call(functools.partial(ffn_kernel, experts, count), out_shape=(...  4.71 us
    pallas_call x1, Pallas kernels, norm_and_pack(): pl.pallas_call(functools.partial(norm_kernel, experts), out_shape=jax.Sha...  1.82 us
  transfers between devices with their start and end apart: 22, of which 13 were waited for; matrix products, arithmetic and copies ran while one was open for 0% of the time, Pallas kernels for 7%

profile of v1, /device:TPU:0, one launch (start us, length us, event | category | flops | bytes accessed | tf_op | source)
XLA Modules:
  0.0 66.5 jit_solution(8450187049895735058)
XLA Ops:
  0.0 1.4 %copy.7.routing_ref = s32[32,2]{1,0:T(8,128)} copy(s32[32,2]{0,1:T(2,128)} %param.7) | data formatting | bytes 512 | tf_op args[1]
  1.4 1.4 %copy.8.gates_ref = f32[32,2]{1,0:T(8,128)} copy(f32[32,2]{0,1:T(2,128)} %param.8) | data formatting | bytes 512 | tf_op args[2]
  2.7 1.8 %norm.1.refs_0_ = bf16[32,2176]{1,0:T(8,128)(2,1)} custom-call(bf16[32,2048]{1,0:T(8,128)(2,1)} %tokens_ref.1, s32[32,2]{1,0:T(8,128)} %copy.7.routing_ref, f32[32,2]{1,0:T(8,128)} %copy.8.gates_ref, f32[1,2048]{1,0:T(1,128)} %bitcast.8), custom_call_target="tpu_custom_call" | custom-call | tf_op jit(solution)/shard_map/norm/pallas_call | solution.py:38
  4.5 4.0 %collective-permute-start.10 = (bf16[32,2176]{1,0:T(8,128)(2,1)}, bf16[32,2176]{1,0:T(8,128)(2,1)S(1)}, u32[]{:S(2)}, u32[]{:S(2)}) collective-permute-start(bf16[32,2176]{1,0:T(8,128)(2,1)} %norm.1.refs_0_), channel_id=1, source_target_pairs={{0,8},{4,12},{8,0},{12,4},{1,9},{5,13},{9,1},{13,5},{2,10},{6,14},... | collective-permute-start | bytes 417800 | tf_op jit(solution)/shard_map/ppermute | solution.py:99
  8.6 1.3 %collective-permute-start.11 = (bf16[32,2176]{1,0:T(8,128)(2,1)}, bf16[32,2176]{1,0:T(8,128)(2,1)S(1)}, u32[]{:S(2)}, u32[]{:S(2)}) collective-permute-start(bf16[32,2176]{1,0:T(8,128)(2,1)} %norm.1.refs_0_), channel_id=1, source_target_pairs={{0,12},{4,8},{8,4},{12,0},{1,13},{5,9},{9,5},{13,1},{2,14},{6,10},... | collective-permute-start | bytes 417800 | tf_op jit(solution)/shard_map/ppermute | solution.py:99
  9.9 9.3 %collective-permute-done.10.refs_0_ = bf16[32,2176]{1,0:T(8,128)(2,1)S(1)} collective-permute-done((bf16[32,2176]{1,0:T(8,128)(2,1)}, bf16[32,2176]{1,0:T(8,128)(2,1)S(1)}, u32[]{:S(2)}, u32[]{:S(2)}) %collective-permute-start.10) | collective-permute-done | bytes 139296 | tf_op jit(solution)/shard_map/ppermute | solution.py:99
  19.3 1.8 %collective-permute-start.12 = (bf16[32,2176]{1,0:T(8,128)(2,1)S(1)}, bf16[32,2176]{1,0:T(8,128)(2,1)S(1)}, u32[]{:S(2)}, u32[]{:S(2)}) collective-permute-start(bf16[32,2176]{1,0:T(8,128)(2,1)S(1)} %collective-permute-done.10.refs_0_), channel_id=1, source_target_pairs={{0,2},{1,3},{2,0},{3,1},{4,6},{5,7},{6,4},{7,5},{8,10},{9,11},{10,... | collective-permute-start | bytes 417800 | tf_op jit(solution)/shard_map/ppermute | solution.py:99
  21.3 2.4 %collective-permute-start = (bf16[32,2176]{1,0:T(8,128)(2,1)}, bf16[32,2176]{1,0:T(8,128)(2,1)S(1)}, u32[]{:S(2)}, u32[]{:S(2)}) collective-permute-start(bf16[32,2176]{1,0:T(8,128)(2,1)} %norm.1.refs_0_), channel_id=1, source_target_pairs={{0,4},{4,0},{8,12},{12,8},{1,5},{5,1},{9,13},{13,9},{2,6},{6,2},{1... | collective-permute-start | bytes 417800 | tf_op jit(solution)/shard_map/ppermute | solution.py:99
  24.8 1.5 %collective-permute-done.13.refs_3_ = bf16[32,2176]{1,0:T(8,128)(2,1)S(1)} collective-permute-done((bf16[32,2176]{1,0:T(8,128)(2,1)S(1)}, bf16[32,2176]{1,0:T(8,128)(2,1)S(1)}, u32[]{:S(2)}, u32[]{:S(2)}) %collective-permute-start.13) | collective-permute-done | bytes 139296 | tf_op jit(solution)/shard_map/ppermute | solution.py:99
  26.3 1.2 %collective-permute-done.refs_1_ = bf16[32,2176]{1,0:T(8,128)(2,1)S(1)} collective-permute-done((bf16[32,2176]{1,0:T(8,128)(2,1)}, bf16[32,2176]{1,0:T(8,128)(2,1)S(1)}, u32[]{:S(2)}, u32[]{:S(2)}) %collective-permute-start) | collective-permute-done | bytes 139296 | tf_op jit(solution)/shard_map/ppermute | solution.py:99
  28.4 1.2 %collective-permute-start.2 = (bf16[32,2176]{1,0:T(8,128)(2,1)S(1)}, bf16[32,2176]{1,0:T(8,128)(2,1)S(1)}, u32[]{:S(2)}, u32[]{:S(2)}) collective-permute-start(bf16[32,2176]{1,0:T(8,128)(2,1)S(1)} %collective-permute-done.refs_1_), channel_id=1, source_target_pairs={{0,2},{1,3},{2,0},{3,1},{4,6},{5,7},{6,4},{7,5},{8,10},{9,11},{10,... | collective-permute-start | bytes 417800 | tf_op jit(solution)/shard_map/ppermute | solution.py:99
  29.6 2.2 %copy-done = bf16[1,2048,1024]{2,1,0:T(8,128)(2,1)S(1)} copy-done((bf16[1,2048,1024]{2,1,0:T(8,128)(2,1)S(1)}, bf16[1,2048,1024]{2,1,0:T(8,128)(2,1)}, u32[]{:S(2)}) %copy-start) | copy-done | bytes 4194328
  31.8 2.2 %copy-done.2 = bf16[1,1024,2048]{2,1,0:T(8,128)(2,1)S(1)} copy-done((bf16[1,1024,2048]{2,1,0:T(8,128)(2,1)S(1)}, bf16[1,1024,2048]{2,1,0:T(8,128)(2,1)}, u32[]{:S(2)}) %copy-start.2) | copy-done | bytes 4194328
  34.0 2.4 %ffn.3 = (bf16[128,2048]{1,0:T(8,128)(2,1)S(1)}, bf16[128,2048]{1,0:T(8,128)(2,1)S(1)}) custom-call(s32[1]{0:T(128)} %bitcast.expert_ref, bf16[32,2176]{1,0:T(8,128)(2,1)S(1)} %collective-permute-done.10.refs_0_, bf16[32,2176]{1,0:T(8,128)(2,1)S(1)} %collective-permute-done.11.refs_1_, bf16[32,2176]{1,0:T(8,128)(2,1)S(1)} %collective-permute-done.12.refs_2_, ...), custom_call_target="tpu_custom_call" | custom-call | flops 2147483648 | bytes 8388608 | tf_op jit(solution)/shard_map/ffn/pallas_call | solution.py:80
  37.5 1.0 %collective-permute-done.3.refs_4_ = bf16[32,2176]{1,0:T(8,128)(2,1)S(1)} collective-permute-done((bf16[32,2176]{1,0:T(8,128)(2,1)S(1)}, bf16[32,2176]{1,0:T(8,128)(2,1)S(1)}, u32[]{:S(2)}, u32[]{:S(2)}) %collective-permute-start.3) | collective-permute-done | bytes 139296 | tf_op jit(solution)/shard_map/ppermute | solution.py:99
  39.1 2.4 %ffn.2 = (bf16[128,2048]{1,0:T(8,128)(2,1)S(1)}, bf16[128,2048]{1,0:T(8,128)(2,1)S(1)}) custom-call(s32[1]{0:T(128)} %bitcast.expert_ref, bf16[32,2176]{1,0:T(8,128)(2,1)S(1)} %copy-done.4, bf16[32,2176]{1,0:T(8,128)(2,1)S(1)} %collective-permute-done.refs_1_, bf16[32,2176]{1,0:T(8,128)(2,1)S(1)} %collective-permute-done.1.refs_2_, ...), custom_call_target="tpu_custom_call" | custom-call | flops 2147483648 | bytes 8388608 | tf_op jit(solution)/shard_map/ffn/pallas_call | solution.py:80
  41.8 0.9 %collective-permute-start.19 = (bf16[64,2048]{1,0:T(8,128)(2,1)S(1)}, bf16[64,2048]{1,0:T(8,128)(2,1)S(1)}, u32[]{:S(2)}, u32[]{:S(2)}) collective-permute-start(bf16[64,2048]{1,0:T(8,128)(2,1)S(1)} %add_convert_fusion), channel_id=1, source_target_pairs={{0,2},{1,3},{2,0},{3,1},{4,6},{5,7},{6,4},{7,5},{8,10},{9,11},{10,... | collective-permute-start | bytes 786440 | tf_op jit(solution)/shard_map/ppermute | solution.py:99
  43.5 0.9 %collective-permute-start.8 = (bf16[64,2048]{1,0:T(8,128)(2,1)S(1)}, bf16[64,2048]{1,0:T(8,128)(2,1)S(1)}, u32[]{:S(2)}, u32[]{:S(2)}) collective-permute-start(bf16[64,2048]{1,0:T(8,128)(2,1)S(1)} %add_convert_fusion.1), channel_id=1, source_target_pairs={{0,2},{1,3},{2,0},{3,1},{4,6},{5,7},{6,4},{7,5},{8,10},{9,11},{10,... | collective-permute-start | bytes 786440 | tf_op jit(solution)/shard_map/ppermute | solution.py:99
  44.5 6.5 %collective-permute-done.19 = bf16[64,2048]{1,0:T(8,128)(2,1)S(1)} collective-permute-done((bf16[64,2048]{1,0:T(8,128)(2,1)S(1)}, bf16[64,2048]{1,0:T(8,128)(2,1)S(1)}, u32[]{:S(2)}, u32[]{:S(2)}) %collective-permute-start.19) | collective-permute-done | bytes 262176 | tf_op jit(solution)/shard_map/ppermute | solution.py:99
  51.1 3.3 %collective-permute-start.21 = (bf16[32,2048]{1,0:T(8,128)(2,1)S(1)}, bf16[32,2048]{1,0:T(8,128)(2,1)S(1)}, u32[]{:S(2)}, u32[]{:S(2)}) collective-permute-start(bf16[32,2048]{1,0:T(8,128)(2,1)S(1)} %get-tuple-element.14), channel_id=1, source_target_pairs={{0,12},{4,8},{8,4},{12,0},{1,13},{5,9},{9,5},{13,1},{2,14},{6,10},... | collective-permute-start | bytes 393224 | tf_op jit(solution)/shard_map/ppermute | solution.py:99
  54.7 1.3 %collective-permute-done.8 = bf16[64,2048]{1,0:T(8,128)(2,1)S(1)} collective-permute-done((bf16[64,2048]{1,0:T(8,128)(2,1)S(1)}, bf16[64,2048]{1,0:T(8,128)(2,1)S(1)}, u32[]{:S(2)}, u32[]{:S(2)}) %collective-permute-start.8) | collective-permute-done | bytes 262176 | tf_op jit(solution)/shard_map/ppermute | solution.py:99
  56.1 1.8 %collective-permute-start.9 = (bf16[32,2048]{1,0:T(8,128)(2,1)S(1)}, bf16[32,2048]{1,0:T(8,128)(2,1)S(1)}, u32[]{:S(2)}, u32[]{:S(2)}) collective-permute-start(bf16[32,2048]{1,0:T(8,128)(2,1)S(1)} %add_convert_fusion.5), channel_id=1, source_target_pairs={{0,4},{4,0},{8,12},{12,8},{1,5},{5,1},{9,13},{13,9},{2,6},{6,2},{1... | collective-permute-start | bytes 393224 | tf_op jit(solution)/shard_map/ppermute | solution.py:99
  57.9 1.2 %collective-permute-done.21 = bf16[32,2048]{1,0:T(8,128)(2,1)S(1)} collective-permute-done((bf16[32,2048]{1,0:T(8,128)(2,1)S(1)}, bf16[32,2048]{1,0:T(8,128)(2,1)S(1)}, u32[]{:S(2)}, u32[]{:S(2)}) %collective-permute-start.21) | collective-permute-done | bytes 131104 | tf_op jit(solution)/shard_map/ppermute | solution.py:99
  59.1 6.7 %collective-permute-done.20 = bf16[32,2048]{1,0:T(8,128)(2,1)S(1)} collective-permute-done((bf16[32,2048]{1,0:T(8,128)(2,1)S(1)}, bf16[32,2048]{1,0:T(8,128)(2,1)S(1)}, u32[]{:S(2)}, u32[]{:S(2)}) %collective-permute-start.20) | collective-permute-done | bytes 131104 | tf_op jit(solution)/shard_map/ppermute | solution.py:99
  (42 shorter events, 6.3 us)
Async XLA Ops:
  4.5 14.7 %collective-permute-start.10 = (bf16[32,2176]{1,0:T(8,128)(2,1)}, bf16[32,2176]{1,0:T(8,128)(2,1)S(1)}, u32[]{:S(2)}, u32[]{:S(2)}) collective-permute-start(bf16[32,2176]{1,0:T(8,128)(2,1)} %norm.1.refs_0_), channel_id=1, source_target_pairs={{0,8},{4,12},{8,0},{12,4},{1,9},{5,13},{9,1},{13,5},{2,10},{6,14},... | collective-permute-start | bytes 417800 | tf_op jit(solution)/shard_map/ppermute | solution.py:99
  8.6 12.5 %collective-permute-start.11 = (bf16[32,2176]{1,0:T(8,128)(2,1)}, bf16[32,2176]{1,0:T(8,128)(2,1)S(1)}, u32[]{:S(2)}, u32[]{:S(2)}) collective-permute-start(bf16[32,2176]{1,0:T(8,128)(2,1)} %norm.1.refs_0_), channel_id=1, source_target_pairs={{0,12},{4,8},{8,4},{12,0},{1,13},{5,9},{9,5},{13,1},{2,14},{6,10},... | collective-permute-start | bytes 417800 | tf_op jit(solution)/shard_map/ppermute | solution.py:99
  19.3 5.5 %collective-permute-start.12 = (bf16[32,2176]{1,0:T(8,128)(2,1)S(1)}, bf16[32,2176]{1,0:T(8,128)(2,1)S(1)}, u32[]{:S(2)}, u32[]{:S(2)}) collective-permute-start(bf16[32,2176]{1,0:T(8,128)(2,1)S(1)} %collective-permute-done.10.refs_0_), channel_id=1, source_target_pairs={{0,2},{1,3},{2,0},{3,1},{4,6},{5,7},{6,4},{7,5},{8,10},{9,11},{10,... | collective-permute-start | bytes 417800 | tf_op jit(solution)/shard_map/ppermute | solution.py:99
  21.1 5.2 %collective-permute-start.13 = (bf16[32,2176]{1,0:T(8,128)(2,1)S(1)}, bf16[32,2176]{1,0:T(8,128)(2,1)S(1)}, u32[]{:S(2)}, u32[]{:S(2)}) collective-permute-start(bf16[32,2176]{1,0:T(8,128)(2,1)S(1)} %collective-permute-done.11.refs_1_), channel_id=1, source_target_pairs={{0,2},{1,3},{2,0},{3,1},{4,6},{5,7},{6,4},{7,5},{8,10},{9,11},{10,... | collective-permute-start | bytes 417800 | tf_op jit(solution)/shard_map/ppermute | solution.py:99
  21.3 6.2 %collective-permute-start = (bf16[32,2176]{1,0:T(8,128)(2,1)}, bf16[32,2176]{1,0:T(8,128)(2,1)S(1)}, u32[]{:S(2)}, u32[]{:S(2)}) collective-permute-start(bf16[32,2176]{1,0:T(8,128)(2,1)} %norm.1.refs_0_), channel_id=1, source_target_pairs={{0,4},{4,0},{8,12},{12,8},{1,5},{5,1},{9,13},{13,9},{2,6},{6,2},{1... | collective-permute-start | bytes 417800 | tf_op jit(solution)/shard_map/ppermute | solution.py:99
  23.7 4.7 %collective-permute-start.14 = (bf16[32,2176]{1,0:T(8,128)(2,1)S(1)}, bf16[32,2176]{1,0:T(8,128)(2,1)S(1)}, u32[]{:S(2)}, u32[]{:S(2)}) collective-permute-start(bf16[32,2176]{1,0:T(8,128)(2,1)S(1)} %collective-permute-done.10.refs_0_), channel_id=1, source_target_pairs={{0,1},{1,0},{2,3},{3,2},{4,5},{5,4},{6,7},{7,6},{8,9},{9,8},{10,11... | collective-permute-start | bytes 417800 | tf_op jit(solution)/shard_map/ppermute | solution.py:99
  23.7 5.8 %collective-permute-start.15 = (bf16[32,2176]{1,0:T(8,128)(2,1)S(1)}, bf16[32,2176]{1,0:T(8,128)(2,1)S(1)}, u32[]{:S(2)}, u32[]{:S(2)}) collective-permute-start(bf16[32,2176]{1,0:T(8,128)(2,1)S(1)} %collective-permute-done.11.refs_1_), channel_id=1, source_target_pairs={{0,1},{1,0},{2,3},{3,2},{4,5},{5,4},{6,7},{7,6},{8,9},{9,8},{10,11... | collective-permute-start | bytes 417800 | tf_op jit(solution)/shard_map/ppermute | solution.py:99
  24.8 4.8 %collective-permute-start.16 = (bf16[32,2176]{1,0:T(8,128)(2,1)S(1)}, bf16[32,2176]{1,0:T(8,128)(2,1)S(1)}, u32[]{:S(2)}, u32[]{:S(2)}) collective-permute-start(bf16[32,2176]{1,0:T(8,128)(2,1)S(1)} %collective-permute-done.12.refs_2_), channel_id=1, source_target_pairs={{0,1},{1,0},{2,3},{3,2},{4,5},{5,4},{6,7},{7,6},{8,9},{9,8},{10,11... | collective-permute-start | bytes 417800 | tf_op jit(solution)/shard_map/ppermute | solution.py:99
  26.3 3.3 %collective-permute-start.17 = (bf16[32,2176]{1,0:T(8,128)(2,1)S(1)}, bf16[32,2176]{1,0:T(8,128)(2,1)S(1)}, u32[]{:S(2)}, u32[]{:S(2)}) collective-permute-start(bf16[32,2176]{1,0:T(8,128)(2,1)S(1)} %collective-permute-done.13.refs_3_), channel_id=1, source_target_pairs={{0,1},{1,0},{2,3},{3,2},{4,5},{5,4},{6,7},{7,6},{8,9},{9,8},{10,11... | collective-permute-start | bytes 417800 | tf_op jit(solution)/shard_map/ppermute | solution.py:99
  27.5 9.5 %collective-permute-start.1 = (bf16[32,2176]{1,0:T(8,128)(2,1)}, bf16[32,2176]{1,0:T(8,128)(2,1)S(1)}, u32[]{:S(2)}, u32[]{:S(2)}) collective-permute-start(bf16[32,2176]{1,0:T(8,128)(2,1)} %norm.1.refs_0_), channel_id=1, source_target_pairs={{0,2},{1,3},{2,0},{3,1},{4,6},{5,7},{6,4},{7,5},{8,10},{9,11},{10,... | collective-permute-start | bytes 417800 | tf_op jit(solution)/shard_map/ppermute | solution.py:99
  28.4 9.0 %collective-permute-start.2 = (bf16[32,2176]{1,0:T(8,128)(2,1)S(1)}, bf16[32,2176]{1,0:T(8,128)(2,1)S(1)}, u32[]{:S(2)}, u32[]{:S(2)}) collective-permute-start(bf16[32,2176]{1,0:T(8,128)(2,1)S(1)} %collective-permute-done.refs_1_), channel_id=1, source_target_pairs={{0,2},{1,3},{2,0},{3,1},{4,6},{5,7},{6,4},{7,5},{8,10},{9,11},{10,... | collective-permute-start | bytes 417800 | tf_op jit(solution)/shard_map/ppermute | solution.py:99
  34.0 5.2 %copy-start.3 = (bf16[1,1024,2048]{2,1,0:T(8,128)(2,1)S(1)}, bf16[1,1024,2048]{2,1,0:T(8,128)(2,1)}, u32[]{:S(2)}) copy-start(bf16[1,1024,2048]{2,1,0:T(8,128)(2,1)} %param.11) | copy-start | bytes 12582916
  36.3 29.4 %copy-start.5 = (bf16[32,2048]{1,0:T(8,128)(2,1)S(1)}, bf16[32,2048]{1,0:T(8,128)(2,1)}, u32[]{:S(2)}) copy-start(bf16[32,2048]{1,0:T(8,128)(2,1)} %tokens_ref.1) | copy-start | bytes 393220
  36.3 5.3 %collective-permute-start.18 = (bf16[128,2048]{1,0:T(8,128)(2,1)S(1)}, bf16[128,2048]{1,0:T(8,128)(2,1)S(1)}, u32[]{:S(2)}, u32[]{:S(2)}) collective-permute-start(bf16[128,2048]{1,0:T(8,128)(2,1)S(1)} %get-tuple-element.12), channel_id=1, source_target_pairs={{0,1},{1,0},{2,3},{3,2},{4,5},{5,4},{6,7},{7,6},{8,9},{9,8},{10,11... | collective-permute-start | bytes 1572872 | tf_op jit(solution)/shard_map/ppermute | solution.py:99
  36.4 2.1 %collective-permute-start.3 = (bf16[32,2176]{1,0:T(8,128)(2,1)S(1)}, bf16[32,2176]{1,0:T(8,128)(2,1)S(1)}, u32[]{:S(2)}, u32[]{:S(2)}) collective-permute-start(bf16[32,2176]{1,0:T(8,128)(2,1)S(1)} %copy-done.4), channel_id=1, source_target_pairs={{0,1},{1,0},{2,3},{3,2},{4,5},{5,4},{6,7},{7,6},{8,9},{9,8},{10,11... | collective-permute-start | bytes 417800 | tf_op jit(solution)/shard_map/ppermute | solution.py:99
  36.9 1.8 %collective-permute-start.4 = (bf16[32,2176]{1,0:T(8,128)(2,1)S(1)}, bf16[32,2176]{1,0:T(8,128)(2,1)S(1)}, u32[]{:S(2)}, u32[]{:S(2)}) collective-permute-start(bf16[32,2176]{1,0:T(8,128)(2,1)S(1)} %collective-permute-done.refs_1_), channel_id=1, source_target_pairs={{0,1},{1,0},{2,3},{3,2},{4,5},{5,4},{6,7},{7,6},{8,9},{9,8},{10,11... | collective-permute-start | bytes 417800 | tf_op jit(solution)/shard_map/ppermute | solution.py:99
  37.0 1.9 %collective-permute-start.5 = (bf16[32,2176]{1,0:T(8,128)(2,1)S(1)}, bf16[32,2176]{1,0:T(8,128)(2,1)S(1)}, u32[]{:S(2)}, u32[]{:S(2)}) collective-permute-start(bf16[32,2176]{1,0:T(8,128)(2,1)S(1)} %collective-permute-done.1.refs_2_), channel_id=1, source_target_pairs={{0,1},{1,0},{2,3},{3,2},{4,5},{5,4},{6,7},{7,6},{8,9},{9,8},{10,11... | collective-permute-start | bytes 417800 | tf_op jit(solution)/shard_map/ppermute | solution.py:99
  37.4 1.7 %collective-permute-start.6 = (bf16[32,2176]{1,0:T(8,128)(2,1)S(1)}, bf16[32,2176]{1,0:T(8,128)(2,1)S(1)}, u32[]{:S(2)}, u32[]{:S(2)}) collective-permute-start(bf16[32,2176]{1,0:T(8,128)(2,1)S(1)} %collective-permute-done.2.refs_3_), channel_id=1, source_target_pairs={{0,1},{1,0},{2,3},{3,2},{4,5},{5,4},{6,7},{7,6},{8,9},{9,8},{10,11... | collective-permute-start | bytes 417800 | tf_op jit(solution)/shard_map/ppermute | solution.py:99
  41.5 2.0 %collective-permute-start.7 = (bf16[128,2048]{1,0:T(8,128)(2,1)S(1)}, bf16[128,2048]{1,0:T(8,128)(2,1)S(1)}, u32[]{:S(2)}, u32[]{:S(2)}) collective-permute-start(bf16[128,2048]{1,0:T(8,128)(2,1)S(1)} %get-tuple-element.10), channel_id=1, source_target_pairs={{0,1},{1,0},{2,3},{3,2},{4,5},{5,4},{6,7},{7,6},{8,9},{9,8},{10,11... | collective-permute-start | bytes 1572872 | tf_op jit(solution)/shard_map/ppermute | solution.py:99
  41.8 9.2 %collective-permute-start.19 = (bf16[64,2048]{1,0:T(8,128)(2,1)S(1)}, bf16[64,2048]{1,0:T(8,128)(2,1)S(1)}, u32[]{:S(2)}, u32[]{:S(2)}) collective-permute-start(bf16[64,2048]{1,0:T(8,128)(2,1)S(1)} %add_convert_fusion), channel_id=1, source_target_pairs={{0,2},{1,3},{2,0},{3,1},{4,6},{5,7},{6,4},{7,5},{8,10},{9,11},{10,... | collective-permute-start | bytes 786440 | tf_op jit(solution)/shard_map/ppermute | solution.py:99
  43.5 12.5 %collective-permute-start.8 = (bf16[64,2048]{1,0:T(8,128)(2,1)S(1)}, bf16[64,2048]{1,0:T(8,128)(2,1)S(1)}, u32[]{:S(2)}, u32[]{:S(2)}) collective-permute-start(bf16[64,2048]{1,0:T(8,128)(2,1)S(1)} %add_convert_fusion.1), channel_id=1, source_target_pairs={{0,2},{1,3},{2,0},{3,1},{4,6},{5,7},{6,4},{7,5},{8,10},{9,11},{10,... | collective-permute-start | bytes 786440 | tf_op jit(solution)/shard_map/ppermute | solution.py:99
  51.1 8.0 %collective-permute-start.21 = (bf16[32,2048]{1,0:T(8,128)(2,1)S(1)}, bf16[32,2048]{1,0:T(8,128)(2,1)S(1)}, u32[]{:S(2)}, u32[]{:S(2)}) collective-permute-start(bf16[32,2048]{1,0:T(8,128)(2,1)S(1)} %get-tuple-element.14), channel_id=1, source_target_pairs={{0,12},{4,8},{8,4},{12,0},{1,13},{5,9},{9,5},{13,1},{2,14},{6,10},... | collective-permute-start | bytes 393224 | tf_op jit(solution)/shard_map/ppermute | solution.py:99
  54.4 11.4 %collective-permute-start.20 = (bf16[32,2048]{1,0:T(8,128)(2,1)S(1)}, bf16[32,2048]{1,0:T(8,128)(2,1)S(1)}, u32[]{:S(2)}, u32[]{:S(2)}) collective-permute-start(bf16[32,2048]{1,0:T(8,128)(2,1)S(1)} %get-tuple-element.13), channel_id=1, source_target_pairs={{0,8},{4,12},{8,0},{12,4},{1,9},{5,13},{9,1},{13,5},{2,10},{6,14},... | collective-permute-start | bytes 393224 | tf_op jit(solution)/shard_map/ppermute | solution.py:99
  56.1 9.7 %collective-permute-start.9 = (bf16[32,2048]{1,0:T(8,128)(2,1)S(1)}, bf16[32,2048]{1,0:T(8,128)(2,1)S(1)}, u32[]{:S(2)}, u32[]{:S(2)}) collective-permute-start(bf16[32,2048]{1,0:T(8,128)(2,1)S(1)} %add_convert_fusion.5), channel_id=1, source_target_pairs={{0,4},{4,0},{8,12},{12,8},{1,5},{5,1},{9,13},{13,9},{2,6},{6,2},{1... | collective-permute-start | bytes 393224 | tf_op jit(solution)/shard_map/ppermute | solution.py:99
  (4 other events, 12.0 us)

commit v2 on v1

--- a/solution.py
+++ b/solution.py
@@ -9,89 +9,237 @@
 
 LANES = 128
 GATE_TERMS = 3
-
-
-def norm_kernel(experts, tokens_ref, routing_ref, gates_ref, gain_ref, out_ref):
+VMEM = pl.BlockSpec(memory_space=pltpu.VMEM)
+SMALL = pltpu.CompilerParams(vmem_limit_bytes=4 * 1024 * 1024)
+CHEAP = pl.CostEstimate(flops=1, bytes_accessed=1, transcendentals=0)
+DEAR = pl.CostEstimate(flops=10**11, bytes_accessed=1, transcendentals=0)
+ANY = pl.BlockSpec(memory_space=pl.ANY)
+
+
+def in_hbm(array):
+    return pltpu.with_memory_space_constraint(array, pltpu.HBM)
+
+
+def in_vmem(array):
+    return pltpu.with_memory_space_constraint(array, pltpu.VMEM)
+
+
+def norm_kernel(experts, *refs):
+    sources, out_ref, targets, sems = refs[:4], refs[4], refs[5:9], refs[9]
+    copies = [
+        pltpu.make_async_copy(source, target, sems.at[i])
+        for i, (source, target) in enumerate(zip(sources, targets))
+    ]
+    for copy in copies:
+        copy.start()
+    for copy in copies:
+        copy.wait()
+    tokens_ref, routing_ref, gates_ref, gain_ref = targets
     width = tokens_ref.shape[1]
     values = tokens_ref[...].astype(jnp.float32)
     center = values - jnp.mean(values, axis=1, keepdims=True)
     variance = jnp.mean(center * center, axis=1, keepdims=True)
     normed = center * lax.rsqrt(variance + 1e-05) * gain_ref[...]
     out_ref[:, :width] = normed.astype(jnp.bfloat16)
-    lane = lax.broadcasted_iota(jnp.int32, (tokens_ref.shape[0], LANES), 1)
+    lane = lax.broadcasted_iota(jnp.int32, (LANES, tokens_ref.shape[0]), 0)
     expert = lax.rem(lane, experts)
     term = lax.div(lane, experts)
     gate = jnp.zeros(lane.shape, jnp.float32)
-    for k in range(routing_ref.shape[1]):
-        gate += jnp.where(routing_ref[:, k : k + 1] == expert, gates_ref[:, k : k + 1], 0.0)
+    for k in range(routing_ref.shape[0]):
+        gate += jnp.where(routing_ref[k : k + 1, :] == expert, gates_ref[k : k + 1, :], 0.0)
     rest = gate
     packed = jnp.zeros(lane.shape, jnp.float32)
     for i in range(GATE_TERMS):
         part = rest.astype(jnp.bfloat16).astype(jnp.float32)
         packed = jnp.where(term == i, part, packed)
         rest = rest - part
-    out_ref[:, width:] = packed.astype(jnp.bfloat16)
+    out_ref[:, width:] = packed.T.astype(jnp.bfloat16)
 
 
 def norm_and_pack(tokens, routing, gates, ln_gain, experts):
     rows, width = tokens.shape
+    arrays = (tokens, routing.T, gates.T, ln_gain.reshape(1, width))
     return pl.pallas_call(
         functools.partial(norm_kernel, experts),
-        out_shape=jax.ShapeDtypeStruct((rows, width + LANES), jnp.bfloat16),
+        out_shape=pltpu.VMEM((rows, width + LANES), jnp.bfloat16),
+        in_specs=[ANY] * 4,
+        out_specs=VMEM,
+        scratch_shapes=[pltpu.VMEM(a.shape, a.dtype) for a in arrays]
+        + [pltpu.SemaphoreType.DMA((4,))],
+        compiler_params=SMALL,
+        cost_estimate=CHEAP,
         name="norm",
-    )(tokens, routing, gates, ln_gain.reshape(1, width))
-
-
-def ffn_kernel(experts, pieces, expert_ref, *refs):
+    )(*[in_hbm(a) for a in arrays])
+
+
+def join_kernel(pieces, *refs):
+    at = 0
+    for ref in refs[:pieces]:
+        refs[-1][at : at + ref.shape[0], :] = ref[...]
+        at += ref.shape[0]
+
+
+def join(arrays, behind=(), cost=CHEAP):
+    rows, width = sum(a.shape[0] for a in arrays), arrays[0].shape[1]
+    return pl.pallas_call(
+        functools.partial(join_kernel, len(arrays)),
+        out_shape=pltpu.VMEM((rows, width), arrays[0].dtype),
+        in_specs=[VMEM] * len(arrays) + [ANY] * len(behind),
+        out_specs=VMEM,
+        compiler_params=SMALL,
+        cost_estimate=cost,
+        name="join",
+    )(*arrays, *behind)
+
+
+def gate_column(experts, expert_ref, tail):
+    lane = lax.broadcasted_iota(jnp.int32, tail.shape, 1)
+    chosen = (lax.rem(lane, experts) == expert_ref[0]) & (lane < GATE_TERMS * experts)
+    return jnp.sum(jnp.where(chosen, tail.astype(jnp.float32), 0.0), axis=1, keepdims=True)
+
+
+def load_ffn_kernel(
+    experts, cuts, expert_ref, kept_ref, sent_ref, first_ref, second_ref, *refs
+):
+    keep_ref, send_ref, weights_ref, rows_ref, hidden_ref, total_ref, sems = refs
+    width, units = first_ref.shape
+    copies = []
+    for j in range(cuts):
+        size = width // cuts
+        part = pl.ds(j * size, size)
+        copies.append(
+            [pltpu.make_async_copy(first_ref.at[part], weights_ref.at[part], sems.at[0, j])]
+        )
+    panels = second_ref.shape[1] // units
+    for j in range(cuts):
+        size = units // cuts
+        copies.append(
+            [
+                pltpu.make_async_copy(
+                    second_ref.at[pl.ds(j * size, size), pl.ds(i * units, units)],
+                    weights_ref.at[pl.ds(width + i * units + j * size, size)],
+                    sems.at[1 + i, j],
+                )
+                for i in range(panels)
+            ]
+        )
+    for group in copies:
+        for copy in group:
+            copy.start()
+    half = kept_ref.shape[0]
+    rows_ref[:half, :] = kept_ref[...]
+    rows_ref[half:, :] = sent_ref[...]
+    gate = gate_column(experts, expert_ref, rows_ref[:, width:])
+    for j in range(cuts):
+        for copy in copies[j]:
+            copy.wait()
+        size = width // cuts
+        part = slice(j * size, (j + 1) * size)
+        dot = jnp.dot(
+            rows_ref[:, part], weights_ref[part, :], preferred_element_type=jnp.float32
+        )
+        if j == 0:
+            total_ref[:, :units] = dot
+        else:
+            total_ref[:, :units] += dot
+    hidden_ref[...] = jnp.maximum(total_ref[:, :units], 0.0).astype(jnp.bfloat16)
+    for j in range(cuts):
+        for copy in copies[cuts + j]:
+            copy.wait()
+        size = units // cuts
+        part = slice(j * size, (j + 1) * size)
+        for i in range(panels):
+            start = width + i * units + j * size
+            columns = slice(i * units, (i + 1) * units)
+            dot = jnp.dot(
+                hidden_ref[:, part],
+                weights_ref[start : start + size, :],
+                preferred_element_type=jnp.float32,
+            )
+            if j > 0:
+                dot += total_ref[:, columns]
+            if j < cuts - 1:
+                total_ref[:, columns] = dot
+            else:
+                out = (dot * gate).astype(jnp.bfloat16)
+                keep_ref[:, columns] = out[:half]
+                send_ref[:, columns] = out[half:]
+
+
+def load_ffn(kept, sent, w_first, w_second, experts, expert):
+    width, units = w_first.shape
+    half, cuts = kept.shape[0], 4
+    out = jax.ShapeDtypeStruct((half, width), jnp.bfloat16)
+    return pl.pallas_call(
+        functools.partial(load_ffn_kernel, experts, cuts),
+        out_shape=(out, out, pltpu.VMEM((2 * width, units), w_first.dtype)),
+        in_specs=[pl.BlockSpec(memory_space=pltpu.SMEM), VMEM, VMEM, ANY, ANY],
+        out_specs=(VMEM, VMEM, VMEM),
+        scratch_shapes=[
+            pltpu.VMEM((2 * half, width + LANES), jnp.bfloat16),
+            pltpu.VMEM((2 * half, units), jnp.bfloat16),
+            pltpu.VMEM((2 * half, width), jnp.float32),
+            pltpu.SemaphoreType.DMA((1 + width // units, cuts)),
+        ],
+        compiler_params=pltpu.CompilerParams(vmem_limit_bytes=16 * 1024 * 1024),
+        cost_estimate=pl.CostEstimate(
+            flops=8 * half * width * units, bytes_accessed=4 * width * units, transcendentals=0
+        ),
+        name="load_ffn",
+    )(expert, kept, sent, in_hbm(w_first), in_hbm(w_second))
+
+
+def ffn_kernel(experts, pieces, skipped, expert_ref, *refs):
     kept, sent = refs[:pieces], refs[pieces : 2 * pieces]
-    w_first, w_second = refs[2 * pieces : 2 * pieces + 2]
-    keep_ref, send_ref, rows_ref, hidden_ref = refs[2 * pieces + 2 :]
-    width, units = w_first.shape
+    weights = refs[2 * pieces]
+    keep_ref, send_ref, rows_ref, hidden_ref = refs[2 * pieces + 1 + skipped :]
+    width, units = keep_ref.shape[1], weights.shape[1]
     at = 0
     for ref in kept + sent:
         rows_ref[at : at + ref.shape[0], :] = ref[...]
         at += ref.shape[0]
     half = at // 2
-    lane = lax.broadcasted_iota(jnp.int32, (at, LANES), 1)
-    chosen = (lax.rem(lane, experts) == expert_ref[0]) & (lane < GATE_TERMS * experts)
-    tail = rows_ref[:, width:].astype(jnp.float32)
-    gate = jnp.sum(jnp.where(chosen, tail, 0.0), axis=1, keepdims=True)
+    gate = gate_column(experts, expert_ref, rows_ref[:, width:])
     step = 256
     for j in range(0, units, step):
         dot = jnp.dot(
-            rows_ref[:, :width], w_first[:, j : j + step], preferred_element_type=jnp.float32
+            rows_ref[:, :width], weights[:width, j : j + step], preferred_element_type=jnp.float32
         )
         hidden_ref[:, j : j + step] = jnp.maximum(dot, 0.0).astype(jnp.bfloat16)
     for j in range(0, width, step):
+        start, column = width + j // units * units, j % units
         dot = jnp.dot(
-            hidden_ref[...], w_second[:, j : j + step], preferred_element_type=jnp.float32
+            hidden_ref[...],
+            weights[start : start + units, column : column + step],
+            preferred_element_type=jnp.float32,
         )
         out = (dot * gate).astype(jnp.bfloat16)
         send_ref[:, j : j + step] = out[half:]
         keep_ref[:, j : j + step] = out[:half]
 
 
-def ffn(kept, sent, w_first, w_second, experts, expert):
-    width, units = w_first.shape
+def ffn(kept, sent, weights, experts, expert, behind):
+    width, units = weights.shape[0] // 2, weights.shape[1]
     half = sum(a.shape[0] for a in kept)
     out = jax.ShapeDtypeStruct((half, width), jnp.bfloat16)
-    vmem = pl.BlockSpec(memory_space=pltpu.VMEM)
     count = len(kept)
     return pl.pallas_call(
-        functools.partial(ffn_kernel, experts, count),
+        functools.partial(ffn_kernel, experts, count, len(behind)),
         out_shape=(out, out),
-        in_specs=[pl.BlockSpec(memory_space=pltpu.SMEM)] + [vmem] * (2 * count + 2),
-        out_specs=(vmem, vmem),
+        in_specs=[pl.BlockSpec(memory_space=pltpu.SMEM)]
+        + [VMEM] * (2 * count + 1)
+        + [ANY] * len(behind),
+        out_specs=(VMEM, VMEM),
         scratch_shapes=[
             pltpu.VMEM((2 * half, width + LANES), jnp.bfloat16),
             pltpu.VMEM((2 * half, units), jnp.bfloat16),
         ],
-        compiler_params=pltpu.CompilerParams(vmem_limit_bytes=32 * 1024 * 1024),
+        compiler_params=pltpu.CompilerParams(vmem_limit_bytes=16 * 1024 * 1024),
         cost_estimate=pl.CostEstimate(
             flops=8 * half * width * units, bytes_accessed=4 * width * units, transcendentals=0
         ),
         name="ffn",
-    )(expert, *kept, *sent, w_first, w_second)
+    )(expert, *kept, *sent, in_vmem(weights), *behind)
 
 
 def swap(array, axis, distance):
@@ -101,39 +249,57 @@
 
 def add(*arrays):
     return sum(a.astype(jnp.float32) for a in arrays)
-
-
-GROUPS = ((0, 1), (2, 3))
 
 
 def dense_body(tokens, routing, gates, ln_gain, w_in, w_out):
     rows = tokens.shape[0]
     experts = lax.axis_size("expert")
     core_bit, chip_bit = 1, 2
-    w_first, w_second = w_in[0], w_out[0]
     expert = lax.axis_index("expert").reshape(1)
+
+    def run(kept, behind=()):
+        sent = swap(kept, "dp", core_bit)
+        keep, send = ffn([kept], [sent], weights, experts, expert, behind)
+        return keep, swap(send, "dp", core_bit)
+
+    def far_sum(pair, i, count):
+        at = slice((count + i) * rows, (count + i + 1) * rows)
+        return add(*[a[at] for a in pair]).astype(jnp.bfloat16)
+
+    def near_sum(pair, far, i):
+        at = slice(i * rows, (i + 1) * rows)
+        return add(*[a[at] for a in pair], swap(far, "dp", chip_bit))
+
     own = norm_and_pack(tokens, routing, gates, ln_gain, experts)
-    lane = [own] + [swap(own, "expert", k) for k in range(1, experts)]
-    across = [swap(a, "dp", chip_bit) for a in lane]
-    lane_other = [swap(a, "dp", core_bit) for a in lane]
-    across_other = [swap(a, "dp", core_bit) for a in across]
-    total = [None] * experts
-    for group in GROUPS:
-        kept = [lane[k] for k in group] + [across[k] for k in group]
-        sent = [lane_other[k] for k in group] + [across_other[k] for k in group]
-        keep, send = ffn(kept, sent, w_first, w_second, experts, expert)
-        back = swap(send, "dp", core_bit)
-        half = keep.shape[0] // 2
-        far = add(keep[half:], back[half:]).astype(jnp.bfloat16)
-        far_back = swap(far, "dp", chip_bit)
-        for i, k in enumerate(group):
-            at = slice(i * rows, (i + 1) * rows)
-            if k == 0:
-                total[k] = add(keep[at], back[at], far_back[at])
-            else:
-                block = add(keep[at], back[at], far_back[at]).astype(jnp.bfloat16)
-                total[k] = swap(block, "expert", k)
-    return add(tokens, *total).astype(jnp.bfloat16)
+    across0 = swap(own, "dp", chip_bit)
+    lane3, lane1 = swap(own, "expert", 3), swap(own, "expert", 1)
+    lane31 = join([lane3, lane1], [across0])
+    across31 = swap(lane31, "dp", chip_bit)
+    lane2 = swap(join([own], [lane31]), "expert", 2)
+    kept0 = join([own, across0], [lane31])
+    keep0, send0, weights = load_ffn(
+        kept0, swap(kept0, "dp", core_bit), w_in[0], w_out[0], experts, expert
+    )
+    pair0 = keep0, swap(send0, "dp", core_bit)
+    pair31 = run(join([lane31, across31], [pair0[0], lane2]))
+    across2 = swap(lane2, "dp", chip_bit)
+    kept2 = join([lane2, across2], [pair31[0]], DEAR)
+    far3 = join([far_sum(pair31, 0, 2)], [kept2])
+    pair2 = run(kept2, [far3])
+    far2 = far_sum(pair2, 0, 1)
+    far1 = join([far_sum(pair31, 1, 2)], [far2])
+    far0 = join([far_sum(pair0, 0, 1)], [far2])
+    near3 = near_sum(pair31, far3, 0).astype(jnp.bfloat16)
+    near2 = near_sum(pair2, far2, 0).astype(jnp.bfloat16)
+    near1 = near_sum(pair31, far1, 1).astype(jnp.bfloat16)
+    near0 = near_sum(pair0, far0, 0)
+    return add(
+        tokens,
+        near0,
+        swap(near3, "expert", 3),
+        swap(near1, "expert", 1),
+        swap(near2, "expert", 2),
+    ).astype(jnp.bfloat16)
 
 
 def layer_norm(tokens, ln_gain):

time: 66.8 us -> 54.6 us (0.82)
  local copies, waits for them, and re-layouts: 7.11 us -> 0.01 us
  waiting for transfers between devices: 30.6 us -> 25.8 us
  starting transfers between devices: 21.1 us -> 18.7 us
  Pallas kernels: 6.53 us -> 8.83 us
    unnamed x14 -> x2, local copies, waits for them, and re-layouts: 7.11 us -> 0.01 us
    ppermute x22 -> x19, waiting for transfers between devices: 30.6 us -> 25.8 us  [swap(): return lax.ppermute(array, axis, pairs)]
    ppermute x22 -> x19, starting transfers between devices: 21.1 us -> 18.7 us  [swap(): return lax.ppermute(array, axis, pairs)]
    pallas_call x3 -> x12, Pallas kernels: 6.53 us -> 8.83 us  [the longest x1 3.8 us: load_ffn(): pl.pallas_call(functools.partial(load_ffn_kernel, experts, cuts), out_sha...]
  transfers between devices with their start and end apart: 22 -> 19, of which waited for: 13 -> 15; matrix products, arithmetic and copies ran while one was open for 0% -> 1% of each run, Pallas kernels for 7% -> 14%
where the time goes in v2:
time: 54.6 us; the launch traced here: 54.5 us
  waiting for transfers between devices  25.8 us (47%)
  starting transfers between devices  18.7 us (34%)
  Pallas kernels  8.83 us (16%)
  other arithmetic  1.06 us (2%)
    ppermute x19, waiting for transfers between devices, swap(): return lax.ppermute(array, axis, pairs)  25.8 us
    ppermute x19, starting transfers between devices, swap(): return lax.ppermute(array, axis, pairs)  18.7 us
    pallas_call x1, Pallas kernels, load_ffn(): pl.pallas_call(functools.partial(load_ffn_kernel, experts, cuts), out_sha...  3.8 us
    pallas_call x2, Pallas kernels, ffn(): pl.pallas_call(functools.partial(ffn_kernel, experts, count, len(behind))...  3.72 us
    pallas_call x1, Pallas kernels, norm_and_pack(): pl.pallas_call(functools.partial(norm_kernel, experts), out_shape=pltpu.V...  1.17 us
  transfers between devices with their start and end apart: 19, of which 15 were waited for; matrix products, arithmetic and copies ran while one was open for 1% of the time, Pallas kernels for 14%

profile of v2, /device:TPU:0, one launch (start us, length us, event | category | flops | bytes accessed | tf_op | source)
XLA Modules:
  0.0 54.5 jit_solution(14636173788854054898)
XLA Ops:
  0.0 1.2 %norm.1.refs_0_ = bf16[32,2176]{1,0:T(8,128)(2,1)S(1)} custom-call(bf16[32,2048]{1,0:T(8,128)(2,1)} %refs_0_.1, s32[2,32]{1,0:T(2,128)} %bitcast.9, f32[2,32]{1,0:T(2,128)} %bitcast.10, f32[1,2048]{1,0:T(1,128)} %bitcast.8), custom_call_target="tpu_custom_call" | custom-call | flops 1 | bytes 1 | tf_op jit(solution)/shard_map/norm/pallas_call | solution.py:62
  1.2 3.0 %collective-permute-start = (bf16[32,2176]{1,0:T(8,128)(2,1)S(1)}, bf16[32,2176]{1,0:T(8,128)(2,1)S(1)}, u32[]{:S(2)}, u32[]{:S(2)}) collective-permute-start(bf16[32,2176]{1,0:T(8,128)(2,1)S(1)} %norm.1.refs_0_), channel_id=1, source_target_pairs={{0,2},{1,3},{2,0},{3,1},{4,6},{5,7},{6,4},{7,5},{8,10},{9,11},{10,... | collective-permute-start | bytes 417800 | tf_op jit(solution)/shard_map/ppermute | solution.py:247
  4.2 3.6 %collective-permute-start.1 = (bf16[32,2176]{1,0:T(8,128)(2,1)S(1)}, bf16[32,2176]{1,0:T(8,128)(2,1)S(1)}, u32[]{:S(2)}, u32[]{:S(2)}) collective-permute-start(bf16[32,2176]{1,0:T(8,128)(2,1)S(1)} %norm.1.refs_0_), channel_id=1, source_target_pairs={{0,12},{4,8},{8,4},{12,0},{1,13},{5,9},{9,5},{13,1},{2,14},{6,10},... | collective-permute-start | bytes 417800 | tf_op jit(solution)/shard_map/ppermute | solution.py:247
  7.9 4.7 %collective-permute-done.1.refs_0_ = bf16[32,2176]{1,0:T(8,128)(2,1)S(1)} collective-permute-done((bf16[32,2176]{1,0:T(8,128)(2,1)S(1)}, bf16[32,2176]{1,0:T(8,128)(2,1)S(1)}, u32[]{:S(2)}, u32[]{:S(2)}) %collective-permute-start.1) | collective-permute-done | bytes 139296 | tf_op jit(solution)/shard_map/ppermute | solution.py:247
  12.6 1.7 %collective-permute-done.2.refs_1_ = bf16[32,2176]{1,0:T(8,128)(2,1)S(1)} collective-permute-done((bf16[32,2176]{1,0:T(8,128)(2,1)S(1)}, bf16[32,2176]{1,0:T(8,128)(2,1)S(1)}, u32[]{:S(2)}, u32[]{:S(2)}) %collective-permute-start.2) | collective-permute-done | bytes 139296 | tf_op jit(solution)/shard_map/ppermute | solution.py:247
  14.4 0.6 %collective-permute-start.7 = (bf16[64,2176]{1,0:T(8,128)(2,1)S(1)}, bf16[64,2176]{1,0:T(8,128)(2,1)S(1)}, u32[]{:S(2)}, u32[]{:S(2)}) collective-permute-start(bf16[64,2176]{1,0:T(8,128)(2,1)S(1)} %join.8.refs_2_.refs_1_.refs_0_), channel_id=1, source_target_pairs={{0,2},{1,3},{2,0},{3,1},{4,6},{5,7},{6,4},{7,5},{8,10},{9,11},{10,... | collective-permute-start | bytes 835592 | tf_op jit(solution)/shard_map/ppermute | solution.py:247
  15.0 0.6 %collective-permute-start.5 = (bf16[32,2176]{1,0:T(8,128)(2,1)S(1)}, bf16[32,2176]{1,0:T(8,128)(2,1)S(1)}, u32[]{:S(2)}, u32[]{:S(2)}) collective-permute-start(bf16[32,2176]{1,0:T(8,128)(2,1)S(1)} %join.10), channel_id=1, source_target_pairs={{0,8},{4,12},{8,0},{12,4},{1,9},{5,13},{9,1},{13,5},{2,10},{6,14},... | collective-permute-start | bytes 417800 | tf_op jit(solution)/shard_map/ppermute | solution.py:247
  15.9 3.8 %load_ffn.1 = (bf16[64,2048]{1,0:T(8,128)(2,1)S(1)}, bf16[64,2048]{1,0:T(8,128)(2,1)S(1)}, bf16[4096,1024]{1,0:T(8,128)(2,1)S(1)}) custom-call(s32[1]{0:T(128)} %bitcast.expert_ref, bf16[64,2176]{1,0:T(8,128)(2,1)S(1)} %join.9.kept_ref, bf16[64,2176]{1,0:T(8,128)(2,1)S(1)} %collective-permute-done.3.sent_ref, bf16[2048,1024]{1,0:T(8,128)(2,1)} %bitcast.6, ...), custom_call_target="tpu_custom_call" | custom-call | flops 1073741824 | bytes 8388608 | tf_op jit(solution)/shard_map/load_ffn/pallas_call | solution.py:173
  19.7 5.0 %collective-permute-done.5.refs_3_.refs_0_ = bf16[32,2176]{1,0:T(8,128)(2,1)S(1)} collective-permute-done((bf16[32,2176]{1,0:T(8,128)(2,1)S(1)}, bf16[32,2176]{1,0:T(8,128)(2,1)S(1)}, u32[]{:S(2)}, u32[]{:S(2)}) %collective-permute-start.5) | collective-permute-done | bytes 139296 | tf_op jit(solution)/shard_map/ppermute | solution.py:247
  24.8 1.6 %collective-permute-start.6 = (bf16[32,2176]{1,0:T(8,128)(2,1)S(1)}, bf16[32,2176]{1,0:T(8,128)(2,1)S(1)}, u32[]{:S(2)}, u32[]{:S(2)}) collective-permute-start(bf16[32,2176]{1,0:T(8,128)(2,1)S(1)} %collective-permute-done.5.refs_3_.refs_0_), channel_id=1, source_target_pairs={{0,2},{1,3},{2,0},{3,1},{4,6},{5,7},{6,4},{7,5},{8,10},{9,11},{10,... | collective-permute-start | bytes 417800 | tf_op jit(solution)/shard_map/ppermute | solution.py:247
  26.8 2.4 %ffn.2 = (bf16[128,2048]{1,0:T(8,128)(2,1)S(1)}, bf16[128,2048]{1,0:T(8,128)(2,1)S(1)}) custom-call(s32[1]{0:T(128)} %bitcast.expert_ref, bf16[128,2176]{1,0:T(8,128)(2,1)S(1)} %join.11.refs_0_, bf16[128,2176]{1,0:T(8,128)(2,1)S(1)} %collective-permute-done.8.refs_1_, bf16[4096,1024]{1,0:T(8,128)(2,1)S(1)} %get-tuple-element.14.refs_2_), custom_call_target="tpu_custom_call" | custom-call | flops 2147483648 | bytes 8388608 | tf_op jit(solution)/shard_map/ffn/pallas_call | solution.py:226
  29.4 1.5 %collective-permute-done.6.refs_1_ = bf16[32,2176]{1,0:T(8,128)(2,1)S(1)} collective-permute-done((bf16[32,2176]{1,0:T(8,128)(2,1)S(1)}, bf16[32,2176]{1,0:T(8,128)(2,1)S(1)}, u32[]{:S(2)}, u32[]{:S(2)}) %collective-permute-start.6) | collective-permute-done | bytes 139296 | tf_op jit(solution)/shard_map/ppermute | solution.py:247
  31.2 1.6 %collective-permute-start.13 = (bf16[32,2048]{1,0:T(8,128)(2,1)S(1)}, bf16[32,2048]{1,0:T(8,128)(2,1)S(1)}, u32[]{:S(2)}, u32[]{:S(2)}) collective-permute-start(bf16[32,2048]{1,0:T(8,128)(2,1)S(1)} %join.13.refs_3_), channel_id=1, source_target_pairs={{0,2},{1,3},{2,0},{3,1},{4,6},{5,7},{6,4},{7,5},{8,10},{9,11},{10,... | collective-permute-start | bytes 393224 | tf_op jit(solution)/shard_map/ppermute | solution.py:247
  32.9 1.3 %ffn.3 = (bf16[64,2048]{1,0:T(8,128)(2,1)S(1)}, bf16[64,2048]{1,0:T(8,128)(2,1)S(1)}) custom-call(s32[1]{0:T(128)} %bitcast.expert_ref, bf16[64,2176]{1,0:T(8,128)(2,1)S(1)} %join.12.refs_1_.refs_0_, bf16[64,2176]{1,0:T(8,128)(2,1)S(1)} %collective-permute-done.9.refs_1_, bf16[4096,1024]{1,0:T(8,128)(2,1)S(1)} %get-tuple-element.14.refs_2_, ...), custom_call_target="tpu_custom_call" | custom-call | flops 1073741824 | bytes 8388608 | tf_op jit(solution)/shard_map/ffn/pallas_call | solution.py:226
  34.7 2.4 %collective-permute-done.13 = bf16[32,2048]{1,0:T(8,128)(2,1)S(1)} collective-permute-done((bf16[32,2048]{1,0:T(8,128)(2,1)S(1)}, bf16[32,2048]{1,0:T(8,128)(2,1)S(1)}, u32[]{:S(2)}, u32[]{:S(2)}) %collective-permute-start.13) | collective-permute-done | bytes 131104 | tf_op jit(solution)/shard_map/ppermute | solution.py:247
  37.2 1.6 %collective-permute-start.15 = (bf16[32,2048]{1,0:T(8,128)(2,1)S(1)}, bf16[32,2048]{1,0:T(8,128)(2,1)S(1)}, u32[]{:S(2)}, u32[]{:S(2)}) collective-permute-start(bf16[32,2048]{1,0:T(8,128)(2,1)S(1)} %join.15), channel_id=1, source_target_pairs={{0,2},{1,3},{2,0},{3,1},{4,6},{5,7},{6,4},{7,5},{8,10},{9,11},{10,... | collective-permute-start | bytes 393224 | tf_op jit(solution)/shard_map/ppermute | solution.py:247
  38.8 1.5 %collective-permute-start.14 = (bf16[32,2048]{1,0:T(8,128)(2,1)S(1)}, bf16[32,2048]{1,0:T(8,128)(2,1)S(1)}, u32[]{:S(2)}, u32[]{:S(2)}) collective-permute-start(bf16[32,2048]{1,0:T(8,128)(2,1)S(1)} %get-tuple-element.19), channel_id=1, source_target_pairs={{0,12},{4,8},{8,4},{12,0},{1,13},{5,9},{9,5},{13,1},{2,14},{6,10},... | collective-permute-start | bytes 393224 | tf_op jit(solution)/shard_map/ppermute | solution.py:247
  40.8 1.6 %collective-permute-start.12 = (bf16[32,2048]{1,0:T(8,128)(2,1)S(1)}, bf16[32,2048]{1,0:T(8,128)(2,1)S(1)}, u32[]{:S(2)}, u32[]{:S(2)}) collective-permute-start(bf16[32,2048]{1,0:T(8,128)(2,1)S(1)} %join.14), channel_id=1, source_target_pairs={{0,2},{1,3},{2,0},{3,1},{4,6},{5,7},{6,4},{7,5},{8,10},{9,11},{10,... | collective-permute-start | bytes 393224 | tf_op jit(solution)/shard_map/ppermute | solution.py:247
  42.7 1.6 %collective-permute-start.16 = (bf16[32,2048]{1,0:T(8,128)(2,1)S(1)}, bf16[32,2048]{1,0:T(8,128)(2,1)S(1)}, u32[]{:S(2)}, u32[]{:S(2)}) collective-permute-start(bf16[32,2048]{1,0:T(8,128)(2,1)S(1)} %add_convert_fusion.2), channel_id=1, source_target_pairs={{0,4},{4,0},{8,12},{12,8},{1,5},{5,1},{9,13},{13,9},{2,6},{6,2},{1... | collective-permute-start | bytes 393224 | tf_op jit(solution)/shard_map/ppermute | solution.py:247
  44.3 2.2 %collective-permute-done.17 = bf16[32,2048]{1,0:T(8,128)(2,1)S(1)} collective-permute-done((bf16[32,2048]{1,0:T(8,128)(2,1)S(1)}, bf16[32,2048]{1,0:T(8,128)(2,1)S(1)}, u32[]{:S(2)}, u32[]{:S(2)}) %collective-permute-start.17) | collective-permute-done | bytes 131104 | tf_op jit(solution)/shard_map/ppermute | solution.py:247
  47.0 0.8 %collective-permute-done.12 = bf16[32,2048]{1,0:T(8,128)(2,1)S(1)} collective-permute-done((bf16[32,2048]{1,0:T(8,128)(2,1)S(1)}, bf16[32,2048]{1,0:T(8,128)(2,1)S(1)}, u32[]{:S(2)}, u32[]{:S(2)}) %collective-permute-start.12) | collective-permute-done | bytes 131104 | tf_op jit(solution)/shard_map/ppermute | solution.py:247
  47.8 1.7 %collective-permute-done.16 = bf16[32,2048]{1,0:T(8,128)(2,1)S(1)} collective-permute-done((bf16[32,2048]{1,0:T(8,128)(2,1)S(1)}, bf16[32,2048]{1,0:T(8,128)(2,1)S(1)}, u32[]{:S(2)}, u32[]{:S(2)}) %collective-permute-start.16) | collective-permute-done | bytes 131104 | tf_op jit(solution)/shard_map/ppermute | solution.py:247
  49.6 4.1 %collective-permute-done.18 = bf16[32,2048]{1,0:T(8,128)(2,1)S(1)} collective-permute-done((bf16[32,2048]{1,0:T(8,128)(2,1)S(1)}, bf16[32,2048]{1,0:T(8,128)(2,1)S(1)}, u32[]{:S(2)}, u32[]{:S(2)}) %collective-permute-start.18) | collective-permute-done | bytes 131104 | tf_op jit(solution)/shard_map/ppermute | solution.py:247
  53.7 0.8 %add_convert_fusion = bf16[32,2048]{1,0:T(8,128)(2,1)} fusion(bf16[32,2048]{1,0:T(8,128)(2,1)S(1)} %collective-permute-done.18, bf16[32,2048]{1,0:T(8,128)(2,1)S(1)} %collective-permute-done.16, bf16[32,2048]{1,0:T(8,128)(2,1)S(1)} %collective-permute-done.14, bf16[32,2048]{1,0:T(8,128)(2,1)S(1)} %collective-permute-done.12, bf16[32,2048]{1,0:T(8,128)(2,1)S(1)} %copy-done, ...), kind=kLoop, calls=%fused_computation | loop fusion | flops 917504 | bytes 1048576 | tf_op jit(solution)/shard_map/convert_element_type | solution.py:302
  (35 shorter events, 3.6 us)
Async XLA Ops:
  1.2 6.7 %collective-permute-start = (bf16[32,2176]{1,0:T(8,128)(2,1)S(1)}, bf16[32,2176]{1,0:T(8,128)(2,1)S(1)}, u32[]{:S(2)}, u32[]{:S(2)}) collective-permute-start(bf16[32,2176]{1,0:T(8,128)(2,1)S(1)} %norm.1.refs_0_), channel_id=1, source_target_pairs={{0,2},{1,3},{2,0},{3,1},{4,6},{5,7},{6,4},{7,5},{8,10},{9,11},{10,... | collective-permute-start | bytes 417800 | tf_op jit(solution)/shard_map/ppermute | solution.py:247
  4.2 8.4 %collective-permute-start.1 = (bf16[32,2176]{1,0:T(8,128)(2,1)S(1)}, bf16[32,2176]{1,0:T(8,128)(2,1)S(1)}, u32[]{:S(2)}, u32[]{:S(2)}) collective-permute-start(bf16[32,2176]{1,0:T(8,128)(2,1)S(1)} %norm.1.refs_0_), channel_id=1, source_target_pairs={{0,12},{4,8},{8,4},{12,0},{1,13},{5,9},{9,5},{13,1},{2,14},{6,10},... | collective-permute-start | bytes 417800 | tf_op jit(solution)/shard_map/ppermute | solution.py:247
  7.8 6.5 %collective-permute-start.2 = (bf16[32,2176]{1,0:T(8,128)(2,1)S(1)}, bf16[32,2176]{1,0:T(8,128)(2,1)S(1)}, u32[]{:S(2)}, u32[]{:S(2)}) collective-permute-start(bf16[32,2176]{1,0:T(8,128)(2,1)S(1)} %norm.1.refs_0_), channel_id=1, source_target_pairs={{0,4},{4,0},{8,12},{12,8},{1,5},{5,1},{9,13},{13,9},{2,6},{6,2},{1... | collective-permute-start | bytes 417800 | tf_op jit(solution)/shard_map/ppermute | solution.py:247
  14.3 1.6 %collective-permute-start.3 = (bf16[64,2176]{1,0:T(8,128)(2,1)S(1)}, bf16[64,2176]{1,0:T(8,128)(2,1)S(1)}, u32[]{:S(2)}, u32[]{:S(2)}) collective-permute-start(bf16[64,2176]{1,0:T(8,128)(2,1)S(1)} %join.9.kept_ref), channel_id=1, source_target_pairs={{0,1},{1,0},{2,3},{3,2},{4,5},{5,4},{6,7},{7,6},{8,9},{9,8},{10,11... | collective-permute-start | bytes 835592 | tf_op jit(solution)/shard_map/ppermute | solution.py:247
  14.4 10.3 %collective-permute-start.7 = (bf16[64,2176]{1,0:T(8,128)(2,1)S(1)}, bf16[64,2176]{1,0:T(8,128)(2,1)S(1)}, u32[]{:S(2)}, u32[]{:S(2)}) collective-permute-start(bf16[64,2176]{1,0:T(8,128)(2,1)S(1)} %join.8.refs_2_.refs_1_.refs_0_), channel_id=1, source_target_pairs={{0,2},{1,3},{2,0},{3,1},{4,6},{5,7},{6,4},{7,5},{8,10},{9,11},{10,... | collective-permute-start | bytes 835592 | tf_op jit(solution)/shard_map/ppermute | solution.py:247
  15.0 9.7 %collective-permute-start.5 = (bf16[32,2176]{1,0:T(8,128)(2,1)S(1)}, bf16[32,2176]{1,0:T(8,128)(2,1)S(1)}, u32[]{:S(2)}, u32[]{:S(2)}) collective-permute-start(bf16[32,2176]{1,0:T(8,128)(2,1)S(1)} %join.10), channel_id=1, source_target_pairs={{0,8},{4,12},{8,0},{12,4},{1,9},{5,13},{9,1},{13,5},{2,10},{6,14},... | collective-permute-start | bytes 417800 | tf_op jit(solution)/shard_map/ppermute | solution.py:247
  24.7 2.0 %collective-permute-start.8 = (bf16[128,2176]{1,0:T(8,128)(2,1)S(1)}, bf16[128,2176]{1,0:T(8,128)(2,1)S(1)}, u32[]{:S(2)}, u32[]{:S(2)}) collective-permute-start(bf16[128,2176]{1,0:T(8,128)(2,1)S(1)} %join.11.refs_0_), channel_id=1, source_target_pairs={{0,1},{1,0},{2,3},{3,2},{4,5},{5,4},{6,7},{7,6},{8,9},{9,8},{10,11... | collective-permute-start | bytes 1671176 | tf_op jit(solution)/shard_map/ppermute | solution.py:247
  24.8 6.1 %collective-permute-start.6 = (bf16[32,2176]{1,0:T(8,128)(2,1)S(1)}, bf16[32,2176]{1,0:T(8,128)(2,1)S(1)}, u32[]{:S(2)}, u32[]{:S(2)}) collective-permute-start(bf16[32,2176]{1,0:T(8,128)(2,1)S(1)} %collective-permute-done.5.refs_3_.refs_0_), channel_id=1, source_target_pairs={{0,2},{1,3},{2,0},{3,1},{4,6},{5,7},{6,4},{7,5},{8,10},{9,11},{10,... | collective-permute-start | bytes 417800 | tf_op jit(solution)/shard_map/ppermute | solution.py:247
  29.2 2.0 %collective-permute-start.10 = (bf16[128,2048]{1,0:T(8,128)(2,1)S(1)}, bf16[128,2048]{1,0:T(8,128)(2,1)S(1)}, u32[]{:S(2)}, u32[]{:S(2)}) collective-permute-start(bf16[128,2048]{1,0:T(8,128)(2,1)S(1)} %get-tuple-element.16), channel_id=1, source_target_pairs={{0,1},{1,0},{2,3},{3,2},{4,5},{5,4},{6,7},{7,6},{8,9},{9,8},{10,11... | collective-permute-start | bytes 1572872 | tf_op jit(solution)/shard_map/ppermute | solution.py:247
  30.9 1.9 %collective-permute-start.9 = (bf16[64,2176]{1,0:T(8,128)(2,1)S(1)}, bf16[64,2176]{1,0:T(8,128)(2,1)S(1)}, u32[]{:S(2)}, u32[]{:S(2)}) collective-permute-start(bf16[64,2176]{1,0:T(8,128)(2,1)S(1)} %join.12.refs_1_.refs_0_), channel_id=1, source_target_pairs={{0,1},{1,0},{2,3},{3,2},{4,5},{5,4},{6,7},{7,6},{8,9},{9,8},{10,11... | collective-permute-start | bytes 835592 | tf_op jit(solution)/shard_map/ppermute | solution.py:247
  31.2 5.8 %collective-permute-start.13 = (bf16[32,2048]{1,0:T(8,128)(2,1)S(1)}, bf16[32,2048]{1,0:T(8,128)(2,1)S(1)}, u32[]{:S(2)}, u32[]{:S(2)}) collective-permute-start(bf16[32,2048]{1,0:T(8,128)(2,1)S(1)} %join.13.refs_3_), channel_id=1, source_target_pairs={{0,2},{1,3},{2,0},{3,1},{4,6},{5,7},{6,4},{7,5},{8,10},{9,11},{10,... | collective-permute-start | bytes 393224 | tf_op jit(solution)/shard_map/ppermute | solution.py:247
  32.8 20.9 %copy-start = (bf16[32,2048]{1,0:T(8,128)(2,1)S(1)}, bf16[32,2048]{1,0:T(8,128)(2,1)}, u32[]{:S(2)}) copy-start(bf16[32,2048]{1,0:T(8,128)(2,1)} %refs_0_.1) | copy-start | bytes 393220
  32.8 6.0 %collective-permute-start.4 = (bf16[64,2048]{1,0:T(8,128)(2,1)S(1)}, bf16[64,2048]{1,0:T(8,128)(2,1)S(1)}, u32[]{:S(2)}, u32[]{:S(2)}) collective-permute-start(bf16[64,2048]{1,0:T(8,128)(2,1)S(1)} %get-tuple-element.13), channel_id=1, source_target_pairs={{0,1},{1,0},{2,3},{3,2},{4,5},{5,4},{6,7},{7,6},{8,9},{9,8},{10,11... | collective-permute-start | bytes 786440 | tf_op jit(solution)/shard_map/ppermute | solution.py:247
  34.2 2.9 %collective-permute-start.11 = (bf16[64,2048]{1,0:T(8,128)(2,1)S(1)}, bf16[64,2048]{1,0:T(8,128)(2,1)S(1)}, u32[]{:S(2)}, u32[]{:S(2)}) collective-permute-start(bf16[64,2048]{1,0:T(8,128)(2,1)S(1)} %get-tuple-element.18), channel_id=1, source_target_pairs={{0,1},{1,0},{2,3},{3,2},{4,5},{5,4},{6,7},{7,6},{8,9},{9,8},{10,11... | collective-permute-start | bytes 786440 | tf_op jit(solution)/shard_map/ppermute | solution.py:247
  37.2 5.4 %collective-permute-start.15 = (bf16[32,2048]{1,0:T(8,128)(2,1)S(1)}, bf16[32,2048]{1,0:T(8,128)(2,1)S(1)}, u32[]{:S(2)}, u32[]{:S(2)}) collective-permute-start(bf16[32,2048]{1,0:T(8,128)(2,1)S(1)} %join.15), channel_id=1, source_target_pairs={{0,2},{1,3},{2,0},{3,1},{4,6},{5,7},{6,4},{7,5},{8,10},{9,11},{10,... | collective-permute-start | bytes 393224 | tf_op jit(solution)/shard_map/ppermute | solution.py:247
  38.8 8.2 %collective-permute-start.14 = (bf16[32,2048]{1,0:T(8,128)(2,1)S(1)}, bf16[32,2048]{1,0:T(8,128)(2,1)S(1)}, u32[]{:S(2)}, u32[]{:S(2)}) collective-permute-start(bf16[32,2048]{1,0:T(8,128)(2,1)S(1)} %get-tuple-element.19), channel_id=1, source_target_pairs={{0,12},{4,8},{8,4},{12,0},{1,13},{5,9},{9,5},{13,1},{2,14},{6,10},... | collective-permute-start | bytes 393224 | tf_op jit(solution)/shard_map/ppermute | solution.py:247
  40.3 6.2 %collective-permute-start.17 = (bf16[32,2048]{1,0:T(8,128)(2,1)S(1)}, bf16[32,2048]{1,0:T(8,128)(2,1)S(1)}, u32[]{:S(2)}, u32[]{:S(2)}) collective-permute-start(bf16[32,2048]{1,0:T(8,128)(2,1)S(1)} %add_convert_fusion.5.refs_1_), channel_id=1, source_target_pairs={{0,2},{1,3},{2,0},{3,1},{4,6},{5,7},{6,4},{7,5},{8,10},{9,11},{10,... | collective-permute-start | bytes 393224 | tf_op jit(solution)/shard_map/ppermute | solution.py:247
  40.8 7.0 %collective-permute-start.12 = (bf16[32,2048]{1,0:T(8,128)(2,1)S(1)}, bf16[32,2048]{1,0:T(8,128)(2,1)S(1)}, u32[]{:S(2)}, u32[]{:S(2)}) collective-permute-start(bf16[32,2048]{1,0:T(8,128)(2,1)S(1)} %join.14), channel_id=1, source_target_pairs={{0,2},{1,3},{2,0},{3,1},{4,6},{5,7},{6,4},{7,5},{8,10},{9,11},{10,... | collective-permute-start | bytes 393224 | tf_op jit(solution)/shard_map/ppermute | solution.py:247
  42.7 6.9 %collective-permute-start.16 = (bf16[32,2048]{1,0:T(8,128)(2,1)S(1)}, bf16[32,2048]{1,0:T(8,128)(2,1)S(1)}, u32[]{:S(2)}, u32[]{:S(2)}) collective-permute-start(bf16[32,2048]{1,0:T(8,128)(2,1)S(1)} %add_convert_fusion.2), channel_id=1, source_target_pairs={{0,4},{4,0},{8,12},{12,8},{1,5},{5,1},{9,13},{13,9},{2,6},{6,2},{1... | collective-permute-start | bytes 393224 | tf_op jit(solution)/shard_map/ppermute | solution.py:247
  46.5 7.2 %collective-permute-start.18 = (bf16[32,2048]{1,0:T(8,128)(2,1)S(1)}, bf16[32,2048]{1,0:T(8,128)(2,1)S(1)}, u32[]{:S(2)}, u32[]{:S(2)}) collective-permute-start(bf16[32,2048]{1,0:T(8,128)(2,1)S(1)} %add_convert_fusion.1), channel_id=1, source_target_pairs={{0,8},{4,12},{8,0},{12,4},{1,9},{5,13},{9,1},{13,5},{2,10},{6,14},... | collective-permute-start | bytes 393224 | tf_op jit(solution)/shard_map/ppermute | solution.py:247

commit v3 on v2

--- a/solution.py
+++ b/solution.py
@@ -12,7 +12,7 @@
 VMEM = pl.BlockSpec(memory_space=pltpu.VMEM)
 SMALL = pltpu.CompilerParams(vmem_limit_bytes=4 * 1024 * 1024)
 CHEAP = pl.CostEstimate(flops=1, bytes_accessed=1, transcendentals=0)
-DEAR = pl.CostEstimate(flops=10**11, bytes_accessed=1, transcendentals=0)
+DEAR = pl.CostEstimate(flops=10**10, bytes_accessed=1, transcendentals=0)
 ANY = pl.BlockSpec(memory_space=pl.ANY)
 
 
@@ -92,6 +92,62 @@
     )(*arrays, *behind)
 
 
+def mark_kernel(*refs):
+    refs[-1][...] = jnp.zeros_like(refs[-1])
+
+
+def mark(behind, cost):
+    return pl.pallas_call(
+        mark_kernel,
+        out_shape=pltpu.VMEM((8, LANES), jnp.float32),
+        in_specs=[ANY] * len(behind),
+        out_specs=VMEM,
+        compiler_params=SMALL,
+        cost_estimate=cost,
+        name="mark",
+    )(*behind)
+
+
+def part_kernel(start, count, *refs):
+    rows = refs[-1].shape[0]
+    total = jnp.zeros(refs[-1].shape, jnp.float32)
+    for ref in refs[:count]:
+        at = start if ref.shape[0] > rows else 0
+        total += ref[at : at + rows, :].astype(jnp.float32)
+    refs[-1][...] = total.astype(refs[-1].dtype)
+
+
+def part_sum(arrays, start, rows, behind=(), cost=CHEAP):
+    return pl.pallas_call(
+        functools.partial(part_kernel, start, len(arrays)),
+        out_shape=pltpu.VMEM((rows, arrays[0].shape[1]), jnp.bfloat16),
+        in_specs=[VMEM] * len(arrays) + [ANY] * len(behind),
+        out_specs=VMEM,
+        compiler_params=SMALL,
+        cost_estimate=cost,
+        name="part",
+    )(*arrays, *behind)
+
+
+def sum_kernel(*refs):
+    total = refs[0][...].astype(jnp.float32)
+    for ref in refs[1:-1]:
+        total += ref[...].astype(jnp.float32)
+    refs[-1][...] = total
+
+
+def sum_arrays(arrays, cost):
+    return pl.pallas_call(
+        sum_kernel,
+        out_shape=pltpu.VMEM(arrays[0].shape, jnp.float32),
+        in_specs=[VMEM] * len(arrays),
+        out_specs=VMEM,
+        compiler_params=SMALL,
+        cost_estimate=cost,
+        name="sum",
+    )(*arrays)
+
+
 def gate_column(experts, expert_ref, tail):
     lane = lax.broadcasted_iota(jnp.int32, tail.shape, 1)
     chosen = (lax.rem(lane, experts) == expert_ref[0]) & (lane < GATE_TERMS * experts)
@@ -99,9 +155,9 @@
 
 
 def load_ffn_kernel(
-    experts, cuts, expert_ref, kept_ref, sent_ref, first_ref, second_ref, *refs
+    experts, cuts, skipped, expert_ref, kept_ref, sent_ref, first_ref, second_ref, *refs
 ):
-    keep_ref, send_ref, weights_ref, rows_ref, hidden_ref, total_ref, sems = refs
+    keep_ref, send_ref, weights_ref, rows_ref, hidden_ref, total_ref, sems = refs[skipped:]
     width, units = first_ref.shape
     copies = []
     for j in range(cuts):
@@ -166,14 +222,14 @@
                 send_ref[:, columns] = out[half:]
 
 
-def load_ffn(kept, sent, w_first, w_second, experts, expert):
+def load_ffn(kept, sent, w_first, w_second, experts, expert, behind):
     width, units = w_first.shape
     half, cuts = kept.shape[0], 4
     out = jax.ShapeDtypeStruct((half, width), jnp.bfloat16)
     return pl.pallas_call(
-        functools.partial(load_ffn_kernel, experts, cuts),
+        functools.partial(load_ffn_kernel, experts, cuts, len(behind)),
         out_shape=(out, out, pltpu.VMEM((2 * width, units), w_first.dtype)),
-        in_specs=[pl.BlockSpec(memory_space=pltpu.SMEM), VMEM, VMEM, ANY, ANY],
+        in_specs=[pl.BlockSpec(memory_space=pltpu.SMEM), VMEM, VMEM] + [ANY] * (2 + len(behind)),
         out_specs=(VMEM, VMEM, VMEM),
         scratch_shapes=[
             pltpu.VMEM((2 * half, width + LANES), jnp.bfloat16),
@@ -182,11 +238,9 @@
             pltpu.SemaphoreType.DMA((1 + width // units, cuts)),
         ],
         compiler_params=pltpu.CompilerParams(vmem_limit_bytes=16 * 1024 * 1024),
-        cost_estimate=pl.CostEstimate(
-            flops=8 * half * width * units, bytes_accessed=4 * width * units, transcendentals=0
-        ),
+        cost_estimate=DEAR,
         name="load_ffn",
-    )(expert, kept, sent, in_hbm(w_first), in_hbm(w_second))
+    )(expert, kept, sent, in_hbm(w_first), in_hbm(w_second), *behind)
 
 
 def ffn_kernel(experts, pieces, skipped, expert_ref, *refs):
@@ -262,44 +316,38 @@
         keep, send = ffn([kept], [sent], weights, experts, expert, behind)
         return keep, swap(send, "dp", core_bit)
 
-    def far_sum(pair, i, count):
-        at = slice((count + i) * rows, (count + i + 1) * rows)
-        return add(*[a[at] for a in pair]).astype(jnp.bfloat16)
-
-    def near_sum(pair, far, i):
-        at = slice(i * rows, (i + 1) * rows)
-        return add(*[a[at] for a in pair], swap(far, "dp", chip_bit))
-
     own = norm_and_pack(tokens, routing, gates, ln_gain, experts)
     across0 = swap(own, "dp", chip_bit)
     lane3, lane1 = swap(own, "expert", 3), swap(own, "expert", 1)
-    lane31 = join([lane3, lane1], [across0])
+    lane31 = join([lane3, lane1])
     across31 = swap(lane31, "dp", chip_bit)
-    lane2 = swap(join([own], [lane31]), "expert", 2)
+    lane2 = swap(own, "expert", 2)
     kept0 = join([own, across0], [lane31])
     keep0, send0, weights = load_ffn(
-        kept0, swap(kept0, "dp", core_bit), w_in[0], w_out[0], experts, expert
+        kept0,
+        swap(kept0, "dp", core_bit),
+        w_in[0],
+        w_out[0],
+        experts,
+        expert,
+        [mark([lane2], DEAR)],
     )
     pair0 = keep0, swap(send0, "dp", core_bit)
-    pair31 = run(join([lane31, across31], [pair0[0], lane2]))
     across2 = swap(lane2, "dp", chip_bit)
-    kept2 = join([lane2, across2], [pair31[0]], DEAR)
-    far3 = join([far_sum(pair31, 0, 2)], [kept2])
-    pair2 = run(kept2, [far3])
-    far2 = far_sum(pair2, 0, 1)
-    far1 = join([far_sum(pair31, 1, 2)], [far2])
-    far0 = join([far_sum(pair0, 0, 1)], [far2])
-    near3 = near_sum(pair31, far3, 0).astype(jnp.bfloat16)
-    near2 = near_sum(pair2, far2, 0).astype(jnp.bfloat16)
-    near1 = near_sum(pair31, far1, 1).astype(jnp.bfloat16)
-    near0 = near_sum(pair0, far0, 0)
-    return add(
-        tokens,
-        near0,
-        swap(near3, "expert", 3),
-        swap(near1, "expert", 1),
-        swap(near2, "expert", 2),
-    ).astype(jnp.bfloat16)
+    kept31 = join([lane31, across31], [keep0])
+    pair31 = run(kept31, [mark([across2, kept31], DEAR)])
+    pair2 = run(join([lane2, across2], [kept31]), [pair31[0]])
+    far3 = part_sum(pair31, 2 * rows, rows, [pair2[0]])
+    far2 = part_sum(pair2, rows, rows)
+    far1 = part_sum(pair31, 3 * rows, rows, [far2])
+    far0 = part_sum(pair0, rows, rows, [far2])
+    near3 = part_sum([*pair31, swap(far3, "dp", chip_bit)], 0, rows)
+    near2 = part_sum([*pair2, swap(far2, "dp", chip_bit)], 0, rows)
+    near1 = part_sum([*pair31, swap(far1, "dp", chip_bit)], rows, rows)
+    near0 = add(*[a[:rows] for a in pair0], swap(far0, "dp", chip_bit))
+    total = sum_arrays([tokens, swap(near3, "expert", 3)], CHEAP)
+    total = sum_arrays([total, swap(near2, "expert", 2)], CHEAP)
+    return add(total, near0, swap(near1, "expert", 1)).astype(jnp.bfloat16)
 
 
 def layer_norm(tokens, ln_gain):

time: 54.6 us -> 51 us (0.934)
  waiting for transfers between devices: 25.8 us -> 22.2 us
    ppermute x19, waiting for transfers between devices: 25.8 us -> 22.2 us  [swap(): return lax.ppermute(array, axis, pairs)]
    pallas_call x1 -> x12, Pallas kernels: 3.8 us -> 4.14 us  [the longest x1 3.8 us: load_ffn(): pl.pallas_call(functools.partial(load_ffn_kernel, experts, cuts, len(behi...]
  transfers between devices with their start and end apart: 19 -> 19, of which waited for: 15 -> 12; matrix products, arithmetic and copies ran while one was open for 1% -> 0% of each run, Pallas kernels for 14% -> 16%
where the time goes in v3:
time: 51 us; the launch traced here: 50.9 us
  waiting for transfers between devices  22.2 us (44%)
  starting transfers between devices  18.6 us (36%)
  Pallas kernels  9.18 us (18%)
  other arithmetic  0.73 us (1%)
    ppermute x19, waiting for transfers between devices, swap(): return lax.ppermute(array, axis, pairs)  22.2 us
    ppermute x19, starting transfers between devices, swap(): return lax.ppermute(array, axis, pairs)  18.6 us
    pallas_call x1, Pallas kernels, load_ffn(): pl.pallas_call(functools.partial(load_ffn_kernel, experts, cuts, len(behi...  3.8 us
    pallas_call x2, Pallas kernels, ffn(): pl.pallas_call(functools.partial(ffn_kernel, experts, count, len(behind))...  3.78 us
    pallas_call x1, Pallas kernels, norm_and_pack(): pl.pallas_call(functools.partial(norm_kernel, experts), out_shape=pltpu.V...  1.17 us
  transfers between devices with their start and end apart: 19, of which 12 were waited for; matrix products, arithmetic and copies ran while one was open for 0% of the time, Pallas kernels for 16%

profile of v3, /device:TPU:0, one launch (start us, length us, event | category | flops | bytes accessed | tf_op | source)
XLA Modules:
  0.0 50.9 jit_solution(12267276016963888445)
XLA Ops:
  0.0 1.2 %norm.1.refs_0_ = bf16[32,2176]{1,0:T(8,128)(2,1)S(1)} custom-call(bf16[32,2048]{1,0:T(8,128)(2,1)} %refs_0_.3, s32[2,32]{1,0:T(2,128)} %bitcast.7, f32[2,32]{1,0:T(2,128)} %bitcast.8, f32[1,2048]{1,0:T(1,128)} %bitcast.6), custom_call_target="tpu_custom_call" | custom-call | flops 1 | bytes 1 | tf_op jit(solution)/shard_map/norm/pallas_call | solution.py:62
  1.2 5.1 %collective-permute-start = (bf16[32,2176]{1,0:T(8,128)(2,1)S(1)}, bf16[32,2176]{1,0:T(8,128)(2,1)S(1)}, u32[]{:S(2)}, u32[]{:S(2)}) collective-permute-start(bf16[32,2176]{1,0:T(8,128)(2,1)S(1)} %norm.1.refs_0_), channel_id=1, source_target_pairs={{0,12},{4,8},{8,4},{12,0},{1,13},{5,9},{9,5},{13,1},{2,14},{6,10},... | collective-permute-start | bytes 417800 | tf_op jit(solution)/shard_map/ppermute | solution.py:301
  6.3 1.5 %collective-permute-start.3 = (bf16[32,2176]{1,0:T(8,128)(2,1)S(1)}, bf16[32,2176]{1,0:T(8,128)(2,1)S(1)}, u32[]{:S(2)}, u32[]{:S(2)}) collective-permute-start(bf16[32,2176]{1,0:T(8,128)(2,1)S(1)} %norm.1.refs_0_), channel_id=1, source_target_pairs={{0,2},{1,3},{2,0},{3,1},{4,6},{5,7},{6,4},{7,5},{8,10},{9,11},{10,... | collective-permute-start | bytes 417800 | tf_op jit(solution)/shard_map/ppermute | solution.py:301
  7.8 0.8 %collective-permute-start.5 = (bf16[32,2176]{1,0:T(8,128)(2,1)S(1)}, bf16[32,2176]{1,0:T(8,128)(2,1)S(1)}, u32[]{:S(2)}, u32[]{:S(2)}) collective-permute-start(bf16[32,2176]{1,0:T(8,128)(2,1)S(1)} %norm.1.refs_0_), channel_id=1, source_target_pairs={{0,8},{4,12},{8,0},{12,4},{1,9},{5,13},{9,1},{13,5},{2,10},{6,14},... | collective-permute-start | bytes 417800 | tf_op jit(solution)/shard_map/ppermute | solution.py:301
  8.6 2.3 %collective-permute-done.refs_0_ = bf16[32,2176]{1,0:T(8,128)(2,1)S(1)} collective-permute-done((bf16[32,2176]{1,0:T(8,128)(2,1)S(1)}, bf16[32,2176]{1,0:T(8,128)(2,1)S(1)}, u32[]{:S(2)}, u32[]{:S(2)}) %collective-permute-start) | collective-permute-done | bytes 139296 | tf_op jit(solution)/shard_map/ppermute | solution.py:301
  10.8 3.2 %collective-permute-done.1.refs_1_ = bf16[32,2176]{1,0:T(8,128)(2,1)S(1)} collective-permute-done((bf16[32,2176]{1,0:T(8,128)(2,1)S(1)}, bf16[32,2176]{1,0:T(8,128)(2,1)S(1)}, u32[]{:S(2)}, u32[]{:S(2)}) %collective-permute-start.1) | collective-permute-done | bytes 139296 | tf_op jit(solution)/shard_map/ppermute | solution.py:301
  14.1 1.5 %collective-permute-start.2 = (bf16[64,2176]{1,0:T(8,128)(2,1)S(1)}, bf16[64,2176]{1,0:T(8,128)(2,1)S(1)}, u32[]{:S(2)}, u32[]{:S(2)}) collective-permute-start(bf16[64,2176]{1,0:T(8,128)(2,1)S(1)} %join.4.refs_2_.refs_0_), channel_id=1, source_target_pairs={{0,2},{1,3},{2,0},{3,1},{4,6},{5,7},{6,4},{7,5},{8,10},{9,11},{10,... | collective-permute-start | bytes 835592 | tf_op jit(solution)/shard_map/ppermute | solution.py:301
  15.6 2.4 %collective-permute-done.5.refs_0_ = bf16[32,2176]{1,0:T(8,128)(2,1)S(1)} collective-permute-done((bf16[32,2176]{1,0:T(8,128)(2,1)S(1)}, bf16[32,2176]{1,0:T(8,128)(2,1)S(1)}, u32[]{:S(2)}, u32[]{:S(2)}) %collective-permute-start.5) | collective-permute-done | bytes 139296 | tf_op jit(solution)/shard_map/ppermute | solution.py:301
  18.1 1.5 %collective-permute-start.7 = (bf16[32,2176]{1,0:T(8,128)(2,1)S(1)}, bf16[32,2176]{1,0:T(8,128)(2,1)S(1)}, u32[]{:S(2)}, u32[]{:S(2)}) collective-permute-start(bf16[32,2176]{1,0:T(8,128)(2,1)S(1)} %collective-permute-done.5.refs_0_), channel_id=1, source_target_pairs={{0,2},{1,3},{2,0},{3,1},{4,6},{5,7},{6,4},{7,5},{8,10},{9,11},{10,... | collective-permute-start | bytes 417800 | tf_op jit(solution)/shard_map/ppermute | solution.py:301
  19.6 3.8 %load_ffn.1 = (bf16[64,2048]{1,0:T(8,128)(2,1)S(1)}, bf16[64,2048]{1,0:T(8,128)(2,1)S(1)}, bf16[4096,1024]{1,0:T(8,128)(2,1)S(1)}) custom-call(s32[1]{0:T(128)} %bitcast.expert_ref, bf16[64,2176]{1,0:T(8,128)(2,1)S(1)} %join.5.kept_ref, bf16[64,2176]{1,0:T(8,128)(2,1)S(1)} %collective-permute-done.4.sent_ref, bf16[2048,1024]{1,0:T(8,128)(2,1)} %bitcast.9, ...), custom_call_target="tpu_custom_call" | custom-call | flops 10000000000 | bytes 1 | tf_op jit(solution)/shard_map/load_ffn/pallas_call | solution.py:229
  23.8 1.6 %collective-permute-done.7.refs_0_.refs_1_ = bf16[32,2176]{1,0:T(8,128)(2,1)S(1)} collective-permute-done((bf16[32,2176]{1,0:T(8,128)(2,1)S(1)}, bf16[32,2176]{1,0:T(8,128)(2,1)S(1)}, u32[]{:S(2)}, u32[]{:S(2)}) %collective-permute-start.7) | collective-permute-done | bytes 139296 | tf_op jit(solution)/shard_map/ppermute | solution.py:301
  25.8 2.4 %ffn.2 = (bf16[128,2048]{1,0:T(8,128)(2,1)S(1)}, bf16[128,2048]{1,0:T(8,128)(2,1)S(1)}) custom-call(s32[1]{0:T(128)} %bitcast.expert_ref, bf16[128,2176]{1,0:T(8,128)(2,1)S(1)} %join.6.refs_1_.refs_0_.refs_2_, bf16[128,2176]{1,0:T(8,128)(2,1)S(1)} %collective-permute-done.6.refs_1_, bf16[4096,1024]{1,0:T(8,128)(2,1)S(1)} %get-tuple-element.13.refs_2_, ...), custom_call_target="tpu_custom_call" | custom-call | flops 2147483648 | bytes 8388608 | tf_op jit(solution)/shard_map/ffn/pallas_call | solution.py:280
  28.5 1.4 %ffn.3 = (bf16[64,2048]{1,0:T(8,128)(2,1)S(1)}, bf16[64,2048]{1,0:T(8,128)(2,1)S(1)}) custom-call(s32[1]{0:T(128)} %bitcast.expert_ref, bf16[64,2176]{1,0:T(8,128)(2,1)S(1)} %join.7.refs_0_, bf16[64,2176]{1,0:T(8,128)(2,1)S(1)} %collective-permute-done.9.refs_1_, bf16[4096,1024]{1,0:T(8,128)(2,1)S(1)} %get-tuple-element.13.refs_2_, ...), custom_call_target="tpu_custom_call" | custom-call | flops 1073741824 | bytes 8388608 | tf_op jit(solution)/shard_map/ffn/pallas_call | solution.py:280
  30.5 1.4 %collective-permute-start.10 = (bf16[32,2048]{1,0:T(8,128)(2,1)S(1)}, bf16[32,2048]{1,0:T(8,128)(2,1)S(1)}, u32[]{:S(2)}, u32[]{:S(2)}) collective-permute-start(bf16[32,2048]{1,0:T(8,128)(2,1)S(1)} %part.7), channel_id=1, source_target_pairs={{0,2},{1,3},{2,0},{3,1},{4,6},{5,7},{6,4},{7,5},{8,10},{9,11},{10,... | collective-permute-start | bytes 393224 | tf_op jit(solution)/shard_map/ppermute | solution.py:301
  31.9 1.0 %collective-permute-start.13 = (bf16[32,2048]{1,0:T(8,128)(2,1)S(1)}, bf16[32,2048]{1,0:T(8,128)(2,1)S(1)}, u32[]{:S(2)}, u32[]{:S(2)}) collective-permute-start(bf16[32,2048]{1,0:T(8,128)(2,1)S(1)} %part.9.refs_2_), channel_id=1, source_target_pairs={{0,2},{1,3},{2,0},{3,1},{4,6},{5,7},{6,4},{7,5},{8,10},{9,11},{10,... | collective-permute-start | bytes 393224 | tf_op jit(solution)/shard_map/ppermute | solution.py:301
  32.9 1.2 %collective-permute-start.17 = (bf16[32,2048]{1,0:T(8,128)(2,1)S(1)}, bf16[32,2048]{1,0:T(8,128)(2,1)S(1)}, u32[]{:S(2)}, u32[]{:S(2)}) collective-permute-start(bf16[32,2048]{1,0:T(8,128)(2,1)S(1)} %part.12), channel_id=1, source_target_pairs={{0,2},{1,3},{2,0},{3,1},{4,6},{5,7},{6,4},{7,5},{8,10},{9,11},{10,... | collective-permute-start | bytes 393224 | tf_op jit(solution)/shard_map/ppermute | solution.py:301
  34.2 1.0 %collective-permute-start.16 = (bf16[32,2048]{1,0:T(8,128)(2,1)S(1)}, bf16[32,2048]{1,0:T(8,128)(2,1)S(1)}, u32[]{:S(2)}, u32[]{:S(2)}) collective-permute-start(bf16[32,2048]{1,0:T(8,128)(2,1)S(1)} %part.11), channel_id=1, source_target_pairs={{0,2},{1,3},{2,0},{3,1},{4,6},{5,7},{6,4},{7,5},{8,10},{9,11},{10,... | collective-permute-start | bytes 393224 | tf_op jit(solution)/shard_map/ppermute | solution.py:301
  35.1 1.7 %collective-permute-done.10.refs_2_ = bf16[32,2048]{1,0:T(8,128)(2,1)S(1)} collective-permute-done((bf16[32,2048]{1,0:T(8,128)(2,1)S(1)}, bf16[32,2048]{1,0:T(8,128)(2,1)S(1)}, u32[]{:S(2)}, u32[]{:S(2)}) %collective-permute-start.10) | collective-permute-done | bytes 131104 | tf_op jit(solution)/shard_map/ppermute | solution.py:301
  36.9 2.1 %collective-permute-start.11 = (bf16[32,2048]{1,0:T(8,128)(2,1)S(1)}, bf16[32,2048]{1,0:T(8,128)(2,1)S(1)}, u32[]{:S(2)}, u32[]{:S(2)}) collective-permute-start(bf16[32,2048]{1,0:T(8,128)(2,1)S(1)} %part.8), channel_id=1, source_target_pairs={{0,12},{4,8},{8,4},{12,0},{1,13},{5,9},{9,5},{13,1},{2,14},{6,10},... | collective-permute-start | bytes 393224 | tf_op jit(solution)/shard_map/ppermute | solution.py:301
  39.1 0.6 %collective-permute-done.13.refs_2_ = bf16[32,2048]{1,0:T(8,128)(2,1)S(1)} collective-permute-done((bf16[32,2048]{1,0:T(8,128)(2,1)S(1)}, bf16[32,2048]{1,0:T(8,128)(2,1)S(1)}, u32[]{:S(2)}, u32[]{:S(2)}) %collective-permute-start.13) | collective-permute-done | bytes 131104 | tf_op jit(solution)/shard_map/ppermute | solution.py:301
  40.1 2.4 %collective-permute-done.17.refs_2_ = bf16[32,2048]{1,0:T(8,128)(2,1)S(1)} collective-permute-done((bf16[32,2048]{1,0:T(8,128)(2,1)S(1)}, bf16[32,2048]{1,0:T(8,128)(2,1)S(1)}, u32[]{:S(2)}, u32[]{:S(2)}) %collective-permute-start.17) | collective-permute-done | bytes 131104 | tf_op jit(solution)/shard_map/ppermute | solution.py:301
  42.8 2.1 %collective-permute-done.11.refs_1_ = bf16[32,2048]{1,0:T(8,128)(2,1)S(1)} collective-permute-done((bf16[32,2048]{1,0:T(8,128)(2,1)S(1)}, bf16[32,2048]{1,0:T(8,128)(2,1)S(1)}, u32[]{:S(2)}, u32[]{:S(2)}) %collective-permute-start.11) | collective-permute-done | bytes 131104 | tf_op jit(solution)/shard_map/ppermute | solution.py:301
  44.9 5.1 %collective-permute-done.14.refs_1_ = bf16[32,2048]{1,0:T(8,128)(2,1)S(1)} collective-permute-done((bf16[32,2048]{1,0:T(8,128)(2,1)S(1)}, bf16[32,2048]{1,0:T(8,128)(2,1)S(1)}, u32[]{:S(2)}, u32[]{:S(2)}) %collective-permute-start.14) | collective-permute-done | bytes 131104 | tf_op jit(solution)/shard_map/ppermute | solution.py:301
  50.2 0.7 %add_convert_fusion = bf16[32,2048]{1,0:T(8,128)(2,1)} fusion(bf16[32,2048]{1,0:T(8,128)(2,1)S(1)} %collective-permute-done.18, f32[32,2048]{1,0:T(8,128)S(1)} %sum.3, bf16[32,2048]{1,0:T(8,128)(2,1)S(1)} %collective-permute-done.16, bf16[64,2048]{1,0:T(8,128)(2,1)S(1)} %collective-permute-done.15.refs_1_, bf16[64,2048]{1,0:T(8,128)(2,1)S(1)} %get-tuple-element.12.refs_2_.refs_0_), kind=kLoop, calls=%fused_computation | loop fusion | flops 589824 | bytes 917504 | tf_op jit(solution)/shard_map/convert_element_type | solution.py:350
  (36 shorter events, 2.7 us)
Async XLA Ops:
  1.2 9.7 %collective-permute-start = (bf16[32,2176]{1,0:T(8,128)(2,1)S(1)}, bf16[32,2176]{1,0:T(8,128)(2,1)S(1)}, u32[]{:S(2)}, u32[]{:S(2)}) collective-permute-start(bf16[32,2176]{1,0:T(8,128)(2,1)S(1)} %norm.1.refs_0_), channel_id=1, source_target_pairs={{0,12},{4,8},{8,4},{12,0},{1,13},{5,9},{9,5},{13,1},{2,14},{6,10},... | collective-permute-start | bytes 417800 | tf_op jit(solution)/shard_map/ppermute | solution.py:301
  6.3 7.7 %collective-permute-start.1 = (bf16[32,2176]{1,0:T(8,128)(2,1)S(1)}, bf16[32,2176]{1,0:T(8,128)(2,1)S(1)}, u32[]{:S(2)}, u32[]{:S(2)}) collective-permute-start(bf16[32,2176]{1,0:T(8,128)(2,1)S(1)} %norm.1.refs_0_), channel_id=1, source_target_pairs={{0,4},{4,0},{8,12},{12,8},{1,5},{5,1},{9,13},{13,9},{2,6},{6,2},{1... | collective-permute-start | bytes 417800 | tf_op jit(solution)/shard_map/ppermute | solution.py:301
  6.3 9.2 %collective-permute-start.3 = (bf16[32,2176]{1,0:T(8,128)(2,1)S(1)}, bf16[32,2176]{1,0:T(8,128)(2,1)S(1)}, u32[]{:S(2)}, u32[]{:S(2)}) collective-permute-start(bf16[32,2176]{1,0:T(8,128)(2,1)S(1)} %norm.1.refs_0_), channel_id=1, source_target_pairs={{0,2},{1,3},{2,0},{3,1},{4,6},{5,7},{6,4},{7,5},{8,10},{9,11},{10,... | collective-permute-start | bytes 417800 | tf_op jit(solution)/shard_map/ppermute | solution.py:301
  7.8 10.3 %collective-permute-start.5 = (bf16[32,2176]{1,0:T(8,128)(2,1)S(1)}, bf16[32,2176]{1,0:T(8,128)(2,1)S(1)}, u32[]{:S(2)}, u32[]{:S(2)}) collective-permute-start(bf16[32,2176]{1,0:T(8,128)(2,1)S(1)} %norm.1.refs_0_), channel_id=1, source_target_pairs={{0,8},{4,12},{8,0},{12,4},{1,9},{5,13},{9,1},{13,5},{2,10},{6,14},... | collective-permute-start | bytes 417800 | tf_op jit(solution)/shard_map/ppermute | solution.py:301
  14.1 9.6 %collective-permute-start.2 = (bf16[64,2176]{1,0:T(8,128)(2,1)S(1)}, bf16[64,2176]{1,0:T(8,128)(2,1)S(1)}, u32[]{:S(2)}, u32[]{:S(2)}) collective-permute-start(bf16[64,2176]{1,0:T(8,128)(2,1)S(1)} %join.4.refs_2_.refs_0_), channel_id=1, source_target_pairs={{0,2},{1,3},{2,0},{3,1},{4,6},{5,7},{6,4},{7,5},{8,10},{9,11},{10,... | collective-permute-start | bytes 835592 | tf_op jit(solution)/shard_map/ppermute | solution.py:301
  15.6 4.0 %collective-permute-start.4 = (bf16[64,2176]{1,0:T(8,128)(2,1)S(1)}, bf16[64,2176]{1,0:T(8,128)(2,1)S(1)}, u32[]{:S(2)}, u32[]{:S(2)}) collective-permute-start(bf16[64,2176]{1,0:T(8,128)(2,1)S(1)} %join.5.kept_ref), channel_id=1, source_target_pairs={{0,1},{1,0},{2,3},{3,2},{4,5},{5,4},{6,7},{7,6},{8,9},{9,8},{10,11... | collective-permute-start | bytes 835592 | tf_op jit(solution)/shard_map/ppermute | solution.py:301
  18.1 7.3 %collective-permute-start.7 = (bf16[32,2176]{1,0:T(8,128)(2,1)S(1)}, bf16[32,2176]{1,0:T(8,128)(2,1)S(1)}, u32[]{:S(2)}, u32[]{:S(2)}) collective-permute-start(bf16[32,2176]{1,0:T(8,128)(2,1)S(1)} %collective-permute-done.5.refs_0_), channel_id=1, source_target_pairs={{0,2},{1,3},{2,0},{3,1},{4,6},{5,7},{6,4},{7,5},{8,10},{9,11},{10,... | collective-permute-start | bytes 417800 | tf_op jit(solution)/shard_map/ppermute | solution.py:301
  23.7 2.0 %collective-permute-start.6 = (bf16[128,2176]{1,0:T(8,128)(2,1)S(1)}, bf16[128,2176]{1,0:T(8,128)(2,1)S(1)}, u32[]{:S(2)}, u32[]{:S(2)}) collective-permute-start(bf16[128,2176]{1,0:T(8,128)(2,1)S(1)} %join.6.refs_1_.refs_0_.refs_2_), channel_id=1, source_target_pairs={{0,1},{1,0},{2,3},{3,2},{4,5},{5,4},{6,7},{7,6},{8,9},{9,8},{10,11... | collective-permute-start | bytes 1671176 | tf_op jit(solution)/shard_map/ppermute | solution.py:301
  25.4 3.1 %collective-permute-start.9 = (bf16[64,2176]{1,0:T(8,128)(2,1)S(1)}, bf16[64,2176]{1,0:T(8,128)(2,1)S(1)}, u32[]{:S(2)}, u32[]{:S(2)}) collective-permute-start(bf16[64,2176]{1,0:T(8,128)(2,1)S(1)} %join.7.refs_0_), channel_id=1, source_target_pairs={{0,1},{1,0},{2,3},{3,2},{4,5},{5,4},{6,7},{7,6},{8,9},{9,8},{10,11... | collective-permute-start | bytes 835592 | tf_op jit(solution)/shard_map/ppermute | solution.py:301
  28.2 2.3 %collective-permute-start.8 = (bf16[128,2048]{1,0:T(8,128)(2,1)S(1)}, bf16[128,2048]{1,0:T(8,128)(2,1)S(1)}, u32[]{:S(2)}, u32[]{:S(2)}) collective-permute-start(bf16[128,2048]{1,0:T(8,128)(2,1)S(1)} %get-tuple-element.15), channel_id=1, source_target_pairs={{0,1},{1,0},{2,3},{3,2},{4,5},{5,4},{6,7},{7,6},{8,9},{9,8},{10,11... | collective-permute-start | bytes 1572872 | tf_op jit(solution)/shard_map/ppermute | solution.py:301
  29.9 15.0 %copy-start = (bf16[32,2048]{1,0:T(8,128)(2,1)S(1)}, bf16[32,2048]{1,0:T(8,128)(2,1)}, u32[]{:S(2)}) copy-start(bf16[32,2048]{1,0:T(8,128)(2,1)} %refs_0_.3) | copy-start | bytes 393220
  29.9 2.0 %collective-permute-start.12 = (bf16[64,2048]{1,0:T(8,128)(2,1)S(1)}, bf16[64,2048]{1,0:T(8,128)(2,1)S(1)}, u32[]{:S(2)}, u32[]{:S(2)}) collective-permute-start(bf16[64,2048]{1,0:T(8,128)(2,1)S(1)} %get-tuple-element.17), channel_id=1, source_target_pairs={{0,1},{1,0},{2,3},{3,2},{4,5},{5,4},{6,7},{7,6},{8,9},{9,8},{10,11... | collective-permute-start | bytes 786440 | tf_op jit(solution)/shard_map/ppermute | solution.py:301
  30.2 3.9 %collective-permute-start.15 = (bf16[64,2048]{1,0:T(8,128)(2,1)S(1)}, bf16[64,2048]{1,0:T(8,128)(2,1)S(1)}, u32[]{:S(2)}, u32[]{:S(2)}) collective-permute-start(bf16[64,2048]{1,0:T(8,128)(2,1)S(1)} %get-tuple-element.18), channel_id=1, source_target_pairs={{0,1},{1,0},{2,3},{3,2},{4,5},{5,4},{6,7},{7,6},{8,9},{9,8},{10,11... | collective-permute-start | bytes 786440 | tf_op jit(solution)/shard_map/ppermute | solution.py:301
  30.5 6.4 %collective-permute-start.10 = (bf16[32,2048]{1,0:T(8,128)(2,1)S(1)}, bf16[32,2048]{1,0:T(8,128)(2,1)S(1)}, u32[]{:S(2)}, u32[]{:S(2)}) collective-permute-start(bf16[32,2048]{1,0:T(8,128)(2,1)S(1)} %part.7), channel_id=1, source_target_pairs={{0,2},{1,3},{2,0},{3,1},{4,6},{5,7},{6,4},{7,5},{8,10},{9,11},{10,... | collective-permute-start | bytes 393224 | tf_op jit(solution)/shard_map/ppermute | solution.py:301
  31.9 7.8 %collective-permute-start.13 = (bf16[32,2048]{1,0:T(8,128)(2,1)S(1)}, bf16[32,2048]{1,0:T(8,128)(2,1)S(1)}, u32[]{:S(2)}, u32[]{:S(2)}) collective-permute-start(bf16[32,2048]{1,0:T(8,128)(2,1)S(1)} %part.9.refs_2_), channel_id=1, source_target_pairs={{0,2},{1,3},{2,0},{3,1},{4,6},{5,7},{6,4},{7,5},{8,10},{9,11},{10,... | collective-permute-start | bytes 393224 | tf_op jit(solution)/shard_map/ppermute | solution.py:301
  32.9 9.6 %collective-permute-start.17 = (bf16[32,2048]{1,0:T(8,128)(2,1)S(1)}, bf16[32,2048]{1,0:T(8,128)(2,1)S(1)}, u32[]{:S(2)}, u32[]{:S(2)}) collective-permute-start(bf16[32,2048]{1,0:T(8,128)(2,1)S(1)} %part.12), channel_id=1, source_target_pairs={{0,2},{1,3},{2,0},{3,1},{4,6},{5,7},{6,4},{7,5},{8,10},{9,11},{10,... | collective-permute-start | bytes 393224 | tf_op jit(solution)/shard_map/ppermute | solution.py:301
  34.2 15.9 %collective-permute-start.16 = (bf16[32,2048]{1,0:T(8,128)(2,1)S(1)}, bf16[32,2048]{1,0:T(8,128)(2,1)S(1)}, u32[]{:S(2)}, u32[]{:S(2)}) collective-permute-start(bf16[32,2048]{1,0:T(8,128)(2,1)S(1)} %part.11), channel_id=1, source_target_pairs={{0,2},{1,3},{2,0},{3,1},{4,6},{5,7},{6,4},{7,5},{8,10},{9,11},{10,... | collective-permute-start | bytes 393224 | tf_op jit(solution)/shard_map/ppermute | solution.py:301
  36.9 7.9 %collective-permute-start.11 = (bf16[32,2048]{1,0:T(8,128)(2,1)S(1)}, bf16[32,2048]{1,0:T(8,128)(2,1)S(1)}, u32[]{:S(2)}, u32[]{:S(2)}) collective-permute-start(bf16[32,2048]{1,0:T(8,128)(2,1)S(1)} %part.8), channel_id=1, source_target_pairs={{0,12},{4,8},{8,4},{12,0},{1,13},{5,9},{9,5},{13,1},{2,14},{6,10},... | collective-permute-start | bytes 393224 | tf_op jit(solution)/shard_map/ppermute | solution.py:301
  39.7 10.3 %collective-permute-start.14 = (bf16[32,2048]{1,0:T(8,128)(2,1)S(1)}, bf16[32,2048]{1,0:T(8,128)(2,1)S(1)}, u32[]{:S(2)}, u32[]{:S(2)}) collective-permute-start(bf16[32,2048]{1,0:T(8,128)(2,1)S(1)} %part.10), channel_id=1, source_target_pairs={{0,8},{4,12},{8,0},{12,4},{1,9},{5,13},{9,1},{13,5},{2,10},{6,14},... | collective-permute-start | bytes 393224 | tf_op jit(solution)/shard_map/ppermute | solution.py:301
  42.6 7.6 %collective-permute-start.18 = (bf16[32,2048]{1,0:T(8,128)(2,1)S(1)}, bf16[32,2048]{1,0:T(8,128)(2,1)S(1)}, u32[]{:S(2)}, u32[]{:S(2)}) collective-permute-start(bf16[32,2048]{1,0:T(8,128)(2,1)S(1)} %part.13), channel_id=1, source_target_pairs={{0,4},{4,0},{8,12},{12,8},{1,5},{5,1},{9,13},{13,9},{2,6},{6,2},{1... | collective-permute-start | bytes 393224 | tf_op jit(solution)/shard_map/ppermute | solution.py:301

commit v4 on v3

--- a/solution.py
+++ b/solution.py
@@ -13,6 +13,7 @@
 SMALL = pltpu.CompilerParams(vmem_limit_bytes=4 * 1024 * 1024)
 CHEAP = pl.CostEstimate(flops=1, bytes_accessed=1, transcendentals=0)
 DEAR = pl.CostEstimate(flops=10**10, bytes_accessed=1, transcendentals=0)
+SOME = pl.CostEstimate(flops=2*10**9, bytes_accessed=1, transcendentals=0)
 ANY = pl.BlockSpec(memory_space=pl.ANY)
 
 
@@ -74,15 +75,16 @@
 
 def join_kernel(pieces, *refs):
     at = 0
-    for ref in refs[:pieces]:
-        refs[-1][at : at + ref.shape[0], :] = ref[...]
-        at += ref.shape[0]
-
-
-def join(arrays, behind=(), cost=CHEAP):
-    rows, width = sum(a.shape[0] for a in arrays), arrays[0].shape[1]
-    return pl.pallas_call(
-        functools.partial(join_kernel, len(arrays)),
+    for ref, (start, size) in zip(refs, pieces):
+        refs[-1][at : at + size, :] = ref[start : start + size, :]
+        at += size
+
+
+def join(arrays, behind=(), pieces=None, cost=CHEAP):
+    pieces = pieces or [(0, a.shape[0]) for a in arrays]
+    rows, width = sum(size for _, size in pieces), arrays[0].shape[1]
+    return pl.pallas_call(
+        functools.partial(join_kernel, pieces),
         out_shape=pltpu.VMEM((rows, width), arrays[0].dtype),
         in_specs=[VMEM] * len(arrays) + [ANY] * len(behind),
         out_specs=VMEM,
@@ -155,9 +157,9 @@
 
 
 def load_ffn_kernel(
-    experts, cuts, skipped, expert_ref, kept_ref, sent_ref, first_ref, second_ref, *refs
+    experts, cuts, skipped, expert_ref, kept_ref, first_ref, second_ref, *refs
 ):
-    keep_ref, send_ref, weights_ref, rows_ref, hidden_ref, total_ref, sems = refs[skipped:]
+    keep_ref, weights_ref, rows_ref, hidden_ref, total_ref, sems = refs[skipped:]
     width, units = first_ref.shape
     copies = []
     for j in range(cuts):
@@ -182,9 +184,7 @@
     for group in copies:
         for copy in group:
             copy.start()
-    half = kept_ref.shape[0]
-    rows_ref[:half, :] = kept_ref[...]
-    rows_ref[half:, :] = sent_ref[...]
+    rows_ref[...] = kept_ref[...]
     gate = gate_column(experts, expert_ref, rows_ref[:, width:])
     for j in range(cuts):
         for copy in copies[j]:
@@ -218,41 +218,41 @@
                 total_ref[:, columns] = dot
             else:
                 out = (dot * gate).astype(jnp.bfloat16)
-                keep_ref[:, columns] = out[:half]
-                send_ref[:, columns] = out[half:]
-
-
-def load_ffn(kept, sent, w_first, w_second, experts, expert, behind):
+                keep_ref[:, columns] = out
+
+
+def load_ffn(kept, w_first, w_second, experts, expert, behind):
     width, units = w_first.shape
-    half, cuts = kept.shape[0], 4
-    out = jax.ShapeDtypeStruct((half, width), jnp.bfloat16)
+    rows, cuts = kept.shape[0], 4
+    out = jax.ShapeDtypeStruct((rows, width), jnp.bfloat16)
     return pl.pallas_call(
         functools.partial(load_ffn_kernel, experts, cuts, len(behind)),
-        out_shape=(out, out, pltpu.VMEM((2 * width, units), w_first.dtype)),
-        in_specs=[pl.BlockSpec(memory_space=pltpu.SMEM), VMEM, VMEM] + [ANY] * (2 + len(behind)),
-        out_specs=(VMEM, VMEM, VMEM),
+        out_shape=(out, pltpu.VMEM((2 * width, units), w_first.dtype)),
+        in_specs=[pl.BlockSpec(memory_space=pltpu.SMEM), VMEM] + [ANY] * (2 + len(behind)),
+        out_specs=(VMEM, VMEM),
         scratch_shapes=[
-            pltpu.VMEM((2 * half, width + LANES), jnp.bfloat16),
-            pltpu.VMEM((2 * half, units), jnp.bfloat16),
-            pltpu.VMEM((2 * half, width), jnp.float32),
+            pltpu.VMEM((rows, width + LANES), jnp.bfloat16),
+            pltpu.VMEM((rows, units), jnp.bfloat16),
+            pltpu.VMEM((rows, width), jnp.float32),
             pltpu.SemaphoreType.DMA((1 + width // units, cuts)),
         ],
         compiler_params=pltpu.CompilerParams(vmem_limit_bytes=16 * 1024 * 1024),
-        cost_estimate=DEAR,
+        cost_estimate=CHEAP,
         name="load_ffn",
-    )(expert, kept, sent, in_hbm(w_first), in_hbm(w_second), *behind)
-
-
-def ffn_kernel(experts, pieces, skipped, expert_ref, *refs):
-    kept, sent = refs[:pieces], refs[pieces : 2 * pieces]
-    weights = refs[2 * pieces]
-    keep_ref, send_ref, rows_ref, hidden_ref = refs[2 * pieces + 1 + skipped :]
+    )(expert, kept, in_hbm(w_first), in_hbm(w_second), *behind)
+
+
+def ffn_kernel(experts, kept_count, sent_count, skipped, expert_ref, *refs):
+    pieces = kept_count + sent_count
+    kept, sent = refs[:kept_count], refs[kept_count:pieces]
+    weights = refs[pieces]
+    keep_ref, send_ref, rows_ref, hidden_ref = refs[pieces + 1 + skipped :]
     width, units = keep_ref.shape[1], weights.shape[1]
     at = 0
     for ref in kept + sent:
         rows_ref[at : at + ref.shape[0], :] = ref[...]
         at += ref.shape[0]
-    half = at // 2
+    half = keep_ref.shape[0]
     gate = gate_column(experts, expert_ref, rows_ref[:, width:])
     step = 256
     for j in range(0, units, step):
@@ -272,25 +272,28 @@
         keep_ref[:, j : j + step] = out[:half]
 
 
-def ffn(kept, sent, weights, experts, expert, behind):
+def ffn(kept, sent, weights, experts, expert, behind, cost):
     width, units = weights.shape[0] // 2, weights.shape[1]
     half = sum(a.shape[0] for a in kept)
-    out = jax.ShapeDtypeStruct((half, width), jnp.bfloat16)
-    count = len(kept)
-    return pl.pallas_call(
-        functools.partial(ffn_kernel, experts, count, len(behind)),
-        out_shape=(out, out),
+    rest = sum(a.shape[0] for a in sent)
+    count = len(kept) + len(sent)
+    return pl.pallas_call(
+        functools.partial(ffn_kernel, experts, len(kept), len(sent), len(behind)),
+        out_shape=(
+            jax.ShapeDtypeStruct((half, width), jnp.bfloat16),
+            jax.ShapeDtypeStruct((rest, width), jnp.bfloat16),
+        ),
         in_specs=[pl.BlockSpec(memory_space=pltpu.SMEM)]
-        + [VMEM] * (2 * count + 1)
+        + [VMEM] * (count + 1)
         + [ANY] * len(behind),
         out_specs=(VMEM, VMEM),
         scratch_shapes=[
-            pltpu.VMEM((2 * half, width + LANES), jnp.bfloat16),
-            pltpu.VMEM((2 * half, units), jnp.bfloat16),
+            pltpu.VMEM((half + rest, width + LANES), jnp.bfloat16),
+            pltpu.VMEM((half + rest, units), jnp.bfloat16),
         ],
         compiler_params=pltpu.CompilerParams(vmem_limit_bytes=16 * 1024 * 1024),
         cost_estimate=pl.CostEstimate(
-            flops=8 * half * width * units, bytes_accessed=4 * width * units, transcendentals=0
+            flops=4 * (half + rest) * width * units, bytes_accessed=4 * width * units, transcendentals=0
         ),
         name="ffn",
     )(expert, *kept, *sent, in_vmem(weights), *behind)
@@ -311,43 +314,44 @@
     core_bit, chip_bit = 1, 2
     expert = lax.axis_index("expert").reshape(1)
 
-    def run(kept, behind=()):
-        sent = swap(kept, "dp", core_bit)
-        keep, send = ffn([kept], [sent], weights, experts, expert, behind)
+    def run(kept, sent, behind=(), cost=CHEAP):
+        keep, send = ffn(kept, sent, weights, experts, expert, behind, cost)
         return keep, swap(send, "dp", core_bit)
 
+    def core_swap(array):
+        return swap(array, "dp", core_bit)
+
     own = norm_and_pack(tokens, routing, gates, ln_gain, experts)
+    lane3, lane1 = swap(own, "expert", 3), swap(own, "expert", 1)
     across0 = swap(own, "dp", chip_bit)
-    lane3, lane1 = swap(own, "expert", 3), swap(own, "expert", 1)
-    lane31 = join([lane3, lane1])
-    across31 = swap(lane31, "dp", chip_bit)
     lane2 = swap(own, "expert", 2)
-    kept0 = join([own, across0], [lane31])
-    keep0, send0, weights = load_ffn(
-        kept0,
-        swap(kept0, "dp", core_bit),
-        w_in[0],
-        w_out[0],
-        experts,
-        expert,
-        [mark([lane2], DEAR)],
-    )
-    pair0 = keep0, swap(send0, "dp", core_bit)
-    across2 = swap(lane2, "dp", chip_bit)
-    kept31 = join([lane31, across31], [keep0])
-    pair31 = run(kept31, [mark([across2, kept31], DEAR)])
-    pair2 = run(join([lane2, across2], [kept31]), [pair31[0]])
-    far3 = part_sum(pair31, 2 * rows, rows, [pair2[0]])
-    far2 = part_sum(pair2, rows, rows)
-    far1 = part_sum(pair31, 3 * rows, rows, [far2])
-    far0 = part_sum(pair0, rows, rows, [far2])
-    near3 = part_sum([*pair31, swap(far3, "dp", chip_bit)], 0, rows)
-    near2 = part_sum([*pair2, swap(far2, "dp", chip_bit)], 0, rows)
-    near1 = part_sum([*pair31, swap(far1, "dp", chip_bit)], rows, rows)
-    near0 = add(*[a[:rows] for a in pair0], swap(far0, "dp", chip_bit))
-    total = sum_arrays([tokens, swap(near3, "expert", 3)], CHEAP)
-    total = sum_arrays([total, swap(near2, "expert", 2)], CHEAP)
-    return add(total, near0, swap(near1, "expert", 1)).astype(jnp.bfloat16)
+    keep0, weights = load_ffn(own, w_in[0], w_out[0], experts, expert, [])
+    lane3 = join([lane3], [keep0])
+    across3 = swap(lane3, "dp", chip_bit)
+    across1, across2 = swap(lane1, "dp", chip_bit), swap(lane2, "dp", chip_bit)
+    kept0 = join([own, across0])
+    kept3 = join([lane3, across3], [mark([lane2, mark([lane1, across0], CHEAP)], CHEAP)])
+    pair3 = run([kept3], [core_swap(kept3)], [mark([across1, kept3], SOME)])
+    far3 = part_sum(pair3, rows, rows, [mark([across2, pair3[0]], SOME)])
+    sent0 = join([core_swap(kept0)], [kept3])
+    kept2 = join([lane2, across2], [far3, sent0])
+    pair2 = run([kept2], [core_swap(kept2)])
+    kept1 = join([lane1, across1], [kept2])
+    keep1, send10 = ffn(
+        [kept1, across0], [core_swap(kept1), sent0], weights, experts, expert, [pair2[0]], CHEAP
+    )
+    back10 = core_swap(send10)
+    near3 = part_sum([*pair3, swap(far3, "dp", chip_bit)], 0, rows, [keep1], DEAR)
+    far2 = part_sum(pair2, rows, rows, [near3])
+    far1 = part_sum([keep1, back10], rows, rows, [far2])
+    near2 = part_sum([*pair2, swap(far2, "dp", chip_bit)], 0, rows, [far1])
+    far0 = join([add(keep1[2 * rows :], back10[3 * rows :]).astype(jnp.bfloat16)], [near2])
+    near1 = part_sum([keep1, back10, swap(far1, "dp", chip_bit)], 0, rows, [near2])
+    near0 = add(keep0, back10[2 * rows : 3 * rows], swap(far0, "dp", chip_bit))
+    total = sum_arrays([tokens, swap(near3, "expert", 3)], DEAR)
+    return add(total, near0, swap(near1, "expert", 1), swap(near2, "expert", 2)).astype(
+        jnp.bfloat16
+    )
 
 
 def layer_norm(tokens, ln_gain):

time: 51 us -> 50 us (0.980)
  waiting for transfers between devices: 22.2 us -> 19.3 us
  Pallas kernels: 9.18 us -> 10.2 us
  starting transfers between devices: 18.6 us -> 19.4 us
    ppermute x19 -> x21, waiting for transfers between devices: 22.2 us -> 19.3 us  [swap(): return lax.ppermute(array, axis, pairs)]
    pallas_call x6 -> x10, Pallas kernels: 3.88 us -> 5.02 us  [the longest x3 4.9 us: ffn(): pl.pallas_call(functools.partial(ffn_kernel, experts, len(kept), len(sent...]
    ppermute x19 -> x21, starting transfers between devices: 18.6 us -> 19.4 us  [swap(): return lax.ppermute(array, axis, pairs)]
  transfers between devices with their start and end apart: 19 -> 21, of which waited for: 12 -> 11; matrix products, arithmetic and copies ran while one was open for 0% -> 0% of each run, Pallas kernels for 16% -> 18%
where the time goes in v4:
time: 50 us; the launch traced here: 49.9 us
  starting transfers between devices  19.4 us (39%)
  waiting for transfers between devices  19.3 us (39%)
  Pallas kernels  10.2 us (20%)
  other arithmetic  0.78 us (2%)
    ppermute x21, starting transfers between devices, swap(): return lax.ppermute(array, axis, pairs)  19.4 us
    ppermute x21, waiting for transfers between devices, swap(): return lax.ppermute(array, axis, pairs)  19.3 us
    pallas_call x3, Pallas kernels, ffn(): pl.pallas_call(functools.partial(ffn_kernel, experts, len(kept), len(sent...  4.9 us
    pallas_call x1, Pallas kernels, load_ffn(): pl.pallas_call(functools.partial(load_ffn_kernel, experts, cuts, len(behi...  3.77 us
    pallas_call x1, Pallas kernels, norm_and_pack(): pl.pallas_call(functools.partial(norm_kernel, experts), out_shape=pltpu.V...  1.17 us
  transfers between devices with their start and end apart: 21, of which 11 were waited for; matrix products, arithmetic and copies ran while one was open for 0% of the time, Pallas kernels for 18%

profile of v4, /device:TPU:0, one launch (start us, length us, event | category | flops | bytes accessed | tf_op | source)
XLA Modules:
  0.0 49.9 jit_solution(17233884611031932706)
XLA Ops:
  0.0 1.2 %norm.1.kept_ref.refs_0_ = bf16[32,2176]{1,0:T(8,128)(2,1)S(1)} custom-call(bf16[32,2048]{1,0:T(8,128)(2,1)} %refs_0_.3, s32[2,32]{1,0:T(2,128)} %bitcast.9, f32[2,32]{1,0:T(2,128)} %bitcast.10, f32[1,2048]{1,0:T(1,128)} %bitcast.8), custom_call_target="tpu_custom_call" | custom-call | flops 1 | bytes 1 | tf_op jit(solution)/shard_map/norm/pallas_call | solution.py:63
  1.2 5.1 %collective-permute-start = (bf16[32,2176]{1,0:T(8,128)(2,1)S(1)}, bf16[32,2176]{1,0:T(8,128)(2,1)S(1)}, u32[]{:S(2)}, u32[]{:S(2)}) collective-permute-start(bf16[32,2176]{1,0:T(8,128)(2,1)S(1)} %norm.1.kept_ref.refs_0_), channel_id=1, source_target_pairs={{0,12},{4,8},{8,4},{12,0},{1,13},{5,9},{9,5},{13,1},{2,14},{6,10},... | collective-permute-start | bytes 417800 | tf_op jit(solution)/shard_map/ppermute | solution.py:304
  6.3 0.6 %collective-permute-start.2 = (bf16[32,2176]{1,0:T(8,128)(2,1)S(1)}, bf16[32,2176]{1,0:T(8,128)(2,1)S(1)}, u32[]{:S(2)}, u32[]{:S(2)}) collective-permute-start(bf16[32,2176]{1,0:T(8,128)(2,1)S(1)} %norm.1.kept_ref.refs_0_), channel_id=1, source_target_pairs={{0,8},{4,12},{8,0},{12,4},{1,9},{5,13},{9,1},{13,5},{2,10},{6,14},... | collective-permute-start | bytes 417800 | tf_op jit(solution)/shard_map/ppermute | solution.py:304
  6.9 1.6 %collective-permute-start.4 = (bf16[32,2176]{1,0:T(8,128)(2,1)S(1)}, bf16[32,2176]{1,0:T(8,128)(2,1)S(1)}, u32[]{:S(2)}, u32[]{:S(2)}) collective-permute-start(bf16[32,2176]{1,0:T(8,128)(2,1)S(1)} %norm.1.kept_ref.refs_0_), channel_id=1, source_target_pairs={{0,2},{1,3},{2,0},{3,1},{4,6},{5,7},{6,4},{7,5},{8,10},{9,11},{10,... | collective-permute-start | bytes 417800 | tf_op jit(solution)/shard_map/ppermute | solution.py:304
  8.6 3.8 %load_ffn.1 = (bf16[32,2048]{1,0:T(8,128)(2,1)S(1)}, bf16[4096,1024]{1,0:T(8,128)(2,1)S(1)}) custom-call(s32[1]{0:T(128)} %bitcast.expert_ref, bf16[32,2176]{1,0:T(8,128)(2,1)S(1)} %norm.1.kept_ref.refs_0_, bf16[2048,1024]{1,0:T(8,128)(2,1)} %bitcast.6, bf16[1024,2048]{1,0:T(8,128)(2,1)} %bitcast.7), custom_call_target="tpu_custom_call" | custom-call | flops 1 | bytes 1 | tf_op jit(solution)/shard_map/load_ffn/pallas_call | solution.py:228
  12.8 1.2 %collective-permute-done.3.refs_0_ = bf16[32,2176]{1,0:T(8,128)(2,1)S(1)} collective-permute-done((bf16[32,2176]{1,0:T(8,128)(2,1)S(1)}, bf16[32,2176]{1,0:T(8,128)(2,1)S(1)}, u32[]{:S(2)}, u32[]{:S(2)}) %collective-permute-start.3) | collective-permute-done | bytes 139296 | tf_op jit(solution)/shard_map/ppermute | solution.py:304
  14.0 1.4 %collective-permute-start.6 = (bf16[32,2176]{1,0:T(8,128)(2,1)S(1)}, bf16[32,2176]{1,0:T(8,128)(2,1)S(1)}, u32[]{:S(2)}, u32[]{:S(2)}) collective-permute-start(bf16[32,2176]{1,0:T(8,128)(2,1)S(1)} %collective-permute-done.3.refs_0_), channel_id=1, source_target_pairs={{0,2},{1,3},{2,0},{3,1},{4,6},{5,7},{6,4},{7,5},{8,10},{9,11},{10,... | collective-permute-start | bytes 417800 | tf_op jit(solution)/shard_map/ppermute | solution.py:304
  15.5 2.6 %collective-permute-done.2.refs_0_ = bf16[32,2176]{1,0:T(8,128)(2,1)S(1)} collective-permute-done((bf16[32,2176]{1,0:T(8,128)(2,1)S(1)}, bf16[32,2176]{1,0:T(8,128)(2,1)S(1)}, u32[]{:S(2)}, u32[]{:S(2)}) %collective-permute-start.2) | collective-permute-done | bytes 139296 | tf_op jit(solution)/shard_map/ppermute | solution.py:304
  18.1 0.7 %collective-permute-done.1.refs_1_ = bf16[32,2176]{1,0:T(8,128)(2,1)S(1)} collective-permute-done((bf16[32,2176]{1,0:T(8,128)(2,1)S(1)}, bf16[32,2176]{1,0:T(8,128)(2,1)S(1)}, u32[]{:S(2)}, u32[]{:S(2)}) %collective-permute-start.1) | collective-permute-done | bytes 139296 | tf_op jit(solution)/shard_map/ppermute | solution.py:304
  19.4 0.8 %collective-permute-start.8 = (bf16[32,2176]{1,0:T(8,128)(2,1)S(1)}, bf16[32,2176]{1,0:T(8,128)(2,1)S(1)}, u32[]{:S(2)}, u32[]{:S(2)}) collective-permute-start(bf16[32,2176]{1,0:T(8,128)(2,1)S(1)} %collective-permute-done.2.refs_0_), channel_id=1, source_target_pairs={{0,2},{1,3},{2,0},{3,1},{4,6},{5,7},{6,4},{7,5},{8,10},{9,11},{10,... | collective-permute-start | bytes 417800 | tf_op jit(solution)/shard_map/ppermute | solution.py:304
  20.5 1.4 %ffn.3 = (bf16[64,2048]{1,0:T(8,128)(2,1)S(1)}, bf16[64,2048]{1,0:T(8,128)(2,1)S(1)}) custom-call(s32[1]{0:T(128)} %bitcast.expert_ref, bf16[64,2176]{1,0:T(8,128)(2,1)S(1)} %join.8.refs_1_.refs_0_, bf16[64,2176]{1,0:T(8,128)(2,1)S(1)} %collective-permute-done.5.refs_1_, bf16[4096,1024]{1,0:T(8,128)(2,1)S(1)} %get-tuple-element.14.refs_2_.refs_4_, ...), custom_call_target="tpu_custom_call" | custom-call | flops 1073741824 | bytes 8388608 | tf_op jit(solution)/shard_map/ffn/pallas_call | solution.py:280
  22.0 3.1 %collective-permute-done.8.refs_0_.refs_1_ = bf16[32,2176]{1,0:T(8,128)(2,1)S(1)} collective-permute-done((bf16[32,2176]{1,0:T(8,128)(2,1)S(1)}, bf16[32,2176]{1,0:T(8,128)(2,1)S(1)}, u32[]{:S(2)}, u32[]{:S(2)}) %collective-permute-start.8) | collective-permute-done | bytes 139296 | tf_op jit(solution)/shard_map/ppermute | solution.py:304
  25.8 0.8 %collective-permute-start.9 = (bf16[32,2048]{1,0:T(8,128)(2,1)S(1)}, bf16[32,2048]{1,0:T(8,128)(2,1)S(1)}, u32[]{:S(2)}, u32[]{:S(2)}) collective-permute-start(bf16[32,2048]{1,0:T(8,128)(2,1)S(1)} %part.6.refs_2_), channel_id=1, source_target_pairs={{0,2},{1,3},{2,0},{3,1},{4,6},{5,7},{6,4},{7,5},{8,10},{9,11},{10,... | collective-permute-start | bytes 393224 | tf_op jit(solution)/shard_map/ppermute | solution.py:304
  26.8 1.4 %ffn.4 = (bf16[64,2048]{1,0:T(8,128)(2,1)S(1)}, bf16[64,2048]{1,0:T(8,128)(2,1)S(1)}) custom-call(s32[1]{0:T(128)} %bitcast.expert_ref, bf16[64,2176]{1,0:T(8,128)(2,1)S(1)} %join.11.refs_2_.refs_0_, bf16[64,2176]{1,0:T(8,128)(2,1)S(1)} %collective-permute-done.12.refs_1_, bf16[4096,1024]{1,0:T(8,128)(2,1)S(1)} %get-tuple-element.14.refs_2_.refs_4_), custom_call_target="tpu_custom_call" | custom-call | flops 1073741824 | bytes 8388608 | tf_op jit(solution)/shard_map/ffn/pallas_call | solution.py:280
  28.3 2.1 %ffn.5 = (bf16[96,2048]{1,0:T(8,128)(2,1)S(1)}, bf16[128,2048]{1,0:T(8,128)(2,1)S(1)}) custom-call(s32[1]{0:T(128)} %bitcast.expert_ref, bf16[64,2176]{1,0:T(8,128)(2,1)S(1)} %join.12.refs_0_, bf16[32,2176]{1,0:T(8,128)(2,1)S(1)} %collective-permute-done.4.refs_1_, bf16[64,2176]{1,0:T(8,128)(2,1)S(1)} %collective-permute-done.11.refs_2_, ...), custom_call_target="tpu_custom_call" | custom-call | flops 1879048192 | bytes 8388608 | tf_op jit(solution)/shard_map/ffn/pallas_call | solution.py:280
  31.4 3.2 %collective-permute-start.13 = (bf16[32,2048]{1,0:T(8,128)(2,1)S(1)}, bf16[32,2048]{1,0:T(8,128)(2,1)S(1)}, u32[]{:S(2)}, u32[]{:S(2)}) collective-permute-start(bf16[32,2048]{1,0:T(8,128)(2,1)S(1)} %part.7.refs_2_), channel_id=1, source_target_pairs={{0,12},{4,8},{8,4},{12,0},{1,13},{5,9},{9,5},{13,1},{2,14},{6,10},... | collective-permute-start | bytes 393224 | tf_op jit(solution)/shard_map/ppermute | solution.py:304
  34.6 0.8 %collective-permute-start.16 = (bf16[32,2048]{1,0:T(8,128)(2,1)S(1)}, bf16[32,2048]{1,0:T(8,128)(2,1)S(1)}, u32[]{:S(2)}, u32[]{:S(2)}) collective-permute-start(bf16[32,2048]{1,0:T(8,128)(2,1)S(1)} %part.8.refs_2_), channel_id=1, source_target_pairs={{0,2},{1,3},{2,0},{3,1},{4,6},{5,7},{6,4},{7,5},{8,10},{9,11},{10,... | collective-permute-start | bytes 393224 | tf_op jit(solution)/shard_map/ppermute | solution.py:304
  35.4 1.4 %collective-permute-start.18 = (bf16[32,2048]{1,0:T(8,128)(2,1)S(1)}, bf16[32,2048]{1,0:T(8,128)(2,1)S(1)}, u32[]{:S(2)}, u32[]{:S(2)}) collective-permute-start(bf16[32,2048]{1,0:T(8,128)(2,1)S(1)} %part.9.refs_3_), channel_id=1, source_target_pairs={{0,2},{1,3},{2,0},{3,1},{4,6},{5,7},{6,4},{7,5},{8,10},{9,11},{10,... | collective-permute-start | bytes 393224 | tf_op jit(solution)/shard_map/ppermute | solution.py:304
  36.8 4.1 %collective-permute-done.16.refs_2_ = bf16[32,2048]{1,0:T(8,128)(2,1)S(1)} collective-permute-done((bf16[32,2048]{1,0:T(8,128)(2,1)S(1)}, bf16[32,2048]{1,0:T(8,128)(2,1)S(1)}, u32[]{:S(2)}, u32[]{:S(2)}) %collective-permute-start.16) | collective-permute-done | bytes 131104 | tf_op jit(solution)/shard_map/ppermute | solution.py:304
  41.1 1.0 %collective-permute-start.17 = (bf16[32,2048]{1,0:T(8,128)(2,1)S(1)}, bf16[32,2048]{1,0:T(8,128)(2,1)S(1)}, u32[]{:S(2)}, u32[]{:S(2)}) collective-permute-start(bf16[32,2048]{1,0:T(8,128)(2,1)S(1)} %join.13), channel_id=1, source_target_pairs={{0,2},{1,3},{2,0},{3,1},{4,6},{5,7},{6,4},{7,5},{8,10},{9,11},{10,... | collective-permute-start | bytes 393224 | tf_op jit(solution)/shard_map/ppermute | solution.py:304
  42.1 1.5 %collective-permute-done.18.refs_2_ = bf16[32,2048]{1,0:T(8,128)(2,1)S(1)} collective-permute-done((bf16[32,2048]{1,0:T(8,128)(2,1)S(1)}, bf16[32,2048]{1,0:T(8,128)(2,1)S(1)}, u32[]{:S(2)}, u32[]{:S(2)}) %collective-permute-start.18) | collective-permute-done | bytes 131104 | tf_op jit(solution)/shard_map/ppermute | solution.py:304
  43.8 4.0 %collective-permute-done.20 = bf16[32,2048]{1,0:T(8,128)(2,1)S(1)} collective-permute-done((bf16[32,2048]{1,0:T(8,128)(2,1)S(1)}, bf16[32,2048]{1,0:T(8,128)(2,1)S(1)}, u32[]{:S(2)}, u32[]{:S(2)}) %collective-permute-start.20) | collective-permute-done | bytes 131104 | tf_op jit(solution)/shard_map/ppermute | solution.py:304
  47.8 1.4 %collective-permute-done.19 = bf16[32,2048]{1,0:T(8,128)(2,1)S(1)} collective-permute-done((bf16[32,2048]{1,0:T(8,128)(2,1)S(1)}, bf16[32,2048]{1,0:T(8,128)(2,1)S(1)}, u32[]{:S(2)}, u32[]{:S(2)}) %collective-permute-start.19) | collective-permute-done | bytes 131104 | tf_op jit(solution)/shard_map/ppermute | solution.py:304
  49.1 0.7 %add_convert_fusion = bf16[32,2048]{1,0:T(8,128)(2,1)} fusion(bf16[32,2048]{1,0:T(8,128)(2,1)S(1)} %collective-permute-done.20, bf16[32,2048]{1,0:T(8,128)(2,1)S(1)} %collective-permute-done.19, f32[32,2048]{1,0:T(8,128)S(1)} %sum.1, bf16[32,2048]{1,0:T(8,128)(2,1)S(1)} %collective-permute-done.17, bf16[32,2048]{1,0:T(8,128)(2,1)S(1)} %get-tuple-element.13.refs_1_, ...), kind=kLoop, calls=%fused_computation | loop fusion | flops 720896 | bytes 1048576 | tf_op jit(solution)/shard_map/convert_element_type | solution.py:352
  (45 shorter events, 3.8 us)
Async XLA Ops:
  1.2 11.2 %collective-permute-start = (bf16[32,2176]{1,0:T(8,128)(2,1)S(1)}, bf16[32,2176]{1,0:T(8,128)(2,1)S(1)}, u32[]{:S(2)}, u32[]{:S(2)}) collective-permute-start(bf16[32,2176]{1,0:T(8,128)(2,1)S(1)} %norm.1.kept_ref.refs_0_), channel_id=1, source_target_pairs={{0,12},{4,8},{8,4},{12,0},{1,13},{5,9},{9,5},{13,1},{2,14},{6,10},... | collective-permute-start | bytes 417800 | tf_op jit(solution)/shard_map/ppermute | solution.py:304
  6.3 7.7 %collective-permute-start.3 = (bf16[32,2176]{1,0:T(8,128)(2,1)S(1)}, bf16[32,2176]{1,0:T(8,128)(2,1)S(1)}, u32[]{:S(2)}, u32[]{:S(2)}) collective-permute-start(bf16[32,2176]{1,0:T(8,128)(2,1)S(1)} %norm.1.kept_ref.refs_0_), channel_id=1, source_target_pairs={{0,4},{4,0},{8,12},{12,8},{1,5},{5,1},{9,13},{13,9},{2,6},{6,2},{1... | collective-permute-start | bytes 417800 | tf_op jit(solution)/shard_map/ppermute | solution.py:304
  6.3 11.8 %collective-permute-start.2 = (bf16[32,2176]{1,0:T(8,128)(2,1)S(1)}, bf16[32,2176]{1,0:T(8,128)(2,1)S(1)}, u32[]{:S(2)}, u32[]{:S(2)}) collective-permute-start(bf16[32,2176]{1,0:T(8,128)(2,1)S(1)} %norm.1.kept_ref.refs_0_), channel_id=1, source_target_pairs={{0,8},{4,12},{8,0},{12,4},{1,9},{5,13},{9,1},{13,5},{2,10},{6,14},... | collective-permute-start | bytes 417800 | tf_op jit(solution)/shard_map/ppermute | solution.py:304
  6.9 8.5 %collective-permute-start.4 = (bf16[32,2176]{1,0:T(8,128)(2,1)S(1)}, bf16[32,2176]{1,0:T(8,128)(2,1)S(1)}, u32[]{:S(2)}, u32[]{:S(2)}) collective-permute-start(bf16[32,2176]{1,0:T(8,128)(2,1)S(1)} %norm.1.kept_ref.refs_0_), channel_id=1, source_target_pairs={{0,2},{1,3},{2,0},{3,1},{4,6},{5,7},{6,4},{7,5},{8,10},{9,11},{10,... | collective-permute-start | bytes 417800 | tf_op jit(solution)/shard_map/ppermute | solution.py:304
  12.4 6.3 %collective-permute-start.1 = (bf16[32,2176]{1,0:T(8,128)(2,1)S(1)}, bf16[32,2176]{1,0:T(8,128)(2,1)S(1)}, u32[]{:S(2)}, u32[]{:S(2)}) collective-permute-start(bf16[32,2176]{1,0:T(8,128)(2,1)S(1)} %join.7.refs_0_), channel_id=1, source_target_pairs={{0,2},{1,3},{2,0},{3,1},{4,6},{5,7},{6,4},{7,5},{8,10},{9,11},{10,... | collective-permute-start | bytes 417800 | tf_op jit(solution)/shard_map/ppermute | solution.py:304
  14.0 6.4 %collective-permute-start.6 = (bf16[32,2176]{1,0:T(8,128)(2,1)S(1)}, bf16[32,2176]{1,0:T(8,128)(2,1)S(1)}, u32[]{:S(2)}, u32[]{:S(2)}) collective-permute-start(bf16[32,2176]{1,0:T(8,128)(2,1)S(1)} %collective-permute-done.3.refs_0_), channel_id=1, source_target_pairs={{0,2},{1,3},{2,0},{3,1},{4,6},{5,7},{6,4},{7,5},{8,10},{9,11},{10,... | collective-permute-start | bytes 417800 | tf_op jit(solution)/shard_map/ppermute | solution.py:304
  18.7 1.7 %collective-permute-start.5 = (bf16[64,2176]{1,0:T(8,128)(2,1)S(1)}, bf16[64,2176]{1,0:T(8,128)(2,1)S(1)}, u32[]{:S(2)}, u32[]{:S(2)}) collective-permute-start(bf16[64,2176]{1,0:T(8,128)(2,1)S(1)} %join.8.refs_1_.refs_0_), channel_id=1, source_target_pairs={{0,1},{1,0},{2,3},{3,2},{4,5},{5,4},{6,7},{7,6},{8,9},{9,8},{10,11... | collective-permute-start | bytes 835592 | tf_op jit(solution)/shard_map/ppermute | solution.py:304
  18.9 3.1 %collective-permute-start.10 = (bf16[64,2176]{1,0:T(8,128)(2,1)S(1)}, bf16[64,2176]{1,0:T(8,128)(2,1)S(1)}, u32[]{:S(2)}, u32[]{:S(2)}) collective-permute-start(bf16[64,2176]{1,0:T(8,128)(2,1)S(1)} %join.9), channel_id=1, source_target_pairs={{0,1},{1,0},{2,3},{3,2},{4,5},{5,4},{6,7},{7,6},{8,9},{9,8},{10,11... | collective-permute-start | bytes 835592 | tf_op jit(solution)/shard_map/ppermute | solution.py:304
  19.4 5.7 %collective-permute-start.8 = (bf16[32,2176]{1,0:T(8,128)(2,1)S(1)}, bf16[32,2176]{1,0:T(8,128)(2,1)S(1)}, u32[]{:S(2)}, u32[]{:S(2)}) collective-permute-start(bf16[32,2176]{1,0:T(8,128)(2,1)S(1)} %collective-permute-done.2.refs_0_), channel_id=1, source_target_pairs={{0,2},{1,3},{2,0},{3,1},{4,6},{5,7},{6,4},{7,5},{8,10},{9,11},{10,... | collective-permute-start | bytes 417800 | tf_op jit(solution)/shard_map/ppermute | solution.py:304
  21.9 3.2 %collective-permute-start.7 = (bf16[64,2048]{1,0:T(8,128)(2,1)S(1)}, bf16[64,2048]{1,0:T(8,128)(2,1)S(1)}, u32[]{:S(2)}, u32[]{:S(2)}) collective-permute-start(bf16[64,2048]{1,0:T(8,128)(2,1)S(1)} %get-tuple-element.16), channel_id=1, source_target_pairs={{0,1},{1,0},{2,3},{3,2},{4,5},{5,4},{6,7},{7,6},{8,9},{9,8},{10,11... | collective-permute-start | bytes 786440 | tf_op jit(solution)/shard_map/ppermute | solution.py:304
  25.1 1.6 %collective-permute-start.12 = (bf16[64,2176]{1,0:T(8,128)(2,1)S(1)}, bf16[64,2176]{1,0:T(8,128)(2,1)S(1)}, u32[]{:S(2)}, u32[]{:S(2)}) collective-permute-start(bf16[64,2176]{1,0:T(8,128)(2,1)S(1)} %join.11.refs_2_.refs_0_), channel_id=1, source_target_pairs={{0,1},{1,0},{2,3},{3,2},{4,5},{5,4},{6,7},{7,6},{8,9},{9,8},{10,11... | collective-permute-start | bytes 835592 | tf_op jit(solution)/shard_map/ppermute | solution.py:304
  25.2 3.1 %collective-permute-start.11 = (bf16[64,2176]{1,0:T(8,128)(2,1)S(1)}, bf16[64,2176]{1,0:T(8,128)(2,1)S(1)}, u32[]{:S(2)}, u32[]{:S(2)}) collective-permute-start(bf16[64,2176]{1,0:T(8,128)(2,1)S(1)} %join.12.refs_0_), channel_id=1, source_target_pairs={{0,1},{1,0},{2,3},{3,2},{4,5},{5,4},{6,7},{7,6},{8,9},{9,8},{10,11... | collective-permute-start | bytes 835592 | tf_op jit(solution)/shard_map/ppermute | solution.py:304
  25.8 5.5 %collective-permute-start.9 = (bf16[32,2048]{1,0:T(8,128)(2,1)S(1)}, bf16[32,2048]{1,0:T(8,128)(2,1)S(1)}, u32[]{:S(2)}, u32[]{:S(2)}) collective-permute-start(bf16[32,2048]{1,0:T(8,128)(2,1)S(1)} %part.6.refs_2_), channel_id=1, source_target_pairs={{0,2},{1,3},{2,0},{3,1},{4,6},{5,7},{6,4},{7,5},{8,10},{9,11},{10,... | collective-permute-start | bytes 393224 | tf_op jit(solution)/shard_map/ppermute | solution.py:304
  28.1 6.4 %collective-permute-start.15 = (bf16[64,2048]{1,0:T(8,128)(2,1)S(1)}, bf16[64,2048]{1,0:T(8,128)(2,1)S(1)}, u32[]{:S(2)}, u32[]{:S(2)}) collective-permute-start(bf16[64,2048]{1,0:T(8,128)(2,1)S(1)} %get-tuple-element.20), channel_id=1, source_target_pairs={{0,1},{1,0},{2,3},{3,2},{4,5},{5,4},{6,7},{7,6},{8,9},{9,8},{10,11... | collective-permute-start | bytes 786440 | tf_op jit(solution)/shard_map/ppermute | solution.py:304
  30.5 4.9 %collective-permute-start.14 = (bf16[128,2048]{1,0:T(8,128)(2,1)S(1)}, bf16[128,2048]{1,0:T(8,128)(2,1)S(1)}, u32[]{:S(2)}, u32[]{:S(2)}) collective-permute-start(bf16[128,2048]{1,0:T(8,128)(2,1)S(1)} %get-tuple-element.19), channel_id=1, source_target_pairs={{0,1},{1,0},{2,3},{3,2},{4,5},{5,4},{6,7},{7,6},{8,9},{9,8},{10,11... | collective-permute-start | bytes 1572872 | tf_op jit(solution)/shard_map/ppermute | solution.py:304
  31.3 12.4 %copy-start = (bf16[32,2048]{1,0:T(8,128)(2,1)S(1)}, bf16[32,2048]{1,0:T(8,128)(2,1)}, u32[]{:S(2)}) copy-start(bf16[32,2048]{1,0:T(8,128)(2,1)} %refs_0_.3) | copy-start | bytes 393220
  31.4 12.3 %collective-permute-start.13 = (bf16[32,2048]{1,0:T(8,128)(2,1)S(1)}, bf16[32,2048]{1,0:T(8,128)(2,1)S(1)}, u32[]{:S(2)}, u32[]{:S(2)}) collective-permute-start(bf16[32,2048]{1,0:T(8,128)(2,1)S(1)} %part.7.refs_2_), channel_id=1, source_target_pairs={{0,12},{4,8},{8,4},{12,0},{1,13},{5,9},{9,5},{13,1},{2,14},{6,10},... | collective-permute-start | bytes 393224 | tf_op jit(solution)/shard_map/ppermute | solution.py:304
  34.6 6.4 %collective-permute-start.16 = (bf16[32,2048]{1,0:T(8,128)(2,1)S(1)}, bf16[32,2048]{1,0:T(8,128)(2,1)S(1)}, u32[]{:S(2)}, u32[]{:S(2)}) collective-permute-start(bf16[32,2048]{1,0:T(8,128)(2,1)S(1)} %part.8.refs_2_), channel_id=1, source_target_pairs={{0,2},{1,3},{2,0},{3,1},{4,6},{5,7},{6,4},{7,5},{8,10},{9,11},{10,... | collective-permute-start | bytes 393224 | tf_op jit(solution)/shard_map/ppermute | solution.py:304
  35.4 8.2 %collective-permute-start.18 = (bf16[32,2048]{1,0:T(8,128)(2,1)S(1)}, bf16[32,2048]{1,0:T(8,128)(2,1)S(1)}, u32[]{:S(2)}, u32[]{:S(2)}) collective-permute-start(bf16[32,2048]{1,0:T(8,128)(2,1)S(1)} %part.9.refs_3_), channel_id=1, source_target_pairs={{0,2},{1,3},{2,0},{3,1},{4,6},{5,7},{6,4},{7,5},{8,10},{9,11},{10,... | collective-permute-start | bytes 393224 | tf_op jit(solution)/shard_map/ppermute | solution.py:304
  41.0 6.8 %collective-permute-start.20 = (bf16[32,2048]{1,0:T(8,128)(2,1)S(1)}, bf16[32,2048]{1,0:T(8,128)(2,1)S(1)}, u32[]{:S(2)}, u32[]{:S(2)}) collective-permute-start(bf16[32,2048]{1,0:T(8,128)(2,1)S(1)} %part.10.refs_1_.refs_3_), channel_id=1, source_target_pairs={{0,8},{4,12},{8,0},{12,4},{1,9},{5,13},{9,1},{13,5},{2,10},{6,14},... | collective-permute-start | bytes 393224 | tf_op jit(solution)/shard_map/ppermute | solution.py:304
  41.1 6.7 %collective-permute-start.17 = (bf16[32,2048]{1,0:T(8,128)(2,1)S(1)}, bf16[32,2048]{1,0:T(8,128)(2,1)S(1)}, u32[]{:S(2)}, u32[]{:S(2)}) collective-permute-start(bf16[32,2048]{1,0:T(8,128)(2,1)S(1)} %join.13), channel_id=1, source_target_pairs={{0,2},{1,3},{2,0},{3,1},{4,6},{5,7},{6,4},{7,5},{8,10},{9,11},{10,... | collective-permute-start | bytes 393224 | tf_op jit(solution)/shard_map/ppermute | solution.py:304
  43.6 5.5 %collective-permute-start.19 = (bf16[32,2048]{1,0:T(8,128)(2,1)S(1)}, bf16[32,2048]{1,0:T(8,128)(2,1)S(1)}, u32[]{:S(2)}, u32[]{:S(2)}) collective-permute-start(bf16[32,2048]{1,0:T(8,128)(2,1)S(1)} %part.11), channel_id=1, source_target_pairs={{0,4},{4,0},{8,12},{12,8},{1,5},{5,1},{9,13},{13,9},{2,6},{6,2},{1... | collective-permute-start | bytes 393224 | tf_op jit(solution)/shard_map/ppermute | solution.py:304

commit v5 on v4

--- a/solution.py
+++ b/solution.py
@@ -13,7 +13,7 @@
 SMALL = pltpu.CompilerParams(vmem_limit_bytes=4 * 1024 * 1024)
 CHEAP = pl.CostEstimate(flops=1, bytes_accessed=1, transcendentals=0)
 DEAR = pl.CostEstimate(flops=10**10, bytes_accessed=1, transcendentals=0)
-SOME = pl.CostEstimate(flops=2*10**9, bytes_accessed=1, transcendentals=0)
+SOME = pl.CostEstimate(flops=4*10**9, bytes_accessed=1, transcendentals=0)
 ANY = pl.BlockSpec(memory_space=pl.ANY)
 
 
@@ -345,8 +345,8 @@
     far2 = part_sum(pair2, rows, rows, [near3])
     far1 = part_sum([keep1, back10], rows, rows, [far2])
     near2 = part_sum([*pair2, swap(far2, "dp", chip_bit)], 0, rows, [far1])
-    far0 = join([add(keep1[2 * rows :], back10[3 * rows :]).astype(jnp.bfloat16)], [near2])
     near1 = part_sum([keep1, back10, swap(far1, "dp", chip_bit)], 0, rows, [near2])
+    far0 = join([add(keep1[2 * rows :], back10[3 * rows :]).astype(jnp.bfloat16)], [near1])
     near0 = add(keep0, back10[2 * rows : 3 * rows], swap(far0, "dp", chip_bit))
     total = sum_arrays([tokens, swap(near3, "expert", 3)], DEAR)
     return add(total, near0, swap(near1, "expert", 1), swap(near2, "expert", 2)).astype(

time: 50 us -> 47.7 us (0.954)
  waiting for transfers between devices: 19.3 us -> 12.5 us
  starting transfers between devices: 19.4 us -> 23.9 us
    ppermute x21, waiting for transfers between devices: 19.3 us -> 12.5 us  [swap(): return lax.ppermute(array, axis, pairs)]
    ppermute x21, starting transfers between devices: 19.4 us -> 23.9 us  [swap(): return lax.ppermute(array, axis, pairs)]
  transfers between devices with their start and end apart: 21 -> 21, of which waited for: 11 -> 11; matrix products, arithmetic and copies ran while one was open for 0% -> 0% of each run, Pallas kernels for 18% -> 19%
where the time goes in v5:
time: 47.7 us; the launch traced here: 47.6 us
  starting transfers between devices  23.9 us (50%)
  waiting for transfers between devices  12.5 us (26%)
  Pallas kernels  10.2 us (21%)
  other arithmetic  0.78 us (2%)
    ppermute x21, starting transfers between devices, swap(): return lax.ppermute(array, axis, pairs)  23.9 us
    ppermute x21, waiting for transfers between devices, swap(): return lax.ppermute(array, axis, pairs)  12.5 us
    pallas_call x3, Pallas kernels, ffn(): pl.pallas_call(functools.partial(ffn_kernel, experts, len(kept), len(sent...  4.89 us
    pallas_call x1, Pallas kernels, load_ffn(): pl.pallas_call(functools.partial(load_ffn_kernel, experts, cuts, len(behi...  3.77 us
    pallas_call x1, Pallas kernels, norm_and_pack(): pl.pallas_call(functools.partial(norm_kernel, experts), out_shape=pltpu.V...  1.17 us
  transfers between devices with their start and end apart: 21, of which 11 were waited for; matrix products, arithmetic and copies ran while one was open for 0% of the time, Pallas kernels for 19%

profile of v5, /device:TPU:0, one launch (start us, length us, event | category | flops | bytes accessed | tf_op | source)
XLA Modules:
  0.0 47.6 jit_solution(13003256466304192922)
XLA Ops:
  0.0 1.2 %norm.1.kept_ref.refs_0_ = bf16[32,2176]{1,0:T(8,128)(2,1)S(1)} custom-call(bf16[32,2048]{1,0:T(8,128)(2,1)} %refs_0_.3, s32[2,32]{1,0:T(2,128)} %bitcast.9, f32[2,32]{1,0:T(2,128)} %bitcast.10, f32[1,2048]{1,0:T(1,128)} %bitcast.8), custom_call_target="tpu_custom_call" | custom-call | flops 1 | bytes 1 | tf_op jit(solution)/shard_map/norm/pallas_call | solution.py:63
  1.2 5.1 %collective-permute-start = (bf16[32,2176]{1,0:T(8,128)(2,1)S(1)}, bf16[32,2176]{1,0:T(8,128)(2,1)S(1)}, u32[]{:S(2)}, u32[]{:S(2)}) collective-permute-start(bf16[32,2176]{1,0:T(8,128)(2,1)S(1)} %norm.1.kept_ref.refs_0_), channel_id=1, source_target_pairs={{0,12},{4,8},{8,4},{12,0},{1,13},{5,9},{9,5},{13,1},{2,14},{6,10},... | collective-permute-start | bytes 417800 | tf_op jit(solution)/shard_map/ppermute | solution.py:304
  6.3 0.6 %collective-permute-start.2 = (bf16[32,2176]{1,0:T(8,128)(2,1)S(1)}, bf16[32,2176]{1,0:T(8,128)(2,1)S(1)}, u32[]{:S(2)}, u32[]{:S(2)}) collective-permute-start(bf16[32,2176]{1,0:T(8,128)(2,1)S(1)} %norm.1.kept_ref.refs_0_), channel_id=1, source_target_pairs={{0,8},{4,12},{8,0},{12,4},{1,9},{5,13},{9,1},{13,5},{2,10},{6,14},... | collective-permute-start | bytes 417800 | tf_op jit(solution)/shard_map/ppermute | solution.py:304
  6.9 1.6 %collective-permute-start.4 = (bf16[32,2176]{1,0:T(8,128)(2,1)S(1)}, bf16[32,2176]{1,0:T(8,128)(2,1)S(1)}, u32[]{:S(2)}, u32[]{:S(2)}) collective-permute-start(bf16[32,2176]{1,0:T(8,128)(2,1)S(1)} %norm.1.kept_ref.refs_0_), channel_id=1, source_target_pairs={{0,2},{1,3},{2,0},{3,1},{4,6},{5,7},{6,4},{7,5},{8,10},{9,11},{10,... | collective-permute-start | bytes 417800 | tf_op jit(solution)/shard_map/ppermute | solution.py:304
  8.6 3.8 %load_ffn.1 = (bf16[32,2048]{1,0:T(8,128)(2,1)S(1)}, bf16[4096,1024]{1,0:T(8,128)(2,1)S(1)}) custom-call(s32[1]{0:T(128)} %bitcast.expert_ref, bf16[32,2176]{1,0:T(8,128)(2,1)S(1)} %norm.1.kept_ref.refs_0_, bf16[2048,1024]{1,0:T(8,128)(2,1)} %bitcast.6, bf16[1024,2048]{1,0:T(8,128)(2,1)} %bitcast.7), custom_call_target="tpu_custom_call" | custom-call | flops 1 | bytes 1 | tf_op jit(solution)/shard_map/load_ffn/pallas_call | solution.py:228
  12.8 1.2 %collective-permute-done.3.refs_0_ = bf16[32,2176]{1,0:T(8,128)(2,1)S(1)} collective-permute-done((bf16[32,2176]{1,0:T(8,128)(2,1)S(1)}, bf16[32,2176]{1,0:T(8,128)(2,1)S(1)}, u32[]{:S(2)}, u32[]{:S(2)}) %collective-permute-start.3) | collective-permute-done | bytes 139296 | tf_op jit(solution)/shard_map/ppermute | solution.py:304
  14.0 1.4 %collective-permute-start.6 = (bf16[32,2176]{1,0:T(8,128)(2,1)S(1)}, bf16[32,2176]{1,0:T(8,128)(2,1)S(1)}, u32[]{:S(2)}, u32[]{:S(2)}) collective-permute-start(bf16[32,2176]{1,0:T(8,128)(2,1)S(1)} %collective-permute-done.3.refs_0_), channel_id=1, source_target_pairs={{0,2},{1,3},{2,0},{3,1},{4,6},{5,7},{6,4},{7,5},{8,10},{9,11},{10,... | collective-permute-start | bytes 417800 | tf_op jit(solution)/shard_map/ppermute | solution.py:304
  15.6 2.5 %collective-permute-done.2.refs_0_ = bf16[32,2176]{1,0:T(8,128)(2,1)S(1)} collective-permute-done((bf16[32,2176]{1,0:T(8,128)(2,1)S(1)}, bf16[32,2176]{1,0:T(8,128)(2,1)S(1)}, u32[]{:S(2)}, u32[]{:S(2)}) %collective-permute-start.2) | collective-permute-done | bytes 139296 | tf_op jit(solution)/shard_map/ppermute | solution.py:304
  18.1 1.5 %collective-permute-start.8 = (bf16[32,2176]{1,0:T(8,128)(2,1)S(1)}, bf16[32,2176]{1,0:T(8,128)(2,1)S(1)}, u32[]{:S(2)}, u32[]{:S(2)}) collective-permute-start(bf16[32,2176]{1,0:T(8,128)(2,1)S(1)} %collective-permute-done.2.refs_0_), channel_id=1, source_target_pairs={{0,2},{1,3},{2,0},{3,1},{4,6},{5,7},{6,4},{7,5},{8,10},{9,11},{10,... | collective-permute-start | bytes 417800 | tf_op jit(solution)/shard_map/ppermute | solution.py:304
  19.7 1.4 %collective-permute-done.6.refs_0_.refs_1_ = bf16[32,2176]{1,0:T(8,128)(2,1)S(1)} collective-permute-done((bf16[32,2176]{1,0:T(8,128)(2,1)S(1)}, bf16[32,2176]{1,0:T(8,128)(2,1)S(1)}, u32[]{:S(2)}, u32[]{:S(2)}) %collective-permute-start.6) | collective-permute-done | bytes 139296 | tf_op jit(solution)/shard_map/ppermute | solution.py:304
  21.2 1.4 %ffn.3 = (bf16[64,2048]{1,0:T(8,128)(2,1)S(1)}, bf16[64,2048]{1,0:T(8,128)(2,1)S(1)}) custom-call(s32[1]{0:T(128)} %bitcast.expert_ref, bf16[64,2176]{1,0:T(8,128)(2,1)S(1)} %join.8.refs_1_.refs_0_, bf16[64,2176]{1,0:T(8,128)(2,1)S(1)} %collective-permute-done.5.refs_1_, bf16[4096,1024]{1,0:T(8,128)(2,1)S(1)} %get-tuple-element.14.refs_2_.refs_4_, ...), custom_call_target="tpu_custom_call" | custom-call | flops 1073741824 | bytes 8388608 | tf_op jit(solution)/shard_map/ffn/pallas_call | solution.py:280
  22.8 0.7 %collective-permute-done.8.refs_0_.refs_1_ = bf16[32,2176]{1,0:T(8,128)(2,1)S(1)} collective-permute-done((bf16[32,2176]{1,0:T(8,128)(2,1)S(1)}, bf16[32,2176]{1,0:T(8,128)(2,1)S(1)}, u32[]{:S(2)}, u32[]{:S(2)}) %collective-permute-start.8) | collective-permute-done | bytes 139296 | tf_op jit(solution)/shard_map/ppermute | solution.py:304
  23.5 0.7 %collective-permute-done.7.refs_1_ = bf16[64,2048]{1,0:T(8,128)(2,1)S(1)} collective-permute-done((bf16[64,2048]{1,0:T(8,128)(2,1)S(1)}, bf16[64,2048]{1,0:T(8,128)(2,1)S(1)}, u32[]{:S(2)}, u32[]{:S(2)}) %collective-permute-start.7) | collective-permute-done | bytes 262176 | tf_op jit(solution)/shard_map/ppermute | solution.py:304
  25.9 1.4 %ffn.4 = (bf16[64,2048]{1,0:T(8,128)(2,1)S(1)}, bf16[64,2048]{1,0:T(8,128)(2,1)S(1)}) custom-call(s32[1]{0:T(128)} %bitcast.expert_ref, bf16[64,2176]{1,0:T(8,128)(2,1)S(1)} %join.11.refs_2_.refs_0_, bf16[64,2176]{1,0:T(8,128)(2,1)S(1)} %collective-permute-done.12.refs_1_, bf16[4096,1024]{1,0:T(8,128)(2,1)S(1)} %get-tuple-element.14.refs_2_.refs_4_), custom_call_target="tpu_custom_call" | custom-call | flops 1073741824 | bytes 8388608 | tf_op jit(solution)/shard_map/ffn/pallas_call | solution.py:280
  27.5 2.1 %ffn.5 = (bf16[96,2048]{1,0:T(8,128)(2,1)S(1)}, bf16[128,2048]{1,0:T(8,128)(2,1)S(1)}) custom-call(s32[1]{0:T(128)} %bitcast.expert_ref, bf16[64,2176]{1,0:T(8,128)(2,1)S(1)} %join.12.refs_0_, bf16[32,2176]{1,0:T(8,128)(2,1)S(1)} %collective-permute-done.4.refs_1_, bf16[64,2176]{1,0:T(8,128)(2,1)S(1)} %collective-permute-done.11.refs_2_, ...), custom_call_target="tpu_custom_call" | custom-call | flops 1879048192 | bytes 8388608 | tf_op jit(solution)/shard_map/ffn/pallas_call | solution.py:280
  30.6 0.7 %collective-permute-start.17 = (bf16[32,2048]{1,0:T(8,128)(2,1)S(1)}, bf16[32,2048]{1,0:T(8,128)(2,1)S(1)}, u32[]{:S(2)}, u32[]{:S(2)}) collective-permute-start(bf16[32,2048]{1,0:T(8,128)(2,1)S(1)} %part.8.refs_2_), channel_id=1, source_target_pairs={{0,2},{1,3},{2,0},{3,1},{4,6},{5,7},{6,4},{7,5},{8,10},{9,11},{10,... | collective-permute-start | bytes 393224 | tf_op jit(solution)/shard_map/ppermute | solution.py:304
  31.3 3.6 %collective-permute-start.13 = (bf16[32,2048]{1,0:T(8,128)(2,1)S(1)}, bf16[32,2048]{1,0:T(8,128)(2,1)S(1)}, u32[]{:S(2)}, u32[]{:S(2)}) collective-permute-start(bf16[32,2048]{1,0:T(8,128)(2,1)S(1)} %part.7.refs_2_), channel_id=1, source_target_pairs={{0,12},{4,8},{8,4},{12,0},{1,13},{5,9},{9,5},{13,1},{2,14},{6,10},... | collective-permute-start | bytes 393224 | tf_op jit(solution)/shard_map/ppermute | solution.py:304
  35.0 1.4 %collective-permute-start.16 = (bf16[32,2048]{1,0:T(8,128)(2,1)S(1)}, bf16[32,2048]{1,0:T(8,128)(2,1)S(1)}, u32[]{:S(2)}, u32[]{:S(2)}) collective-permute-start(bf16[32,2048]{1,0:T(8,128)(2,1)S(1)} %part.9.refs_3_), channel_id=1, source_target_pairs={{0,2},{1,3},{2,0},{3,1},{4,6},{5,7},{6,4},{7,5},{8,10},{9,11},{10,... | collective-permute-start | bytes 393224 | tf_op jit(solution)/shard_map/ppermute | solution.py:304
  36.5 3.0 %collective-permute-start.20 = (bf16[32,2048]{1,0:T(8,128)(2,1)S(1)}, bf16[32,2048]{1,0:T(8,128)(2,1)S(1)}, u32[]{:S(2)}, u32[]{:S(2)}) collective-permute-start(bf16[32,2048]{1,0:T(8,128)(2,1)S(1)} %part.10.refs_3_), channel_id=1, source_target_pairs={{0,8},{4,12},{8,0},{12,4},{1,9},{5,13},{9,1},{13,5},{2,10},{6,14},... | collective-permute-start | bytes 393224 | tf_op jit(solution)/shard_map/ppermute | solution.py:304
  40.1 1.3 %collective-permute-start.19 = (bf16[32,2048]{1,0:T(8,128)(2,1)S(1)}, bf16[32,2048]{1,0:T(8,128)(2,1)S(1)}, u32[]{:S(2)}, u32[]{:S(2)}) collective-permute-start(bf16[32,2048]{1,0:T(8,128)(2,1)S(1)} %part.11.refs_1_), channel_id=1, source_target_pairs={{0,4},{4,0},{8,12},{12,8},{1,5},{5,1},{9,13},{13,9},{2,6},{6,2},{1... | collective-permute-start | bytes 393224 | tf_op jit(solution)/shard_map/ppermute | solution.py:304
  41.4 0.8 %collective-permute-start.18 = (bf16[32,2048]{1,0:T(8,128)(2,1)S(1)}, bf16[32,2048]{1,0:T(8,128)(2,1)S(1)}, u32[]{:S(2)}, u32[]{:S(2)}) collective-permute-start(bf16[32,2048]{1,0:T(8,128)(2,1)S(1)} %join.13), channel_id=1, source_target_pairs={{0,2},{1,3},{2,0},{3,1},{4,6},{5,7},{6,4},{7,5},{8,10},{9,11},{10,... | collective-permute-start | bytes 393224 | tf_op jit(solution)/shard_map/ppermute | solution.py:304
  42.3 4.0 %collective-permute-done.20 = bf16[32,2048]{1,0:T(8,128)(2,1)S(1)} collective-permute-done((bf16[32,2048]{1,0:T(8,128)(2,1)S(1)}, bf16[32,2048]{1,0:T(8,128)(2,1)S(1)}, u32[]{:S(2)}, u32[]{:S(2)}) %collective-permute-start.20) | collective-permute-done | bytes 131104 | tf_op jit(solution)/shard_map/ppermute | solution.py:304
  46.3 0.6 %collective-permute-done.19 = bf16[32,2048]{1,0:T(8,128)(2,1)S(1)} collective-permute-done((bf16[32,2048]{1,0:T(8,128)(2,1)S(1)}, bf16[32,2048]{1,0:T(8,128)(2,1)S(1)}, u32[]{:S(2)}, u32[]{:S(2)}) %collective-permute-start.19) | collective-permute-done | bytes 131104 | tf_op jit(solution)/shard_map/ppermute | solution.py:304
  46.8 0.8 %add_convert_fusion = bf16[32,2048]{1,0:T(8,128)(2,1)} fusion(bf16[32,2048]{1,0:T(8,128)(2,1)S(1)} %collective-permute-done.20, bf16[32,2048]{1,0:T(8,128)(2,1)S(1)} %collective-permute-done.19, f32[32,2048]{1,0:T(8,128)S(1)} %sum.1, bf16[32,2048]{1,0:T(8,128)(2,1)S(1)} %collective-permute-done.18, bf16[32,2048]{1,0:T(8,128)(2,1)S(1)} %get-tuple-element.13.refs_1_, ...), kind=kLoop, calls=%fused_computation | loop fusion | flops 720896 | bytes 1048576 | tf_op jit(solution)/shard_map/convert_element_type | solution.py:352
  (45 shorter events, 4.5 us)
Async XLA Ops:
  1.2 11.2 %collective-permute-start = (bf16[32,2176]{1,0:T(8,128)(2,1)S(1)}, bf16[32,2176]{1,0:T(8,128)(2,1)S(1)}, u32[]{:S(2)}, u32[]{:S(2)}) collective-permute-start(bf16[32,2176]{1,0:T(8,128)(2,1)S(1)} %norm.1.kept_ref.refs_0_), channel_id=1, source_target_pairs={{0,12},{4,8},{8,4},{12,0},{1,13},{5,9},{9,5},{13,1},{2,14},{6,10},... | collective-permute-start | bytes 417800 | tf_op jit(solution)/shard_map/ppermute | solution.py:304
  6.3 7.7 %collective-permute-start.3 = (bf16[32,2176]{1,0:T(8,128)(2,1)S(1)}, bf16[32,2176]{1,0:T(8,128)(2,1)S(1)}, u32[]{:S(2)}, u32[]{:S(2)}) collective-permute-start(bf16[32,2176]{1,0:T(8,128)(2,1)S(1)} %norm.1.kept_ref.refs_0_), channel_id=1, source_target_pairs={{0,4},{4,0},{8,12},{12,8},{1,5},{5,1},{9,13},{13,9},{2,6},{6,2},{1... | collective-permute-start | bytes 417800 | tf_op jit(solution)/shard_map/ppermute | solution.py:304
  6.3 11.8 %collective-permute-start.2 = (bf16[32,2176]{1,0:T(8,128)(2,1)S(1)}, bf16[32,2176]{1,0:T(8,128)(2,1)S(1)}, u32[]{:S(2)}, u32[]{:S(2)}) collective-permute-start(bf16[32,2176]{1,0:T(8,128)(2,1)S(1)} %norm.1.kept_ref.refs_0_), channel_id=1, source_target_pairs={{0,8},{4,12},{8,0},{12,4},{1,9},{5,13},{9,1},{13,5},{2,10},{6,14},... | collective-permute-start | bytes 417800 | tf_op jit(solution)/shard_map/ppermute | solution.py:304
  6.9 8.5 %collective-permute-start.4 = (bf16[32,2176]{1,0:T(8,128)(2,1)S(1)}, bf16[32,2176]{1,0:T(8,128)(2,1)S(1)}, u32[]{:S(2)}, u32[]{:S(2)}) collective-permute-start(bf16[32,2176]{1,0:T(8,128)(2,1)S(1)} %norm.1.kept_ref.refs_0_), channel_id=1, source_target_pairs={{0,2},{1,3},{2,0},{3,1},{4,6},{5,7},{6,4},{7,5},{8,10},{9,11},{10,... | collective-permute-start | bytes 417800 | tf_op jit(solution)/shard_map/ppermute | solution.py:304
  12.4 7.2 %collective-permute-start.1 = (bf16[32,2176]{1,0:T(8,128)(2,1)S(1)}, bf16[32,2176]{1,0:T(8,128)(2,1)S(1)}, u32[]{:S(2)}, u32[]{:S(2)}) collective-permute-start(bf16[32,2176]{1,0:T(8,128)(2,1)S(1)} %join.7.refs_0_), channel_id=1, source_target_pairs={{0,2},{1,3},{2,0},{3,1},{4,6},{5,7},{6,4},{7,5},{8,10},{9,11},{10,... | collective-permute-start | bytes 417800 | tf_op jit(solution)/shard_map/ppermute | solution.py:304
  14.0 7.0 %collective-permute-start.6 = (bf16[32,2176]{1,0:T(8,128)(2,1)S(1)}, bf16[32,2176]{1,0:T(8,128)(2,1)S(1)}, u32[]{:S(2)}, u32[]{:S(2)}) collective-permute-start(bf16[32,2176]{1,0:T(8,128)(2,1)S(1)} %collective-permute-done.3.refs_0_), channel_id=1, source_target_pairs={{0,2},{1,3},{2,0},{3,1},{4,6},{5,7},{6,4},{7,5},{8,10},{9,11},{10,... | collective-permute-start | bytes 417800 | tf_op jit(solution)/shard_map/ppermute | solution.py:304
  15.5 5.6 %collective-permute-start.10 = (bf16[64,2176]{1,0:T(8,128)(2,1)S(1)}, bf16[64,2176]{1,0:T(8,128)(2,1)S(1)}, u32[]{:S(2)}, u32[]{:S(2)}) collective-permute-start(bf16[64,2176]{1,0:T(8,128)(2,1)S(1)} %join.9), channel_id=1, source_target_pairs={{0,1},{1,0},{2,3},{3,2},{4,5},{5,4},{6,7},{7,6},{8,9},{9,8},{10,11... | collective-permute-start | bytes 835592 | tf_op jit(solution)/shard_map/ppermute | solution.py:304
  18.1 5.4 %collective-permute-start.8 = (bf16[32,2176]{1,0:T(8,128)(2,1)S(1)}, bf16[32,2176]{1,0:T(8,128)(2,1)S(1)}, u32[]{:S(2)}, u32[]{:S(2)}) collective-permute-start(bf16[32,2176]{1,0:T(8,128)(2,1)S(1)} %collective-permute-done.2.refs_0_), channel_id=1, source_target_pairs={{0,2},{1,3},{2,0},{3,1},{4,6},{5,7},{6,4},{7,5},{8,10},{9,11},{10,... | collective-permute-start | bytes 417800 | tf_op jit(solution)/shard_map/ppermute | solution.py:304
  19.6 1.6 %collective-permute-start.5 = (bf16[64,2176]{1,0:T(8,128)(2,1)S(1)}, bf16[64,2176]{1,0:T(8,128)(2,1)S(1)}, u32[]{:S(2)}, u32[]{:S(2)}) collective-permute-start(bf16[64,2176]{1,0:T(8,128)(2,1)S(1)} %join.8.refs_1_.refs_0_), channel_id=1, source_target_pairs={{0,1},{1,0},{2,3},{3,2},{4,5},{5,4},{6,7},{7,6},{8,9},{9,8},{10,11... | collective-permute-start | bytes 835592 | tf_op jit(solution)/shard_map/ppermute | solution.py:304
  22.6 1.6 %collective-permute-start.7 = (bf16[64,2048]{1,0:T(8,128)(2,1)S(1)}, bf16[64,2048]{1,0:T(8,128)(2,1)S(1)}, u32[]{:S(2)}, u32[]{:S(2)}) collective-permute-start(bf16[64,2048]{1,0:T(8,128)(2,1)S(1)} %get-tuple-element.16), channel_id=1, source_target_pairs={{0,1},{1,0},{2,3},{3,2},{4,5},{5,4},{6,7},{7,6},{8,9},{9,8},{10,11... | collective-permute-start | bytes 786440 | tf_op jit(solution)/shard_map/ppermute | solution.py:304
  24.3 1.6 %collective-permute-start.12 = (bf16[64,2176]{1,0:T(8,128)(2,1)S(1)}, bf16[64,2176]{1,0:T(8,128)(2,1)S(1)}, u32[]{:S(2)}, u32[]{:S(2)}) collective-permute-start(bf16[64,2176]{1,0:T(8,128)(2,1)S(1)} %join.11.refs_2_.refs_0_), channel_id=1, source_target_pairs={{0,1},{1,0},{2,3},{3,2},{4,5},{5,4},{6,7},{7,6},{8,9},{9,8},{10,11... | collective-permute-start | bytes 835592 | tf_op jit(solution)/shard_map/ppermute | solution.py:304
  24.5 3.0 %collective-permute-start.11 = (bf16[64,2176]{1,0:T(8,128)(2,1)S(1)}, bf16[64,2176]{1,0:T(8,128)(2,1)S(1)}, u32[]{:S(2)}, u32[]{:S(2)}) collective-permute-start(bf16[64,2176]{1,0:T(8,128)(2,1)S(1)} %join.12.refs_0_), channel_id=1, source_target_pairs={{0,1},{1,0},{2,3},{3,2},{4,5},{5,4},{6,7},{7,6},{8,9},{9,8},{10,11... | collective-permute-start | bytes 835592 | tf_op jit(solution)/shard_map/ppermute | solution.py:304
  24.9 5.5 %collective-permute-start.9 = (bf16[32,2048]{1,0:T(8,128)(2,1)S(1)}, bf16[32,2048]{1,0:T(8,128)(2,1)S(1)}, u32[]{:S(2)}, u32[]{:S(2)}) collective-permute-start(bf16[32,2048]{1,0:T(8,128)(2,1)S(1)} %part.6.refs_2_), channel_id=1, source_target_pairs={{0,2},{1,3},{2,0},{3,1},{4,6},{5,7},{6,4},{7,5},{8,10},{9,11},{10,... | collective-permute-start | bytes 393224 | tf_op jit(solution)/shard_map/ppermute | solution.py:304
  27.3 3.3 %collective-permute-start.15 = (bf16[64,2048]{1,0:T(8,128)(2,1)S(1)}, bf16[64,2048]{1,0:T(8,128)(2,1)S(1)}, u32[]{:S(2)}, u32[]{:S(2)}) collective-permute-start(bf16[64,2048]{1,0:T(8,128)(2,1)S(1)} %get-tuple-element.20), channel_id=1, source_target_pairs={{0,1},{1,0},{2,3},{3,2},{4,5},{5,4},{6,7},{7,6},{8,9},{9,8},{10,11... | collective-permute-start | bytes 786440 | tf_op jit(solution)/shard_map/ppermute | solution.py:304
  29.6 5.3 %collective-permute-start.14 = (bf16[128,2048]{1,0:T(8,128)(2,1)S(1)}, bf16[128,2048]{1,0:T(8,128)(2,1)S(1)}, u32[]{:S(2)}, u32[]{:S(2)}) collective-permute-start(bf16[128,2048]{1,0:T(8,128)(2,1)S(1)} %get-tuple-element.19), channel_id=1, source_target_pairs={{0,1},{1,0},{2,3},{3,2},{4,5},{5,4},{6,7},{7,6},{8,9},{9,8},{10,11... | collective-permute-start | bytes 1572872 | tf_op jit(solution)/shard_map/ppermute | solution.py:304
  30.5 11.7 %copy-start = (bf16[32,2048]{1,0:T(8,128)(2,1)S(1)}, bf16[32,2048]{1,0:T(8,128)(2,1)}, u32[]{:S(2)}) copy-start(bf16[32,2048]{1,0:T(8,128)(2,1)} %refs_0_.3) | copy-start | bytes 393220
  30.6 5.8 %collective-permute-start.17 = (bf16[32,2048]{1,0:T(8,128)(2,1)S(1)}, bf16[32,2048]{1,0:T(8,128)(2,1)S(1)}, u32[]{:S(2)}, u32[]{:S(2)}) collective-permute-start(bf16[32,2048]{1,0:T(8,128)(2,1)S(1)} %part.8.refs_2_), channel_id=1, source_target_pairs={{0,2},{1,3},{2,0},{3,1},{4,6},{5,7},{6,4},{7,5},{8,10},{9,11},{10,... | collective-permute-start | bytes 393224 | tf_op jit(solution)/shard_map/ppermute | solution.py:304
  31.3 10.9 %collective-permute-start.13 = (bf16[32,2048]{1,0:T(8,128)(2,1)S(1)}, bf16[32,2048]{1,0:T(8,128)(2,1)S(1)}, u32[]{:S(2)}, u32[]{:S(2)}) collective-permute-start(bf16[32,2048]{1,0:T(8,128)(2,1)S(1)} %part.7.refs_2_), channel_id=1, source_target_pairs={{0,12},{4,8},{8,4},{12,0},{1,13},{5,9},{9,5},{13,1},{2,14},{6,10},... | collective-permute-start | bytes 393224 | tf_op jit(solution)/shard_map/ppermute | solution.py:304
  35.0 5.0 %collective-permute-start.16 = (bf16[32,2048]{1,0:T(8,128)(2,1)S(1)}, bf16[32,2048]{1,0:T(8,128)(2,1)S(1)}, u32[]{:S(2)}, u32[]{:S(2)}) collective-permute-start(bf16[32,2048]{1,0:T(8,128)(2,1)S(1)} %part.9.refs_3_), channel_id=1, source_target_pairs={{0,2},{1,3},{2,0},{3,1},{4,6},{5,7},{6,4},{7,5},{8,10},{9,11},{10,... | collective-permute-start | bytes 393224 | tf_op jit(solution)/shard_map/ppermute | solution.py:304
  36.5 9.8 %collective-permute-start.20 = (bf16[32,2048]{1,0:T(8,128)(2,1)S(1)}, bf16[32,2048]{1,0:T(8,128)(2,1)S(1)}, u32[]{:S(2)}, u32[]{:S(2)}) collective-permute-start(bf16[32,2048]{1,0:T(8,128)(2,1)S(1)} %part.10.refs_3_), channel_id=1, source_target_pairs={{0,8},{4,12},{8,0},{12,4},{1,9},{5,13},{9,1},{13,5},{2,10},{6,14},... | collective-permute-start | bytes 393224 | tf_op jit(solution)/shard_map/ppermute | solution.py:304
  40.1 6.8 %collective-permute-start.19 = (bf16[32,2048]{1,0:T(8,128)(2,1)S(1)}, bf16[32,2048]{1,0:T(8,128)(2,1)S(1)}, u32[]{:S(2)}, u32[]{:S(2)}) collective-permute-start(bf16[32,2048]{1,0:T(8,128)(2,1)S(1)} %part.11.refs_1_), channel_id=1, source_target_pairs={{0,4},{4,0},{8,12},{12,8},{1,5},{5,1},{9,13},{13,9},{2,6},{6,2},{1... | collective-permute-start | bytes 393224 | tf_op jit(solution)/shard_map/ppermute | solution.py:304
  41.4 5.4 %collective-permute-start.18 = (bf16[32,2048]{1,0:T(8,128)(2,1)S(1)}, bf16[32,2048]{1,0:T(8,128)(2,1)S(1)}, u32[]{:S(2)}, u32[]{:S(2)}) collective-permute-start(bf16[32,2048]{1,0:T(8,128)(2,1)S(1)} %join.13), channel_id=1, source_target_pairs={{0,2},{1,3},{2,0},{3,1},{4,6},{5,7},{6,4},{7,5},{8,10},{9,11},{10,... | collective-permute-start | bytes 393224 | tf_op jit(solution)/shard_map/ppermute | solution.py:304
